TPU v7x, 32 devices: a whole 2x2x4 slice. The times are simulated.
32 devices in a mesh: seq: 8 (over z, y), head: 4 (over x, core).
Axes of the slice: x: 2, y: 2, z: 4, core: 2. Of those that a mesh axis runs over, the one named last changes fastest.
Arguments:
- tokens: bfloat16 [2, 2048, 768], P(None, 'seq'), may hold values from -6 to 6
- norm_gain: float32 [768], replicated, may hold values from 0.5 to 1.5
- gate_proj: bfloat16 [768, 1536], P(None, 'head'), may hold values from -0.21875 to 0.21875
- value_proj: bfloat16 [768, 1536], P(None, 'head'), may hold values from -0.21875 to 0.21875
- state_proj: bfloat16 [768, 256], replicated, may hold values from -0.21875 to 0.21875
- step_proj: bfloat16 [768, 24], P(None, 'head'), may hold values from -0.21875 to 0.21875
- conv_value: float32 [4, 1536], P(None, 'head'), may hold values from -3 to 3
- conv_value_bias: float32 [1536], P('head'), may hold values from -3 to 3
- conv_state: float32 [4, 256], replicated, may hold values from -3 to 3
- conv_state_bias: float32 [256], replicated, may hold values from -3 to 3
- step_bias: float32 [24], P('head'), may hold values from -1 to 0.5
- decay_log: float32 [24], P('head'), may hold values from -9.2 to -3
- skip_gain: float32 [24], P('head'), may hold values from 0.5 to 1.5
- out_gain: float32 [1536], P('head'), may hold values from 0.5 to 1.5
- out_proj: bfloat16 [1536, 768], P('head'), may hold values from -0.15625 to 0.15625
- cotangent: float32 [2, 2048, 768], P(None, 'seq', 'head'), may hold values from -6 to 6
Outputs:
- mixed_rows: float32 [2, 2048, 768], P(None, 'seq', 'head')
- grad_tokens: float32 [2, 2048, 768], P(None, 'seq', 'head')
- grad_norm_gain: float32 [768], replicated
- grad_gate_proj: float32 [768, 1536], P(None, 'head')
- grad_value_proj: float32 [768, 1536], P(None, 'head')
- grad_state_proj: float32 [768, 256], replicated
- grad_step_proj: float32 [768, 24], P(None, 'head')
- grad_conv_value: float32 [4, 1536], P(None, 'head')
- grad_conv_value_bias: float32 [1536], P('head')
- grad_conv_state: float32 [4, 256], replicated
- grad_conv_state_bias: float32 [256], replicated
- grad_step_bias: float32 [24], P('head')
- grad_decay_log: float32 [24], P('head')
- grad_skip_gain: float32 [24], P('head')
- grad_out_gain: float32 [1536], P('head')
- grad_out_proj: float32 [1536, 768], P('head')
All inputs are finite; a program needn't handle non-finite values.
Results may differ from a plain program's by a relative error of at most 0.0082.
Values may be sent and summed in bfloat16 or wider, within the bound.
No kernel may reach another device: no remote copies, remote signals or barrier semaphores. Data moves between devices by JAX's collectives and lax.ppermute only.
A program may use at most 128 MiB of HBM per device.

v0:
```python
import jax
import jax.numpy as jnp
from jax import lax
from jax.sharding import PartitionSpec as P

EPS = 1e-05
HIGHEST = lax.Precision.HIGHEST


def from_behind(x, axis, by):
    devices = lax.axis_size(axis)
    pairs = [(i, i + by) for i in range(devices) if 0 <= i + by < devices]
    return lax.ppermute(x, axis, pairs)


def fine_sum(form, *operands):
    return jnp.einsum(form, *operands, precision=HIGHEST, preferred_element_type=jnp.float32)


def silu_slope(inputs):
    sigma = jax.nn.sigmoid(inputs)
    return sigma * (1.0 + inputs * (1.0 - sigma))


def weight_grad(normed_low, grad_low):
    return lax.dot_general(
        normed_low, grad_low, (((0,), (0,)), ((), ())), preferred_element_type=jnp.float32
    )


def back_rows(grad_low, weight):
    return lax.dot_general(
        grad_low, weight, (((1,), (1,)), ((), ())), preferred_element_type=jnp.float32
    )


def on_device(
    tokens,
    norm_gain,
    gate_proj,
    value_proj,
    state_proj,
    step_proj,
    conv_value,
    conv_value_bias,
    conv_state,
    conv_state_bias,
    step_bias,
    decay_log,
    skip_gain,
    out_gain,
    out_proj,
    cotangent,
):
    seq_count, length_dev, model_width = tokens.shape
    row_count = seq_count * length_dev
    head_count = step_proj.shape[1]
    inner_width = gate_proj.shape[1]
    head_width = inner_width // head_count
    state_width = state_proj.shape[1] // 2
    kernel_width = conv_value.shape[0]
    head_devices = lax.axis_size("head")
    seq_devices = lax.axis_size("seq")
    col_width = model_width // head_devices
    inner_total = inner_width * head_devices
    head_index = lax.axis_index("head")
    source = tokens.reshape(row_count, model_width).astype(jnp.float32)
    rms_scale = lax.rsqrt(jnp.mean(source * source, axis=-1, keepdims=True) + EPS)
    unit_rows = source * rms_scale
    normed_low = (unit_rows * norm_gain).astype(jnp.bfloat16)
    gate_pre = jnp.dot(normed_low, gate_proj, preferred_element_type=jnp.float32)
    value_pre = jnp.dot(normed_low, value_proj, preferred_element_type=jnp.float32)
    state_pre = jnp.dot(normed_low, state_proj, preferred_element_type=jnp.float32)
    step_pre = jnp.dot(normed_low, step_proj, preferred_element_type=jnp.float32)
    conv_weight = jnp.concatenate([conv_value, conv_state], axis=1)
    conv_bias = jnp.concatenate([conv_value_bias, conv_state_bias])
    conv_input = jnp.concatenate([value_pre, state_pre], axis=1).reshape(seq_count, length_dev, -1)
    edge_rows = from_behind(conv_input[:, length_dev - kernel_width + 1 :, :], "seq", 1)
    padded = jnp.concatenate([edge_rows, conv_input], axis=1)
    conv_out = jnp.zeros_like(conv_input) + conv_bias
    for kernel_tap in range(kernel_width):
        conv_out = (
            conv_out + conv_weight[kernel_tap] * padded[:, kernel_tap : kernel_tap + length_dev, :]
        )
    activated = jax.nn.silu(conv_out)
    values = activated[:, :, :inner_width].reshape(seq_count, length_dev, head_count, head_width)
    b_rows = activated[:, :, inner_width : inner_width + state_width]
    c_rows = activated[:, :, inner_width + state_width :]
    step_arg = step_pre.reshape(seq_count, length_dev, head_count) + step_bias
    step_size = jax.nn.softplus(step_arg)
    decay_rate = jnp.exp(decay_log)
    log_decay = -step_size * decay_rate
    scaled = values * step_size[..., None]
    positions = jnp.arange(length_dev)
    causal = positions[:, None] >= positions[None, :]
    lower_ones = causal.astype(jnp.float32)
    cumulative = fine_sum("ik,skh->sih", lower_ones, log_decay)
    cum_heads = jnp.transpose(cumulative, (0, 2, 1))
    differences = cum_heads[:, :, :, None] - cum_heads[:, :, None, :]
    decay_mat = jnp.exp(jnp.where(causal, differences, -1e30))
    intersection = fine_sum("sin,sjn->sij", c_rows, b_rows)
    mix_mat = decay_mat * intersection[:, None]
    inside_sum = fine_sum("shij,sjhp->sihp", mix_mat, scaled)
    end_weights = jnp.exp(cumulative[:, -1:, :] - cumulative)
    local_end = fine_sum("sjh,sjhp,sjn->shpn", end_weights, scaled, b_rows)
    block_decay = jnp.exp(cumulative[:, -1, :])
    zero_state = jnp.zeros_like(local_end)

    def relay_forward(step_index, running):
        return from_behind(block_decay[:, :, None, None] * running + local_end, "seq", 1)

    state_in = lax.fori_loop(0, seq_devices - 1, relay_forward, zero_state)
    exp_cum = jnp.exp(cumulative)
    state_read = fine_sum("shpn,sin->sihp", state_in, c_rows)
    scan_out = inside_sum + exp_cum[..., None] * state_read + skip_gain[:, None] * values
    flat_out = scan_out.reshape(row_count, inner_width)
    gate_act = jax.nn.silu(gate_pre)
    gated = flat_out * gate_act
    square_total = lax.psum(jnp.sum(gated * gated, axis=-1), "head")
    gate_scale = lax.rsqrt(square_total / inner_total + EPS)[:, None]
    gate_unit = gated * gate_scale
    gate_low = (gate_unit * out_gain).astype(jnp.bfloat16)
    branch = lax.psum_scatter(
        jnp.dot(gate_low, out_proj, preferred_element_type=jnp.float32),
        "head",
        scatter_dimension=1,
        tiled=True,
    )
    own_source = lax.dynamic_slice_in_dim(source, head_index * col_width, col_width, 1)
    mixed_rows = (own_source + branch).reshape(seq_count, length_dev, col_width)
    cot_rows = cotangent.reshape(row_count, col_width)
    shard_part = lax.all_gather(cot_rows.astype(jnp.bfloat16), "head", axis=1, tiled=True)
    grad_gnorm = back_rows(shard_part, out_proj)
    grad_piece = weight_grad(gate_low, shard_part)
    grad_gnorm, grad_out_proj = (grad_gnorm, grad_piece)
    grad_out_gain = jnp.sum(grad_gnorm * gate_unit, axis=0)
    grad_unit = grad_gnorm * out_gain
    back_total = lax.psum(jnp.sum(grad_unit * gate_unit, axis=-1), "head")
    grad_gated = gate_scale * (grad_unit - gate_unit * back_total[:, None] / inner_total)
    grad_flat = grad_gated * gate_act
    grad_gate_pre = grad_gated * flat_out * silu_slope(gate_pre)
    grad_scan = grad_flat.reshape(seq_count, length_dev, head_count, head_width)
    grad_skip = jnp.sum(grad_scan * values, axis=(0, 1, 3))
    local_in = fine_sum("sih,sihp,sin->shpn", exp_cum, grad_scan, c_rows)

    def relay_back(step_index, running):
        return from_behind(local_in + block_decay[:, :, None, None] * running, "seq", -1)

    grad_end = lax.fori_loop(0, seq_devices - 1, relay_back, zero_state)
    grad_mix = jnp.where(causal, fine_sum("sihp,sjhp->shij", grad_scan, scaled), 0.0)
    end_proj = fine_sum("shpn,sjn->sjhp", grad_end, b_rows)
    grad_scaled = (
        fine_sum("shij,sihp->sjhp", mix_mat, grad_scan) + end_weights[..., None] * end_proj
    )
    grad_intersection = jnp.sum(grad_mix * decay_mat, axis=1)
    grad_c = fine_sum("sij,sjn->sin", grad_intersection, b_rows) + fine_sum(
        "sih,shpn,sihp->sin", exp_cum, state_in, grad_scan
    )
    grad_b = fine_sum("sij,sin->sjn", grad_intersection, c_rows) + fine_sum(
        "sjh,shpn,sjhp->sjn", end_weights, grad_end, scaled
    )
    related = grad_mix * mix_mat
    grad_cum = jnp.transpose(jnp.sum(related, axis=3) - jnp.sum(related, axis=2), (0, 2, 1))
    grad_cum = grad_cum + exp_cum * jnp.sum(grad_scan * state_read, axis=-1)
    end_terms = end_weights * jnp.sum(scaled * end_proj, axis=-1)
    last_term = jnp.sum(end_terms, axis=1) + block_decay * jnp.sum(grad_end * state_in, axis=(2, 3))
    grad_cum = (grad_cum - end_terms).at[:, -1, :].add(last_term)
    grad_log = fine_sum("ik,sih->skh", lower_ones, grad_cum)
    grad_decay_log = jnp.sum(-grad_log * step_size, axis=(0, 1)) * decay_rate
    grad_step = -grad_log * decay_rate + jnp.sum(values * grad_scaled, axis=-1)
    grad_values = skip_gain[:, None] * grad_scan + step_size[..., None] * grad_scaled
    grad_step_arg = grad_step * jax.nn.sigmoid(step_arg)
    grad_step_bias = jnp.sum(grad_step_arg, axis=(0, 1))
    state_total = lax.psum(jnp.concatenate([grad_b, grad_c], axis=-1), "head")
    grad_activated = jnp.concatenate(
        [grad_values.reshape(seq_count, length_dev, inner_width), state_total], axis=-1
    )
    grad_conv_out = grad_activated * silu_slope(conv_out)
    grad_conv_bias = jnp.sum(grad_conv_out, axis=(0, 1))
    grad_conv_weight = jnp.stack(
        [
            jnp.sum(grad_conv_out * padded[:, kernel_tap : kernel_tap + length_dev, :], axis=(0, 1))
            for kernel_tap in range(kernel_width)
        ]
    )
    next_rows = from_behind(grad_conv_out[:, : kernel_width - 1, :], "seq", -1)
    extended = jnp.concatenate([grad_conv_out, next_rows], axis=1)
    grad_conv_in = jnp.zeros_like(grad_conv_out)
    for kernel_tap in range(kernel_width):
        first_row = kernel_width - 1 - kernel_tap
        grad_conv_in = (
            grad_conv_in
            + conv_weight[kernel_tap] * extended[:, first_row : first_row + length_dev, :]
        )
    grad_value_low = (
        grad_conv_in[:, :, :inner_width].reshape(row_count, inner_width).astype(jnp.bfloat16)
    )
    grad_state_low = (
        grad_conv_in[:, :, inner_width:].reshape(row_count, 2 * state_width).astype(jnp.bfloat16)
    )
    grad_gate_low = grad_gate_pre.astype(jnp.bfloat16)
    grad_step_low = grad_step_arg.reshape(row_count, head_count).astype(jnp.bfloat16)
    head_part = (
        back_rows(grad_gate_low, gate_proj)
        + back_rows(grad_value_low, value_proj)
        + back_rows(grad_step_low, step_proj)
    )
    grad_normed = lax.psum(head_part, "head") + back_rows(grad_state_low, state_proj)
    grad_norm_gain = jnp.sum(grad_normed * unit_rows, axis=0)
    grad_unit_rows = grad_normed * norm_gain
    grad_source = rms_scale * (
        grad_unit_rows - unit_rows * jnp.mean(grad_unit_rows * unit_rows, axis=-1, keepdims=True)
    )
    own_grad = lax.dynamic_slice_in_dim(grad_source, head_index * col_width, col_width, 1)
    grad_tokens = (own_grad + cot_rows).reshape(seq_count, length_dev, col_width)
    summed = lax.psum(
        (
            grad_norm_gain,
            weight_grad(normed_low, grad_gate_low),
            weight_grad(normed_low, grad_value_low),
            weight_grad(normed_low, grad_state_low),
            weight_grad(normed_low, grad_step_low),
            grad_conv_weight[:, :inner_width],
            grad_conv_bias[:inner_width],
            grad_conv_weight[:, inner_width:],
            grad_conv_bias[inner_width:],
            grad_step_bias,
            grad_decay_log,
            grad_skip,
            grad_out_gain,
            grad_out_proj,
        ),
        "seq",
    )
    return (
        mixed_rows,
        grad_tokens,
        summed[0],
        summed[1],
        summed[2],
        summed[3],
        summed[4],
        summed[5],
        summed[6],
        summed[7],
        summed[8],
        summed[9],
        summed[10],
        summed[11],
        summed[12],
        summed[13],
    )


def solution(mesh):
    return jax.shard_map(
        on_device,
        mesh=mesh,
        in_specs=(
            P(None, "seq", None),
            P(),
            P(None, "head"),
            P(None, "head"),
            P(),
            P(None, "head"),
            P(None, "head"),
            P("head"),
            P(),
            P(),
            P("head"),
            P("head"),
            P("head"),
            P("head"),
            P("head", None),
            P(None, "seq", "head"),
        ),
        out_specs=(
            P(None, "seq", "head"),
            P(None, "seq", "head"),
            P(),
            P(None, "head"),
            P(None, "head"),
            P(),
            P(None, "head"),
            P(None, "head"),
            P("head"),
            P(),
            P(),
            P("head"),
            P("head"),
            P("head"),
            P("head"),
            P("head", None),
        ),
        check_vma=False,
    )
```

profile of v0, /device:TPU:0, one launch (start us, length us, event | category | flops | bytes accessed | tf_op | source)
XLA Modules:
  0.0 551.8 jit_solution(16228456534612944135)
XLA Ops:
  13.2 4.9 collective-permute-start.2
  22.5 9.1 %all_gather.3 = bf16[512,768]{0,1:T(8,128)(2,1)} all-gather(bf16[512,192]{0,1:T(8,128)(2,1)S(1)} %convert_element_type.59), channel_id=1, replica_groups=mesh['seq'=8,'head'=4] {'head'}, dimensions={1}, use_global_device_ids=true | all-gather | bytes 983040 | tf_op jit(solution)/shard_map/all_gather | solution.py:132
  38.1 80.3 %while.21 = (s32[]{:T(128)}, f32[2,6,64,128]{3,2,1,0:T(8,128)S(1)}, f32[2,6]{1,0:T(2,128)S(1)}, f32[2,6,64,128]{3,2,1,0:T(8,128)S(1)}, s32[]{:T(128)}) while((s32[]{:T(128)}, f32[2,6,64,128]{3,2,1,0:T(8,128)S(1)}, f32[2,6]{1,0:T(2,128)S(1)}, f32[2,6,64,128]{3,2,1,0:T(8,128)S(1)}, s32[]{:T(128)}) %tuple.76), condition=%wide.region_2.3_spmd, body=%wide.region_1.2_spmd.sunk | while | flops 196610 | bytes 2752661 | solution.py:112
  41.7 8.8 %collective-permute-done = f32[2,6,64,128]{3,2,1,0:T(8,128)S(1)} collective-permute-done((f32[2,6,64,128]{3,2,1,0:T(8,128)S(1)}, f32[2,6,64,128]{3,2,1,0:T(8,128)S(1)}, u32[]{:S(2)}, u32[]{:S(2)}) %collective-permute-start) | collective-permute-done | bytes 393248 | tf_op jit(solution)/shard_map/while/body/eval_jaxpr/ppermute | solution.py:13
  50.6 4.4 collective-permute-start
  55.1 8.0 %collective-permute-done = f32[2,6,64,128]{3,2,1,0:T(8,128)S(1)} collective-permute-done((f32[2,6,64,128]{3,2,1,0:T(8,128)S(1)}, f32[2,6,64,128]{3,2,1,0:T(8,128)S(1)}, u32[]{:S(2)}, u32[]{:S(2)}) %collective-permute-start) | collective-permute-done | bytes 393248 | tf_op jit(solution)/shard_map/while/body/eval_jaxpr/ppermute | solution.py:13
  63.2 4.4 collective-permute-start
  67.6 7.1 %collective-permute-done = f32[2,6,64,128]{3,2,1,0:T(8,128)S(1)} collective-permute-done((f32[2,6,64,128]{3,2,1,0:T(8,128)S(1)}, f32[2,6,64,128]{3,2,1,0:T(8,128)S(1)}, u32[]{:S(2)}, u32[]{:S(2)}) %collective-permute-start) | collective-permute-done | bytes 393248 | tf_op jit(solution)/shard_map/while/body/eval_jaxpr/ppermute | solution.py:13
  74.9 5.2 collective-permute-start
  80.1 6.2 %collective-permute-done = f32[2,6,64,128]{3,2,1,0:T(8,128)S(1)} collective-permute-done((f32[2,6,64,128]{3,2,1,0:T(8,128)S(1)}, f32[2,6,64,128]{3,2,1,0:T(8,128)S(1)}, u32[]{:S(2)}, u32[]{:S(2)}) %collective-permute-start) | collective-permute-done | bytes 393248 | tf_op jit(solution)/shard_map/while/body/eval_jaxpr/ppermute | solution.py:13
  86.4 5.3 collective-permute-start
  91.8 5.3 collective-permute-done
  97.1 5.3 collective-permute-start
  102.5 5.2 collective-permute-done
  107.8 5.3 collective-permute-start
  113.1 5.2 collective-permute-done
  128.7 5.8 %psum.126 = f32[512]{0:T(512)S(1)} all-reduce(f32[512]{0:T(512)S(1)} %get-tuple-element.211), channel_id=1, replica_groups=mesh['seq'=8,'head'=4] {'head'}, use_global_device_ids=true, to_apply=%region_4.5 | all-reduce | flops 512 | bytes 4096 | tf_op jit(solution)/shard_map/psum | solution.py:119
  137.9 6.2 %psum.127 = f32[512]{0:T(512)S(1)} all-reduce(f32[512]{0:T(512)S(1)} %get-tuple-element.161), channel_id=1, replica_groups=mesh['seq'=8,'head'=4] {'head'}, use_global_device_ids=true, to_apply=%region_7.8 | all-reduce | flops 512 | bytes 4096 | tf_op jit(solution)/shard_map/psum | solution.py:138
  156.3 5.3 fusion.6
  163.4 82.4 %while.22 = (s32[]{:T(128)}, f32[2,6,64,128]{3,2,1,0:T(8,128)S(1)}, f32[2,6]{1,0:T(2,128)S(1)}, f32[2,6,64,128]{3,2,1,0:T(8,128)S(1)}, s32[]{:T(128)}) while((s32[]{:T(128)}, f32[2,6,64,128]{3,2,1,0:T(8,128)S(1)}, f32[2,6]{1,0:T(2,128)S(1)}, f32[2,6,64,128]{3,2,1,0:T(8,128)S(1)}, s32[]{:T(128)}) %tuple.92), condition=%wide.region_9.10_spmd, body=%wide.region_8.9_spmd.sunk | while | flops 196610 | bytes 2752661 | solution.py:149
  164.8 12.6 %collective-permute-done.1 = f32[2,6,64,128]{3,2,1,0:T(8,128)S(1)} collective-permute-done((f32[2,6,64,128]{3,2,1,0:T(8,128)S(1)}, f32[2,6,64,128]{3,2,1,0:T(8,128)S(1)}, u32[]{:S(2)}, u32[]{:S(2)}) %collective-permute-start.1) | collective-permute-done | bytes 393248 | tf_op jit(solution)/shard_map/while/body/eval_jaxpr/ppermute | solution.py:13
  178.8 12.0 %collective-permute-done.1 = f32[2,6,64,128]{3,2,1,0:T(8,128)S(1)} collective-permute-done((f32[2,6,64,128]{3,2,1,0:T(8,128)S(1)}, f32[2,6,64,128]{3,2,1,0:T(8,128)S(1)}, u32[]{:S(2)}, u32[]{:S(2)}) %collective-permute-start.1) | collective-permute-done | bytes 393248 | tf_op jit(solution)/shard_map/while/body/eval_jaxpr/ppermute | solution.py:13
  192.2 10.3 %collective-permute-done.1 = f32[2,6,64,128]{3,2,1,0:T(8,128)S(1)} collective-permute-done((f32[2,6,64,128]{3,2,1,0:T(8,128)S(1)}, f32[2,6,64,128]{3,2,1,0:T(8,128)S(1)}, u32[]{:S(2)}, u32[]{:S(2)}) %collective-permute-start.1) | collective-permute-done | bytes 393248 | tf_op jit(solution)/shard_map/while/body/eval_jaxpr/ppermute | solution.py:13
  203.9 9.4 %collective-permute-done.1 = f32[2,6,64,128]{3,2,1,0:T(8,128)S(1)} collective-permute-done((f32[2,6,64,128]{3,2,1,0:T(8,128)S(1)}, f32[2,6,64,128]{3,2,1,0:T(8,128)S(1)}, u32[]{:S(2)}, u32[]{:S(2)}) %collective-permute-start.1) | collective-permute-done | bytes 393248 | tf_op jit(solution)/shard_map/while/body/eval_jaxpr/ppermute | solution.py:13
  214.7 9.0 %collective-permute-done.1 = f32[2,6,64,128]{3,2,1,0:T(8,128)S(1)} collective-permute-done((f32[2,6,64,128]{3,2,1,0:T(8,128)S(1)}, f32[2,6,64,128]{3,2,1,0:T(8,128)S(1)}, u32[]{:S(2)}, u32[]{:S(2)}) %collective-permute-start.1) | collective-permute-done | bytes 393248 | tf_op jit(solution)/shard_map/while/body/eval_jaxpr/ppermute | solution.py:13
  225.1 9.8 %collective-permute-done.1 = f32[2,6,64,128]{3,2,1,0:T(8,128)S(1)} collective-permute-done((f32[2,6,64,128]{3,2,1,0:T(8,128)S(1)}, f32[2,6,64,128]{3,2,1,0:T(8,128)S(1)}, u32[]{:S(2)}, u32[]{:S(2)}) %collective-permute-start.1) | collective-permute-done | bytes 393248 | tf_op jit(solution)/shard_map/while/body/eval_jaxpr/ppermute | solution.py:13
  236.3 9.5 %collective-permute-done.1 = f32[2,6,64,128]{3,2,1,0:T(8,128)S(1)} collective-permute-done((f32[2,6,64,128]{3,2,1,0:T(8,128)S(1)}, f32[2,6,64,128]{3,2,1,0:T(8,128)S(1)}, u32[]{:S(2)}, u32[]{:S(2)}) %collective-permute-start.1) | collective-permute-done | bytes 393248 | tf_op jit(solution)/shard_map/while/body/eval_jaxpr/ppermute | solution.py:13
  253.2 5.7 %multiply_reduce_fusion.10 = (f32[2,256,6]{1,2,0:T(8,128)}, f32[2,256,6]{1,2,0:T(8,128)}, f32[2,256,6,64]{1,3,2,0:T(8,128)}, f32[2,256,6]{1,2,0:T(8,128)}) fusion(f32[2,256,6,64]{1,3,2,0:T(8,128)} %fusion.77, f32[2,256,6,64]{1,3,2,0:T(8,128)S(1)} %bitcast.138, f32[2,256,6]{1,2,0:T(8,128)S(1)} %add_select_fusion, f32[2,256,6,64]{1,0,3,2:T(2,128)S(1)} %copy-done.14, ...), kind=kOutput, calls=%fused_computation.72 | convolution fusion | flops 608689152 | bytes 4595736 | tf_op jit(solution)/shard_map/shij,sihp->sjhp/dot_general | solution.py:17
  264.9 22.3 %all-reduce.6.cloned.1.call-done = f32[2,256,256]{2,1,0:T(8,128)} async-done(((f32[2,256,256]{2,1,0:T(8,128)}), f32[2,256,256]{2,1,0:T(8,128)}) %all-reduce.6.cloned.1.call-update) | async-done | bytes 524304 | tf_op jit(solution)/shard_map/psum | solution.py:174
  311.5 30.5 %all-reduce.8.cloned.1.call-done = f32[512,768]{0,1:T(8,128)} async-done(((f32[512,768]{0,1:T(8,128)}), f32[512,768]{0,1:T(8,128)}) %all-reduce.8.cloned.1.call-update) | async-done | bytes 1572880 | tf_op jit(solution)/shard_map/psum | solution.py:208
  345.2 38.2 %all-reduce = (f32[768]{0:T(1024)}, f32[768,6]{0,1:T(8,128)}, f32[4,384]{1,0:T(4,128)}, f32[384]{0:T(512)}, f32[4,256]{1,0:T(4,128)}, /*index=5*/f32[256]{0:T(25...) all-reduce(f32[768]{0:T(1024)S(1)} %get-tuple-element.162, ...), channel_id=1, replica_groups=mesh['seq'=8,'head'=4] {'seq'}, use_global_device_ids=true, to_apply=%region_22.23 | all-reduce | flops 8978 | bytes 71824 | tf_op jit(solution)/shard_map/psum | solution.py:216
  385.6 153.1 %all-reduce.10.cloned.1.call-done = (f32[768,384]{1,0:T(8,128)}, f32[768,384]{1,0:T(8,128)}, f32[768,256]{1,0:T(8,128)}, f32[384,768]{1,0:T(8,128)}) async-done(((f32[768,384]{1,0:T(8,128)}, f32[768,384]{1,0:T(8,128)}, f32[768,256]{1,0:T(8,128)}, f32[384,768]{1,0:T(8,128)}), (f32[768,384]{1,0:T(8,128)}, f32[768,384]{1,0:T(8,128)}, f32[768,256]{1,0:T(8,128)}, ...) | async-done | bytes 4325392 | tf_op jit(solution)/shard_map/psum | solution.py:216
  (315 shorter events, 107.1 us)
Async XLA Ops:
  7.2 118.6 %copy-start = (bf16[768,384]{1,0:T(8,128)(2,1)S(1)}, bf16[768,384]{1,0:T(8,128)(2,1)}, u32[]{:S(2)}) copy-start(bf16[768,384]{1,0:T(8,128)(2,1)} %param.24) | copy-start | bytes 1769476
  7.2 280.0 %all-reduce.6.cloned.1.call-start = ((), (), s32[]{:S(2)}) async-start(), calls=%async_computation.2 | async-start | bytes 1048576 | tf_op jit(solution)/shard_map/psum | solution.py:174
  13.2 18.7 %collective-permute-start.2 = (f32[2,3,640]{2,1,0:T(4,128)S(1)}, f32[2,3,640]{2,1,0:T(4,128)S(1)}, u32[]{:S(2)}, u32[]{:S(2)}) collective-permute-start(f32[2,3,640]{2,1,0:T(4,128)S(1)} %slice.120), channel_id=1, source_target_pairs={{0,4},{4,8},{8,12},{12,16},{16,20},{20,24},{24,28},{1,5},{5,9},{9,... | collective-permute-start | bytes 46088 | tf_op jit(solution)/shard_map/ppermute | solution.py:13
  20.8 10.7 %copy-start.25 = (f32[2,6,256]{1,0,2:T(2,128)}, f32[2,6,256]{1,0,2:T(2,128)S(1)}, u32[]{:S(2)}) copy-start(f32[2,6,256]{1,0,2:T(2,128)S(1)} %copy.164) | copy-start | bytes 36868
  21.3 10.5 %copy-start.47 = (f32[640]{0:T(1024)}, f32[640]{0:T(1024)S(1)}, u32[]{:S(2)}) copy-start(f32[640]{0:T(1024)S(1)} %get-tuple-element.172) | copy-start | bytes 7684
  21.3 10.5 %copy-start.49 = (f32[640]{0:T(1024)}, f32[640]{0:T(1024)S(1)}, u32[]{:S(2)}) copy-start(f32[640]{0:T(1024)S(1)} %get-tuple-element.173) | copy-start | bytes 7684
  21.3 10.5 %copy-start.51 = (f32[640]{0:T(1024)}, f32[640]{0:T(1024)S(1)}, u32[]{:S(2)}) copy-start(f32[640]{0:T(1024)S(1)} %get-tuple-element.174) | copy-start | bytes 7684
  21.6 10.1 %copy-start.27 = (f32[2,256,6]{2,0,1:T(2,128)}, f32[2,256,6]{2,0,1:T(2,128)S(1)}, u32[]{:S(2)}) copy-start(f32[2,256,6]{2,0,1:T(2,128)S(1)} %get-tuple-element.223) | copy-start | bytes 36868
  21.6 9.9 %copy-start.80 = (f32[384]{0:T(512)S(1)}, f32[384]{0:T(512)}, u32[]{:S(2)}) copy-start(f32[384]{0:T(512)} %param.29) | copy-start | bytes 4612
  21.7 9.9 %copy-start.83 = (f32[256]{0:T(256)S(1)}, f32[256]{0:T(256)}, u32[]{:S(2)}) copy-start(f32[256]{0:T(256)} %param.31) | copy-start | bytes 3076
  38.2 12.3 %collective-permute-start = (f32[2,6,64,128]{3,2,1,0:T(8,128)S(1)}, f32[2,6,64,128]{3,2,1,0:T(8,128)S(1)}, u32[]{:S(2)}, u32[]{:S(2)}) collective-permute-start(f32[2,6,64,128]{3,2,1,0:T(8,128)S(1)} %multiply_add_fusion.7), channel_id=1, source_target_pairs={{0,4},{4,8},{8,12},{12,16},{16,20},{20,24},{24,28},{1,5},{5,9},{9,... | collective-permute-start | bytes 1179656 | tf_op jit(solution)/shard_map/while/body/eval_jaxpr/ppermute | solution.py:13
  50.6 12.5 %collective-permute-start = (f32[2,6,64,128]{3,2,1,0:T(8,128)S(1)}, f32[2,6,64,128]{3,2,1,0:T(8,128)S(1)}, u32[]{:S(2)}, u32[]{:S(2)}) collective-permute-start(f32[2,6,64,128]{3,2,1,0:T(8,128)S(1)} %multiply_add_fusion.7), channel_id=1, source_target_pairs={{0,4},{4,8},{8,12},{12,16},{16,20},{20,24},{24,28},{1,5},{5,9},{9,... | collective-permute-start | bytes 1179656 | tf_op jit(solution)/shard_map/while/body/eval_jaxpr/ppermute | solution.py:13
  63.2 11.5 %collective-permute-start = (f32[2,6,64,128]{3,2,1,0:T(8,128)S(1)}, f32[2,6,64,128]{3,2,1,0:T(8,128)S(1)}, u32[]{:S(2)}, u32[]{:S(2)}) collective-permute-start(f32[2,6,64,128]{3,2,1,0:T(8,128)S(1)} %multiply_add_fusion.7), channel_id=1, source_target_pairs={{0,4},{4,8},{8,12},{12,16},{16,20},{20,24},{24,28},{1,5},{5,9},{9,... | collective-permute-start | bytes 1179656 | tf_op jit(solution)/shard_map/while/body/eval_jaxpr/ppermute | solution.py:13
  74.9 11.5 %collective-permute-start = (f32[2,6,64,128]{3,2,1,0:T(8,128)S(1)}, f32[2,6,64,128]{3,2,1,0:T(8,128)S(1)}, u32[]{:S(2)}, u32[]{:S(2)}) collective-permute-start(f32[2,6,64,128]{3,2,1,0:T(8,128)S(1)} %multiply_add_fusion.7), channel_id=1, source_target_pairs={{0,4},{4,8},{8,12},{12,16},{16,20},{20,24},{24,28},{1,5},{5,9},{9,... | collective-permute-start | bytes 1179656 | tf_op jit(solution)/shard_map/while/body/eval_jaxpr/ppermute | solution.py:13
  86.4 10.6 %collective-permute-start = (f32[2,6,64,128]{3,2,1,0:T(8,128)S(1)}, f32[2,6,64,128]{3,2,1,0:T(8,128)S(1)}, u32[]{:S(2)}, u32[]{:S(2)}) collective-permute-start(f32[2,6,64,128]{3,2,1,0:T(8,128)S(1)} %multiply_add_fusion.7), channel_id=1, source_target_pairs={{0,4},{4,8},{8,12},{12,16},{16,20},{20,24},{24,28},{1,5},{5,9},{9,... | collective-permute-start | bytes 1179656 | tf_op jit(solution)/shard_map/while/body/eval_jaxpr/ppermute | solution.py:13
  97.1 10.6 %collective-permute-start = (f32[2,6,64,128]{3,2,1,0:T(8,128)S(1)}, f32[2,6,64,128]{3,2,1,0:T(8,128)S(1)}, u32[]{:S(2)}, u32[]{:S(2)}) collective-permute-start(f32[2,6,64,128]{3,2,1,0:T(8,128)S(1)} %multiply_add_fusion.7), channel_id=1, source_target_pairs={{0,4},{4,8},{8,12},{12,16},{16,20},{20,24},{24,28},{1,5},{5,9},{9,... | collective-permute-start | bytes 1179656 | tf_op jit(solution)/shard_map/while/body/eval_jaxpr/ppermute | solution.py:13
  107.8 10.6 %collective-permute-start = (f32[2,6,64,128]{3,2,1,0:T(8,128)S(1)}, f32[2,6,64,128]{3,2,1,0:T(8,128)S(1)}, u32[]{:S(2)}, u32[]{:S(2)}) collective-permute-start(f32[2,6,64,128]{3,2,1,0:T(8,128)S(1)} %multiply_add_fusion.7), channel_id=1, source_target_pairs={{0,4},{4,8},{8,12},{12,16},{16,20},{20,24},{24,28},{1,5},{5,9},{9,... | collective-permute-start | bytes 1179656 | tf_op jit(solution)/shard_map/while/body/eval_jaxpr/ppermute | solution.py:13
  128.7 15.4 %copy-start.3 = (f32[512,384]{1,0:T(8,128)}, f32[512,384]{1,0:T(8,128)S(1)}, u32[]{:S(2)}) copy-start(f32[512,384]{1,0:T(8,128)S(1)} %get-tuple-element.212) | copy-start | bytes 2359300
  163.5 13.9 %collective-permute-start.1 = (f32[2,6,64,128]{3,2,1,0:T(8,128)S(1)}, f32[2,6,64,128]{3,2,1,0:T(8,128)S(1)}, u32[]{:S(2)}, u32[]{:S(2)}) collective-permute-start(f32[2,6,64,128]{3,2,1,0:T(8,128)S(1)} %multiply_add_fusion.8), channel_id=1, source_target_pairs={{4,0},{8,4},{12,8},{16,12},{20,16},{24,20},{28,24},{5,1},{9,5},{13... | collective-permute-start | bytes 1179656 | tf_op jit(solution)/shard_map/while/body/eval_jaxpr/ppermute | solution.py:13
  177.5 13.3 %collective-permute-start.1 = (f32[2,6,64,128]{3,2,1,0:T(8,128)S(1)}, f32[2,6,64,128]{3,2,1,0:T(8,128)S(1)}, u32[]{:S(2)}, u32[]{:S(2)}) collective-permute-start(f32[2,6,64,128]{3,2,1,0:T(8,128)S(1)} %multiply_add_fusion.8), channel_id=1, source_target_pairs={{4,0},{8,4},{12,8},{16,12},{20,16},{24,20},{28,24},{5,1},{9,5},{13... | collective-permute-start | bytes 1179656 | tf_op jit(solution)/shard_map/while/body/eval_jaxpr/ppermute | solution.py:13
  190.9 11.6 %collective-permute-start.1 = (f32[2,6,64,128]{3,2,1,0:T(8,128)S(1)}, f32[2,6,64,128]{3,2,1,0:T(8,128)S(1)}, u32[]{:S(2)}, u32[]{:S(2)}) collective-permute-start(f32[2,6,64,128]{3,2,1,0:T(8,128)S(1)} %multiply_add_fusion.8), channel_id=1, source_target_pairs={{4,0},{8,4},{12,8},{16,12},{20,16},{24,20},{28,24},{5,1},{9,5},{13... | collective-permute-start | bytes 1179656 | tf_op jit(solution)/shard_map/while/body/eval_jaxpr/ppermute | solution.py:13
  202.6 10.7 %collective-permute-start.1 = (f32[2,6,64,128]{3,2,1,0:T(8,128)S(1)}, f32[2,6,64,128]{3,2,1,0:T(8,128)S(1)}, u32[]{:S(2)}, u32[]{:S(2)}) collective-permute-start(f32[2,6,64,128]{3,2,1,0:T(8,128)S(1)} %multiply_add_fusion.8), channel_id=1, source_target_pairs={{4,0},{8,4},{12,8},{16,12},{20,16},{24,20},{28,24},{5,1},{9,5},{13... | collective-permute-start | bytes 1179656 | tf_op jit(solution)/shard_map/while/body/eval_jaxpr/ppermute | solution.py:13
  213.4 10.3 %collective-permute-start.1 = (f32[2,6,64,128]{3,2,1,0:T(8,128)S(1)}, f32[2,6,64,128]{3,2,1,0:T(8,128)S(1)}, u32[]{:S(2)}, u32[]{:S(2)}) collective-permute-start(f32[2,6,64,128]{3,2,1,0:T(8,128)S(1)} %multiply_add_fusion.8), channel_id=1, source_target_pairs={{4,0},{8,4},{12,8},{16,12},{20,16},{24,20},{28,24},{5,1},{9,5},{13... | collective-permute-start | bytes 1179656 | tf_op jit(solution)/shard_map/while/body/eval_jaxpr/ppermute | solution.py:13
  223.8 11.1 %collective-permute-start.1 = (f32[2,6,64,128]{3,2,1,0:T(8,128)S(1)}, f32[2,6,64,128]{3,2,1,0:T(8,128)S(1)}, u32[]{:S(2)}, u32[]{:S(2)}) collective-permute-start(f32[2,6,64,128]{3,2,1,0:T(8,128)S(1)} %multiply_add_fusion.8), channel_id=1, source_target_pairs={{4,0},{8,4},{12,8},{16,12},{20,16},{24,20},{28,24},{5,1},{9,5},{13... | collective-permute-start | bytes 1179656 | tf_op jit(solution)/shard_map/while/body/eval_jaxpr/ppermute | solution.py:13
  235.0 10.8 %collective-permute-start.1 = (f32[2,6,64,128]{3,2,1,0:T(8,128)S(1)}, f32[2,6,64,128]{3,2,1,0:T(8,128)S(1)}, u32[]{:S(2)}, u32[]{:S(2)}) collective-permute-start(f32[2,6,64,128]{3,2,1,0:T(8,128)S(1)} %multiply_add_fusion.8), channel_id=1, source_target_pairs={{4,0},{8,4},{12,8},{16,12},{20,16},{24,20},{28,24},{5,1},{9,5},{13... | collective-permute-start | bytes 1179656 | tf_op jit(solution)/shard_map/while/body/eval_jaxpr/ppermute | solution.py:13
  252.9 89.1 %all-reduce.8.cloned.1.call-start = ((), (), s32[]{:S(2)}) async-start(), calls=%async_computation.3 | async-start | bytes 3145728 | tf_op jit(solution)/shard_map/psum | solution.py:208
  290.3 5.7 %collective-permute-start.3 = (f32[2,3,640]{2,1,0:T(4,128)S(1)}, f32[2,3,640]{2,1,0:T(4,128)S(1)}, u32[]{:S(2)}, u32[]{:S(2)}) collective-permute-start(f32[2,3,640]{2,1,0:T(4,128)S(1)} %slice.132), channel_id=1, source_target_pairs={{4,0},{8,4},{12,8},{16,12},{20,16},{24,20},{28,24},{5,1},{9,5},{13... | collective-permute-start | bytes 46088 | tf_op jit(solution)/shard_map/ppermute | solution.py:13
  299.0 84.4 %reduce-scatter.2.cloned.1.call-start = ((), (), s32[]{:S(2)}) async-start(), calls=%async_computation.1 | async-start | bytes 1966080 | tf_op jit(solution)/shard_map/reduce_scatter | solution.py:123
  302.2 236.4 %all-reduce.10.cloned.1.call-start = ((), (), s32[]{:S(2)}) async-start(), calls=%async_computation.4 | async-start | bytes 8650752 | tf_op jit(solution)/shard_map/psum | solution.py:216
  309.9 32.1 %copy-start.8 = (f32[512,768]{0,1:T(8,128)S(1)}, f32[512,768]{0,1:T(8,128)}, u32[]{:S(2)}) copy-start(f32[512,768]{0,1:T(8,128)} %get-tuple-element.216) | copy-start | bytes 4718596
  309.9 32.1 %slice-start = ((bf16[2,256,640]{2,1,0:T(8,128)(2,1)}), bf16[2,256,256]{2,1,0:T(8,128)(2,1)S(1)}, s32[]{:S(2)}) async-start(bf16[2,256,640]{2,1,0:T(8,128)(2,1)} %copy-done.23), calls=%async_computation.5 | async-start | bytes 524288 | tf_op jit(solution)/shard_map/slice | solution.py:199
  311.5 32.7 %copy-start.55 = (f32[4,640]{1,0:T(4,128)}, f32[4,640]{1,0:T(4,128)S(1)}, u32[]{:S(2)}) copy-start(f32[4,640]{1,0:T(4,128)S(1)} %pad_maximum_fusion.4) | copy-start | bytes 30724
  (81 other events, 223.8 us)
Sparse Core Ops, SparseCore 0:
  253.1 34.0 all-reduce.5
  299.1 42.8 all-reduce.7
  344.6 28.2 reduce-scatter.1
  378.3 160.3 all-reduce.9
where the time goes:
time: 553 us; the launch traced here: 552 us
  waiting for transfers between devices  328 us (59%)
  blocking collectives  59.2 us (11%)
  matrix products  55.6 us (10%)
  starting transfers between devices  49 us (9%)
  local copies, waits for them, and re-layouts  27 us (5%)
  other arithmetic  18 us (3%)
  between operations  15 us (3%)
    psum x1, waiting for transfers between devices, on_device(): lax.psum((grad_norm_gain, weight_grad(normed_low, grad_gate_low), weight_...  153 us
    ppermute x16, waiting for transfers between devices, from_behind(): return lax.ppermute(x, axis, pairs)  122 us
    ppermute x16, starting transfers between devices, from_behind(): return lax.ppermute(x, axis, pairs)  48.6 us
    psum x1, blocking collectives, on_device(): lax.psum((grad_norm_gain, weight_grad(normed_low, grad_gate_low), weight_...  38.2 us
    dot_general x14, matrix products, fine_sum(): jnp.einsum(form, *operands, precision=HIGHEST, preferred_element_type=jnp...  32.3 us
    psum x1, waiting for transfers between devices, on_device(): lax.psum(head_part, 'head') + back_rows(grad_state_low, state_proj)  30.5 us
    psum x1, waiting for transfers between devices, on_device(): state_total = lax.psum(jnp.concatenate([grad_b, grad_c], axis=-1), 'head')  22.3 us
    unnamed x189, local copies, waits for them, and re-layouts  14.1 us
  transfers between devices with their start and end apart: 20, of which 18 were waited for; matrix products, arithmetic and copies ran while one was open for 5% of the time, Pallas kernels for 0%

commit v1 on v0

v1 whole, which is shorter than its diff:
```python
import functools

import jax
import jax.numpy as jnp
from jax import lax
from jax.experimental import pallas as pl
from jax.experimental.pallas import tpu as pltpu
from jax.sharding import PartitionSpec as P

EPS = 1e-05
F32 = jnp.float32
BF16 = jnp.bfloat16
NN = ((1,), (0,))
NT = ((1,), (1,))
TN = ((0,), (0,))
PAD = 16
LANES = 128


def shift(x, axis, by):
    devices = lax.axis_size(axis)
    pairs = [(i, i + by) for i in range(devices) if 0 <= i + by < devices]
    return lax.ppermute(x, axis, pairs)


def swap(x, axis, mask):
    devices = lax.axis_size(axis)
    return lax.ppermute(x, axis, [(i, i ^ mask) for i in range(devices)])


def masks(axis):
    found, mask = [], 1
    while mask < lax.axis_size(axis):
        found.append(mask)
        mask *= 2
    return found


def sum_all(x, axis):
    for mask in masks(axis):
        x = x + swap(x, axis, mask)
    return x


def orders(axis_size):
    near = [1 << t for t in range(axis_size.bit_length() - 1)]
    return near, near[1:2] + near[:1] + near[2:]


def places(order):
    bits = len(order)
    return [
        sum(((p >> (bits - 1 - t)) & 1) * order[t] for t in range(bits))
        for p in range(1 << bits)
    ]


def add_wide(left, right):
    return (left.astype(F32) + right.astype(F32)).astype(left.dtype)


class Reduce:
    def __init__(self, keep, send, axis, order):
        self.keep, self.send, self.axis, self.order = keep, send, axis, list(order)

    def step(self, after=()):
        got = swap(self.send, self.axis, self.order.pop(0))
        got = lax.optimization_barrier((got, after))[0]
        half = self.keep.shape[0] // 2
        if half == 0:
            self.keep, self.send = add_wide(self.keep[0], got[0]), None
        else:
            self.send = add_wide(self.keep[half:], got[half:])
            self.keep = add_wide(self.keep[:half], got[:half])

    def finish(self):
        while self.order:
            self.step()
        return self.keep


class Gather:
    def __init__(self, x, axis, order):
        self.near, self.far, self.axis, self.order = x[None], None, axis, list(order)

    def step(self):
        if self.far is not None:
            self.near = jnp.concatenate([self.near, self.far], axis=0)
        self.far = swap(self.near, self.axis, self.order.pop())

    def finish(self):
        while self.order:
            self.step()
        return self.near, self.far


def hold(x, *chains):
    held = [(c.keep, c.send) if isinstance(c, Reduce) else (c.near, c.far) for c in chains]
    x, held = lax.optimization_barrier((x, held))
    for chain, state in zip(chains, held):
        if isinstance(chain, Reduce):
            chain.keep, chain.send = state
        else:
            chain.near, chain.far = state
    return x


def dot(left, right, dims=NN):
    return lax.dot_general(left, right, (dims, ((), ())), preferred_element_type=F32)


def parts(x, count):
    found = []
    for _ in range(count):
        term = x.astype(BF16)
        found.append(term)
        x = x - term.astype(F32)
    return found


def dot_fine(left, right, dims=NN):
    left_high, left_low = parts(left, 2)
    right_high, right_low = parts(right, 2)
    return (
        dot(left_high, right_high, dims)
        + dot(left_low, right_high, dims)
        + dot(left_high, right_low, dims)
    )


def dot_left(left, right, dims=NN, count=2):
    return sum(dot(term, right, dims) for term in parts(left, count))


def dot_right(left, right, dims=NN, count=2):
    return sum(dot(left, term, dims) for term in parts(right, count))


def silu(x):
    return x * jax.nn.sigmoid(x)


def silu_slope(inputs):
    sigma = jax.nn.sigmoid(inputs)
    return sigma * (1.0 + inputs * (1.0 - sigma))


def softplus(x):
    return jnp.maximum(x, 0.0) + jnp.log1p(jnp.exp(-jnp.abs(x)))


def iota(shape, dim):
    return lax.broadcasted_iota(jnp.int32, shape, dim)


def spread(heads, inner):
    lane, head = iota((heads, inner), 1), iota((heads, inner), 0)
    size = inner // heads
    inside = (lane >= head * size) & (lane < (head + 1) * size)
    return jnp.where(inside, 1.0, 0.0).astype(BF16)


def lane_blocks(heads, inner):
    size = inner // heads
    for start in range(0, inner, LANES):
        stop = min(start + LANES, inner)
        yield start, stop, range(start // size, stop // size)


def head_lanes(start, stop, head, size, length):
    lane = iota((length, stop - start), 1) + start
    return (lane >= head * size) & (lane < (head + 1) * size)


def local(body, outs, args, scratch=(), steps=1, flops=100_000_000):
    def spec(shape, dim, smem=False):
        if smem:
            return pl.BlockSpec(memory_space=pltpu.SMEM)
        block = [size // steps if at == dim else size for at, size in enumerate(shape)]
        return pl.BlockSpec(
            tuple(block),
            lambda step, dim=dim: tuple(step if at == dim else 0 for at in range(len(shape))),
        )

    pairs = [a if isinstance(a, tuple) else (a, None) for a in args]
    trio = [o if len(o) == 3 else (*o, None) for o in outs]
    size = sum(a.size * a.dtype.itemsize for a, _ in pairs)
    return pl.pallas_call(
        body,
        grid=(steps,),
        out_shape=[jax.ShapeDtypeStruct(shape, dtype) for shape, dtype, _ in trio],
        in_specs=[spec(a.shape, dim, a.dtype == jnp.int32) for a, dim in pairs],
        out_specs=[spec(shape, dim) for shape, _, dim in trio],
        scratch_shapes=list(scratch),
        compiler_params=pltpu.CompilerParams(vmem_limit_bytes=60 * 2**20),
        cost_estimate=pl.CostEstimate(
            flops=flops, bytes_accessed=size // 4, transcendentals=0
        ),
    )(*[a for a, _ in pairs])


def accumulate(ref, value):
    first = pl.program_id(0) == 0

    @pl.when(first)
    def _():
        ref[...] = value

    @pl.when(jnp.logical_not(first))
    def _():
        ref[...] += value


def as_row(ref):
    return ref[...].reshape(1, -1)


def as_column(row):
    count = row.shape[1]
    eye = iota((count, count), 0) == iota((count, count), 1)
    return jnp.sum(jnp.where(eye, row, 0.0), axis=1, keepdims=True)


def first_kernel(
    tokens_ref,
    edge_ref,
    gain_ref,
    value_proj_ref,
    state_proj_ref,
    step_proj_ref,
    conv_value_ref,
    conv_value_bias_ref,
    conv_state_ref,
    conv_state_bias_ref,
    step_bias_ref,
    decay_log_ref,
    normed_ref,
    value_in_ref,
    state_in_ref,
    values_ref,
    states_ref,
    value_slope_ref,
    state_slope_ref,
    step_x_ref,
    exp_cum_x_ref,
    end_x_ref,
    cum_ref,
    cum_t_ref,
    step_arg_t_ref,
    ends_ref,
):
    _, length, _ = tokens_ref.shape
    inner = values_ref.shape[2]
    heads = cum_ref.shape[2]
    nstate = states_ref.shape[2] // 2
    blocks, share = ends_ref.shape[0], ends_ref.shape[1] - 8
    spread_mat = spread(heads, inner)
    row, col = iota((length, length), 0), iota((length, length), 1)
    lower = jnp.where(row >= col, 1.0, 0.0).astype(BF16)
    upper = jnp.where(row <= col, 1.0, 0.0).astype(BF16)
    step_bias = as_row(step_bias_ref)
    rate = jnp.exp(as_row(decay_log_ref))
    for source, first, count in ((edge_ref, 0, PAD), (tokens_ref, PAD, length)):
        x = source[0].astype(F32)
        scale = lax.rsqrt(jnp.mean(x * x, axis=-1, keepdims=True) + EPS)
        normed_ref[0, first : first + count] = (x * scale * as_row(gain_ref)).astype(BF16)
    normed = normed_ref[0, PAD:]
    step_arg = dot(normed, step_proj_ref[...], NT) + step_bias
    step_arg_t = dot(step_proj_ref[...], normed, NT) + as_column(step_bias)
    step_arg_t_ref[0] = step_arg_t
    step = softplus(step_arg)
    cum = dot_right(lower, -step * rate, NN, 3)
    cum_ref[0] = cum
    cum_t_ref[0] = dot_left(-softplus(step_arg_t) * as_column(rate), upper, NN, 3)
    step_x = dot_left(step, spread_mat)
    exp_cum_x = dot_left(jnp.exp(cum), spread_mat)
    end_x = dot_left(jnp.exp(cum[length - 1 :] - cum), spread_mat)
    step_x_ref[0] = step_x
    exp_cum_x_ref[0] = exp_cum_x
    end_x_ref[0] = end_x

    def convolve(proj_ref, weight_ref, bias_ref, in_ref, out_ref, slope_ref):
        taps = weight_ref.shape[0]
        in_ref[0] = dot(normed_ref[0], proj_ref[...])
        conv_out = as_row(bias_ref)
        for tap in range(taps):
            first = PAD - taps + 1 + tap
            conv_out = conv_out + weight_ref[tap : tap + 1] * in_ref[0, first : first + length]
        sigma = jax.nn.sigmoid(conv_out)
        slope_ref[0] = sigma * (1.0 + conv_out * (1.0 - sigma))
        out_ref[0] = conv_out * sigma

    convolve(
        state_proj_ref,
        conv_state_ref,
        conv_state_bias_ref,
        state_in_ref,
        states_ref,
        state_slope_ref,
    )
    convolve(
        value_proj_ref,
        conv_value_ref,
        conv_value_bias_ref,
        value_in_ref,
        values_ref,
        value_slope_ref,
    )
    ends = dot_fine(states_ref[0, :, :nstate], end_x * step_x * values_ref[0], TN)
    for block in range(blocks):
        ends_ref[block, 0:8] = jnp.broadcast_to(exp_cum_x[length - 1 :], (8, inner))
        ends_ref[block, 8:] = ends[block * share : (block + 1) * share]


def scan_kernel(got_ref, entering_ref):
    running = jnp.zeros(entering_ref.shape[1:], F32)
    for block in range(got_ref.shape[0]):
        entering_ref[block] = running
        running = got_ref[block, 0:1] * running + got_ref[block, 8:]


def back_scan_kernel(got_ref, back_ref, leaving_ref):
    running = jnp.zeros(leaving_ref.shape[1:], F32)
    for block in reversed(range(got_ref.shape[0])):
        leaving_ref[block] = running
        running = got_ref[block, 0:1] * running + back_ref[block]


def inside_kernel(
    normed_ref,
    gate_proj_ref,
    values_ref,
    states_ref,
    step_x_ref,
    cum_ref,
    cum_t_ref,
    cot_ref,
    out_proj_ref,
    skip_ref,
    base_ref,
    gnorm_ref,
    gate_pre_ref,
):
    seqs, length, inner = base_ref.shape
    heads = cum_ref.shape[2]
    size = inner // heads
    nstate = states_ref.shape[2] // 2
    skip = dot_left(as_row(skip_ref), spread(heads, inner), NN, 3)
    causal = iota((length, length), 0) >= iota((length, length), 1)
    for seq in range(seqs):
        gate_pre_ref[seq] = dot(normed_ref[seq, PAD:], gate_proj_ref[...])
        products = dot_fine(states_ref[seq, :, nstate:], states_ref[seq, :, :nstate], NT)
        for start, stop, block_heads in lane_blocks(heads, inner):
            values = values_ref[seq, :, start:stop]
            scaled = parts(values * step_x_ref[seq, :, start:stop], 2)
            total = None
            for head in block_heads:
                gap = cum_ref[seq, :, head : head + 1] - cum_t_ref[seq, head : head + 1, :]
                decay = jnp.exp(jnp.where(causal, gap, -1e30))
                high, low = parts(decay * products, 2)
                part = dot(high, scaled[0]) + dot(low, scaled[0]) + dot(high, scaled[1])
                if total is None:
                    total = part
                else:
                    total = jnp.where(head_lanes(start, stop, head, size, length), part, total)
            base_ref[seq, :, start:stop] = total + skip[:, start:stop] * values
        gnorm_ref[seq] = dot(cot_ref[seq * length : (seq + 1) * length], out_proj_ref[...], NT)


def read_kernel(
    state_ref,
    states_ref,
    exp_cum_x_ref,
    base_ref,
    gate_pre_ref,
    gnorm_ref,
    out_gain_ref,
    read_ref,
    sums_ref,
):
    seqs, length, inner = base_ref.shape
    nstate = states_ref.shape[2] // 2
    ones = jnp.ones((8, inner), BF16)
    for seq in range(seqs):
        read = exp_cum_x_ref[seq] * dot_fine(states_ref[seq, :, nstate:], state_ref[seq])
        read_ref[seq] = read
        gated = (base_ref[seq] + read) * silu(gate_pre_ref[seq])
        squares = dot_right(ones, gated * gated, NT)
        backs = dot_right(ones, gnorm_ref[seq] * as_row(out_gain_ref) * gated, NT)
        row = iota((8, length), 0)
        sums_ref[:, seq * length : (seq + 1) * length] = jnp.where(row == 0, squares, backs)


def gate_kernel(
    sums_ref,
    read_ref,
    base_ref,
    gate_pre_ref,
    gnorm_ref,
    out_gain_ref,
    exp_cum_x_ref,
    states_ref,
    grad_scan_ref,
    back_ref,
    *,
    inner_total,
):
    nstate = states_ref.shape[2] // 2
    blocks, share = back_ref.shape[0], back_ref.shape[1]
    sums = jnp.transpose(sums_ref[...])
    scale = lax.rsqrt(sums[:, 0:1] / inner_total + EPS)
    back_mean = scale * sums[:, 1:2] / inner_total
    gate_act = silu(gate_pre_ref[0])
    unit = (base_ref[0] + read_ref[0]) * gate_act * scale
    grad_gated = scale * (gnorm_ref[0] * as_row(out_gain_ref) - unit * back_mean)
    grad_scan = grad_gated * gate_act
    grad_scan_ref[0] = grad_scan
    back = dot_fine(states_ref[0, :, nstate:], exp_cum_x_ref[0] * grad_scan, TN)
    for block in range(blocks):
        back_ref[block] = back[block * share : (block + 1) * share]


def cut_lines(held, value):
    count = held.shape[1]
    for piece in range(held.shape[0]):
        held[piece] = value[piece * count : (piece + 1) * count]


def stacked(lines, lanes):
    return [lines[:, at : at + lanes] for at in range(0, lines.shape[1], lanes)]


def ordered_piece(own, at, value, keep_ref, send_ref):
    half = keep_ref.shape[0]
    for p, mask in enumerate(places(orders(2 * half)[0])):

        @pl.when((own ^ mask) == at)
        def _():
            (keep_ref if p < half else send_ref)[p % half] = value


def low_kernel(
    own_ref,
    sums_ref,
    read_ref,
    base_ref,
    gate_pre_ref,
    gnorm_ref,
    out_gain_ref,
    grad_scan_ref,
    values_ref,
    normed_ref,
    cot_ref,
    out_proj_ref,
    grad_gate_ref,
    rows_ref,
    keep_ref,
    send_ref,
    branch_keep_ref,
    branch_send_ref,
    gate_low,
    grad_gate_proj,
    grad_out_proj,
    *,
    inner_total,
):
    seqs, length, inner = base_ref.shape
    gain_sum = jnp.zeros((1, inner), F32)
    skip_sum = jnp.zeros((1, inner), F32)
    pieces = 2 * branch_keep_ref.shape[0]
    col_width = branch_keep_ref.shape[2]
    total = None
    for seq in range(seqs):
        sums = jnp.transpose(sums_ref[:, seq * length : (seq + 1) * length])
        scale = lax.rsqrt(sums[:, 0:1] / inner_total + EPS)
        back_mean = scale * sums[:, 1:2] / inner_total
        gate_pre = gate_pre_ref[seq]
        sigma = jax.nn.sigmoid(gate_pre)
        scan_out = base_ref[seq] + read_ref[seq]
        unit = scan_out * gate_pre * sigma * scale
        gnorm = gnorm_ref[seq]
        gate_low[seq * length : (seq + 1) * length] = (unit * as_row(out_gain_ref)).astype(BF16)
        grad_gated = scale * (gnorm * as_row(out_gain_ref) - unit * back_mean)
        slope = sigma * (1.0 + gate_pre * (1.0 - sigma))
        grad_gate = (grad_gated * scan_out * slope).astype(BF16)
        grad_gate_ref[seq] = grad_gate
        part = dot(normed_ref[seq, PAD:], grad_gate, TN)
        total = part if total is None else total + part
        gain_sum = gain_sum + jnp.sum(gnorm * unit, axis=0, keepdims=True)
        skip_sum = skip_sum + jnp.sum(
            grad_scan_ref[seq] * values_ref[seq], axis=0, keepdims=True
        )
    rows_ref[:, :inner] = gain_sum
    rows_ref[:, inner:] = skip_sum
    cut_lines(grad_gate_proj, total)
    cut_lines(grad_out_proj, dot(gate_low[...], cot_ref[...], TN))
    blocks = 2 * keep_ref.shape[0]
    for p, mask in enumerate(places(orders(blocks)[0])):
        at = own_ref[0] ^ mask
        ref = keep_ref if p < blocks // 2 else send_ref
        value = jnp.concatenate(
            [grad_gate_proj[at], *stacked(grad_out_proj[at], inner)], axis=0
        )
        ref[p % (blocks // 2)] = value.astype(BF16)
    branch = dot(gate_low[...], out_proj_ref[...])
    for piece in range(pieces):
        value = branch[:, piece * col_width : (piece + 1) * col_width].astype(BF16)
        ordered_piece(own_ref[1], piece, value, branch_keep_ref, branch_send_ref)


def mix_kernel(
    values_ref,
    states_ref,
    step_x_ref,
    exp_cum_x_ref,
    cum_ref,
    cum_t_ref,
    grad_scan_ref,
    state_ref,
    scaled_grad_ref,
    grad_b_ref,
    grad_c_ref,
    gaps_ref,
):
    seqs, length, inner = grad_scan_ref.shape
    heads = cum_ref.shape[2]
    size = inner // heads
    nstate = states_ref.shape[2] // 2
    causal = iota((length, length), 0) >= iota((length, length), 1)
    ones = jnp.ones((8, length), BF16)
    for seq in range(seqs):
        b_rows = states_ref[seq, :, :nstate]
        c_rows = states_ref[seq, :, nstate:]
        products = dot_fine(c_rows, b_rows, NT)
        grad_products = jnp.zeros((length, length), F32)
        for start, stop, block_heads in lane_blocks(heads, inner):
            scaled = values_ref[seq, :, start:stop] * step_x_ref[seq, :, start:stop]
            scaled_high, scaled_low = parts(scaled, 2)
            scan_high, scan_low = parts(grad_scan_ref[seq, :, start:stop], 2)
            total = None
            for head in block_heads:
                gap = cum_ref[seq, :, head : head + 1] - cum_t_ref[seq, head : head + 1, :]
                decay = jnp.exp(jnp.where(causal, gap, -1e30))
                own = head_lanes(start, stop, head, size, length)
                own_high = jnp.where(own, scan_high, jnp.zeros_like(scan_high))
                own_low = jnp.where(own, scan_low, jnp.zeros_like(scan_low))
                grad_mix = (
                    dot(own_high, scaled_high, NT)
                    + dot(own_low, scaled_high, NT)
                    + dot(own_high, scaled_low, NT)
                )
                grad_decayed = grad_mix * decay
                grad_products = grad_products + grad_decayed
                related = (grad_decayed * products).astype(BF16)
                gaps = dot(ones, related, NT) - dot(ones, related)
                gaps_ref[seq, head : head + 1] = gaps[0:1]
                part = dot((decay * products).astype(BF16), own_high, TN)
                total = part if total is None else total + part
            scaled_grad_ref[seq, :, start:stop] = total
        carried = exp_cum_x_ref[seq] * grad_scan_ref[seq]
        grad_c_ref[seq] = dot_fine(grad_products, b_rows) + dot_fine(
            carried, state_ref[seq], NT
        )
        grad_b_ref[seq] = dot_fine(grad_products, c_rows, TN)


def state_sum_kernel(
    own_ref,
    grad_end_ref,
    values_ref,
    step_x_ref,
    end_x_ref,
    grad_b_ref,
    grad_c_ref,
    keep_ref,
    send_ref,
):
    pieces, part = 2 * keep_ref.shape[0], keep_ref.shape[2]
    weighted = end_x_ref[0] * step_x_ref[0] * values_ref[0]
    grad_b = grad_b_ref[0] + dot_fine(weighted, grad_end_ref[0], NT)
    both = jnp.concatenate([grad_b, grad_c_ref[0]], axis=1)
    for piece in range(pieces):
        value = both[:, piece * part : (piece + 1) * part]
        ordered_piece(own_ref[1], piece, value, keep_ref, send_ref)


def conv_back(grad_out, in_ref, weight_ref, seq, around):
    length = grad_out.shape[0]
    taps = weight_ref.shape[0]
    around[PAD : PAD + length] = grad_out
    grad_in = None
    sums = []
    for tap in range(taps):
        first = PAD - taps + 1 + tap
        sums.append(
            jnp.sum(grad_out * in_ref[seq, first : first + length], axis=0, keepdims=True)
        )
        first = taps - 1 - tap
        part = weight_ref[tap : tap + 1] * around[first : first + PAD + length]
        grad_in = part if grad_in is None else grad_in + part
    sums.append(jnp.sum(grad_out, axis=0, keepdims=True))
    return grad_in, jnp.concatenate(sums, axis=0)


def clear_edges(around):
    zeros = jnp.zeros((PAD, around.shape[1]), F32)
    around[0:PAD] = zeros
    around[around.shape[0] - PAD :] = zeros


def value_kernel(
    grad_end_ref,
    state_ref,
    values_ref,
    states_ref,
    slope_ref,
    conv_in_ref,
    conv_weight_ref,
    step_x_ref,
    exp_cum_x_ref,
    end_x_ref,
    step_arg_t_ref,
    decay_log_ref,
    skip_ref,
    read_ref,
    grad_scan_ref,
    scaled_grad_ref,
    gaps_ref,
    grad_in_ref,
    grad_step_t_ref,
    conv_rows_ref,
    head_rows_ref,
    around,
):
    _, length, inner = values_ref.shape
    heads = gaps_ref.shape[1]
    nstate = states_ref.shape[2] // 2
    spread_mat = spread(heads, inner)
    row, col = iota((length, length), 0), iota((length, length), 1)
    lower = jnp.where(row >= col, 1.0, 0.0).astype(BF16)
    rate_t = as_column(jnp.exp(as_row(decay_log_ref)))
    skip = dot_left(as_row(skip_ref), spread_mat, NN, 3)
    last = iota((heads, length), 1) == length - 1
    clear_edges(around)
    values = values_ref[0]
    grad_end = grad_end_ref[0]
    step_x = step_x_ref[0]
    grad_scan = grad_scan_ref[0]
    end_proj = end_x_ref[0] * dot(
        states_ref[0, :, :nstate].astype(BF16), grad_end.astype(BF16)
    )
    scaled_grad = scaled_grad_ref[0] + end_proj
    grad_in, conv_rows = conv_back(
        (skip * grad_scan + step_x * scaled_grad) * slope_ref[0],
        conv_in_ref,
        conv_weight_ref,
        0,
        around,
    )
    grad_in_ref[0] = grad_in
    end_terms = dot_right(spread_mat, step_x * values * end_proj, NT)
    crossed = jnp.sum(grad_end * state_ref[0], axis=0, keepdims=True)
    crossed = crossed * exp_cum_x_ref[0, length - 1 :]
    last_term = jnp.sum(end_terms, axis=1, keepdims=True) + jnp.sum(
        jnp.where(spread_mat.astype(F32) > 0.0, crossed, 0.0), axis=1, keepdims=True
    )
    grad_cum = (
        gaps_ref[0] + dot_right(spread_mat, grad_scan * read_ref[0], NT) - end_terms
    ) + jnp.where(last, last_term, 0.0)
    grad_log = dot_left(grad_cum, lower, NN, 3)
    step_arg = step_arg_t_ref[0]
    rate_sum = -jnp.sum(grad_log * softplus(step_arg), axis=1, keepdims=True)
    grad_step = dot_right(spread_mat, values * scaled_grad, NT) - grad_log * rate_t
    grad_step = grad_step * jax.nn.sigmoid(step_arg)
    bias_sum = jnp.sum(grad_step, axis=1, keepdims=True)
    grad_step_t_ref[0] = grad_step.astype(BF16)
    lane = iota((heads, LANES), 1)
    accumulate(conv_rows_ref, conv_rows)
    accumulate(head_rows_ref, jnp.where(lane == 0, bias_sum, rate_sum * rate_t))


def weight_kernel(
    normed_ref,
    value_in_ref,
    grad_step_t_ref,
    state_grad_ref,
    slope_ref,
    conv_in_ref,
    conv_weight_ref,
    state_in_ref,
    conv_rows_ref,
    step_rows_ref,
    late_ref,
    around,
):
    seqs, length, _ = slope_ref.shape
    width = normed_ref.shape[2]
    blocks, _, inner = late_ref.shape
    value_total = state_total = step_total = conv_total = None

    def add(total, part):
        return part if total is None else total + part

    clear_edges(around)
    for seq in range(seqs):
        normed = normed_ref[seq]
        grad = state_grad_ref[seq * length : (seq + 1) * length] * slope_ref[seq]
        grad_in, conv_rows = conv_back(grad, conv_in_ref, conv_weight_ref, seq, around)
        state_in_ref[seq] = grad_in
        conv_total = add(conv_total, conv_rows)
        value_total = add(value_total, dot(normed, value_in_ref[seq].astype(BF16), TN))
        state_total = add(state_total, dot(grad_in.astype(BF16), normed, TN))
        step_total = add(step_total, dot(grad_step_t_ref[seq], normed_ref[seq, PAD:]))
    conv_rows_ref[...] = conv_total
    step_rows_ref[...] = step_total
    value_lines = width // blocks
    state_lines = state_total.shape[0] // blocks
    for block in range(blocks):
        value = value_total[block * value_lines : (block + 1) * value_lines]
        state = state_total[block * state_lines : (block + 1) * state_lines]
        value = jnp.concatenate([value, *stacked(state, inner)], axis=0)
        late_ref[block] = value.astype(BF16)


def sum_kernel(got_ref, value_ref, state_ref):
    total = got_ref[0].astype(F32)
    for block in range(1, got_ref.shape[0]):
        total = total + got_ref[block].astype(F32)
    total = total.astype(BF16)
    lines = value_ref.shape[1]
    for block in range(value_ref.shape[0]):
        value_ref[block] = total[:lines]
    state_ref[...] = total[lines:]


def place_kernel(own_ref, near_ref, far_ref, gate_ref, out_ref):
    blocks, lines, inner = gate_ref.shape
    count = out_ref.shape[1]
    for p, mask in enumerate(places(orders(blocks)[0])):
        ref = near_ref if p < blocks // 2 else far_ref
        value = ref[p % (blocks // 2)].astype(F32)
        at = own_ref[0] ^ mask
        gate_ref[at] = value[:lines]
        for group in range(out_ref.shape[2] // inner):
            first = lines + group * count
            out_ref[at, :, group * inner : (group + 1) * inner] = value[first : first + count]


def place_state_kernel(own_ref, near_ref, far_ref, out_ref, held):
    half, pieces, _, inner = near_ref.shape
    _, each, width = held.shape
    for p, mask in enumerate(places(orders(2 * half)[0])):
        ref = near_ref if p < half else far_ref
        for q, head_mask in enumerate(places(orders(pieces)[0])):
            value = ref[p % half, q].astype(F32)
            at = (own_ref[1] ^ head_mask) * 2 * half + (own_ref[0] ^ mask)
            for group in range(width // inner):
                held[at, :, group * inner : (group + 1) * inner] = value[
                    group * each : (group + 1) * each
                ]
    out_ref[...] = jnp.transpose(held[...].reshape(-1, width))


def back_kernel(
    own_ref,
    tokens_ref,
    gain_ref,
    value_in_ref,
    state_in_ref,
    value_over_ref,
    state_over_ref,
    value_proj_ref,
    state_proj_ref,
    grad_gate_ref,
    gate_proj_ref,
    grad_step_t_ref,
    step_proj_t_ref,
    keep_ref,
    send_ref,
    sums_ref,
    gain_sum_ref,
):
    _, length, width = tokens_ref.shape
    pieces, col_width = 2 * keep_ref.shape[0], keep_ref.shape[2]
    ones = jnp.ones((8, width), BF16)
    def whole(in_ref, over_ref, seq):
        return jnp.concatenate(
            [
                in_ref[seq, PAD:length].astype(BF16),
                (in_ref[seq, length:] + over_ref[seq]).astype(BF16),
            ],
            axis=0,
        )

    x = tokens_ref[0].astype(F32)
    unit = x * lax.rsqrt(jnp.mean(x * x, axis=-1, keepdims=True) + EPS)
    normed_grad = (
        dot(whole(value_in_ref, value_over_ref, 0), value_proj_ref[...], NT)
        + dot(whole(state_in_ref, state_over_ref, 0), state_proj_ref[...], NT)
        + dot(grad_gate_ref[0], gate_proj_ref[...], NT)
        + dot(grad_step_t_ref[0], step_proj_t_ref[...], TN)
    )
    accumulate(gain_sum_ref, jnp.sum(normed_grad * unit, axis=0, keepdims=True))
    unit_grad = normed_grad * as_row(gain_ref)
    sums_ref[...] = dot_right(ones, unit_grad * unit, NT)
    for piece in range(pieces):
        value = unit_grad[:, piece * col_width : (piece + 1) * col_width].astype(BF16)
        ordered_piece(own_ref[1], piece, value, keep_ref, send_ref)


def on_device(
    tokens,
    norm_gain,
    gate_proj,
    value_proj,
    state_proj,
    step_proj,
    conv_value,
    conv_value_bias,
    conv_state,
    conv_state_bias,
    step_bias,
    decay_log,
    skip_gain,
    out_gain,
    out_proj,
    cotangent,
):
    seqs, length, width = tokens.shape
    rows = seqs * length
    heads = step_proj.shape[1]
    inner = gate_proj.shape[1]
    head_dim = inner // heads
    nstate = state_proj.shape[1] // 2
    taps = conv_value.shape[0]
    channels = inner + 2 * nstate
    head_devices = lax.axis_size("head")
    blocks = lax.axis_size("seq")
    head_index = lax.axis_index("head")
    own = jnp.stack([lax.axis_index("seq"), head_index]).astype(jnp.int32)
    col_width = width // head_devices
    share = seqs * nstate // blocks
    part = 2 * nstate // head_devices
    full = (seqs, length, inner)
    inner_total = inner * head_devices

    def own_cols(x, size):
        return lax.dynamic_slice_in_dim(x, head_index * size, size, x.ndim - 1)

    def cut(*arrays):
        return [(x, 0) for x in arrays]

    edge_tokens = shift(tokens[:, length - PAD :, :], "seq", 1)
    step_proj_t = jnp.transpose(step_proj)
    (
        normed,
        value_conv_in,
        state_conv_in,
        values,
        states,
        value_slope,
        state_slope,
        step_x,
        exp_cum_x,
        end_x,
        cum,
        cum_t,
        step_arg_t,
        ends,
    ) = local(
        first_kernel,
        [
            ((seqs, PAD + length, width), BF16, 0),
            ((seqs, PAD + length, inner), F32, 0),
            ((seqs, PAD + length, 2 * nstate), F32, 0),
            (full, F32, 0),
            ((seqs, length, 2 * nstate), F32, 0),
            (full, F32, 0),
            ((seqs, length, 2 * nstate), F32, 0),
            (full, F32, 0),
            (full, F32, 0),
            (full, F32, 0),
            ((seqs, length, heads), F32, 0),
            ((seqs, heads, length), F32, 0),
            ((seqs, heads, length), F32, 0),
            ((blocks, 8 + share, inner), F32, 0),
        ],
        [
            *cut(tokens, edge_tokens),
            norm_gain,
            value_proj,
            state_proj,
            step_proj_t,
            conv_value,
            conv_value_bias,
            conv_state,
            conv_state_bias,
            step_bias,
            decay_log,
        ],
        steps=seqs,
    )
    got = lax.all_to_all(ends, "seq", 0, 0)
    cot_rows = cotangent.reshape(rows, col_width)
    cot_low, _ = lax.optimization_barrier((cot_rows.astype(BF16), ends))
    cot_low = lax.all_gather(cot_low, "head", axis=1, tiled=True)
    got, cot_low = lax.optimization_barrier((got, cot_low))
    (entering,) = local(scan_kernel, [((blocks, share, inner), F32)], [got])
    state_in = lax.all_to_all(entering, "seq", 0, 0).reshape(seqs, nstate, inner)
    base, gnorm, gate_pre = local(
        inside_kernel,
        [(full, F32, 0), (full, F32, 0), (full, F32, 0)],
        [
            (normed, 0),
            gate_proj,
            *cut(values, states, step_x, cum, cum_t, cot_low),
            out_proj,
            skip_gain,
        ],
        steps=seqs,
    )
    read, row_sums = local(
        read_kernel,
        [(full, F32, 0), ((8, rows), F32, 1)],
        [*cut(state_in, states, exp_cum_x, base, gate_pre, gnorm), out_gain],
        steps=seqs,
    )
    row_sums = sum_all(row_sums, "head")
    grad_scan, back = local(
        functools.partial(gate_kernel, inner_total=inner_total),
        [(full, F32, 0), ((blocks, share, inner), F32, 0)],
        [
            (row_sums, 1),
            *cut(read, base, gate_pre, gnorm),
            out_gain,
            *cut(exp_cum_x, states),
        ],
        steps=seqs,
    )
    got_back = lax.all_to_all(back, "seq", 0, 0)

    def halves(axis_size, lines, lanes, dtype=BF16, dim=None):
        return [((axis_size // 2, lines, lanes), dtype, dim)] * 2

    (
        grad_gate,
        inner_row,
        early_keep,
        early_send,
        branch_keep,
        branch_send,
    ) = local(
        functools.partial(low_kernel, inner_total=inner_total),
        [
            (full, BF16),
            ((1, 2 * inner), F32),
            *halves(blocks, 2 * (width // blocks), inner),
            *halves(head_devices, rows, col_width),
        ],
        [
            own,
            row_sums,
            read,
            base,
            gate_pre,
            gnorm,
            out_gain,
            grad_scan,
            values,
            normed,
            cot_low,
            out_proj,
        ],
        [
            pltpu.VMEM((rows, inner), BF16),
            pltpu.VMEM((blocks, width // blocks, inner), F32),
            pltpu.VMEM((blocks, inner // blocks, width), F32),
        ],
    )

    got_back = lax.optimization_barrier((got_back, early_send))[0]
    (leaving,) = local(back_scan_kernel, [((blocks, share, inner), F32)], [got, got_back])
    grad_end = lax.all_to_all(leaving, "seq", 0, 0).reshape(seqs, nstate, inner)
    near = orders(blocks)[0]
    near_head = orders(head_devices)[0]
    early_chain = Reduce(early_keep, early_send, "seq", near)
    branch_chain = Reduce(branch_keep, branch_send, "head", near_head)
    grad_scan = lax.optimization_barrier((grad_scan, leaving))[0]
    scaled_grad, grad_b, grad_c, gaps = local(
        mix_kernel,
        [
            (full, F32, 0),
            ((seqs, length, nstate), F32, 0),
            ((seqs, length, nstate), F32, 0),
            ((seqs, heads, length), F32, 0),
        ],
        cut(values, states, step_x, exp_cum_x, cum, cum_t, grad_scan, state_in),
        steps=seqs,
    )
    early_chain.step(after=(gaps, grad_end))
    state_keep, state_send = local(
        state_sum_kernel,
        halves(head_devices, rows, part, F32, 1),
        [own, *cut(grad_end, values, step_x, end_x, grad_b, grad_c)],
        steps=seqs,
    )
    state_part = Reduce(state_keep, state_send, "head", near_head).finish()
    value_in, grad_step_t, value_rows, head_rows = local(
        value_kernel,
        [
            ((seqs, PAD + length, inner), F32, 0),
            ((seqs, heads, length), BF16, 0),
            ((taps + 1, inner), F32),
            ((heads, LANES), F32),
        ],
        [
            *cut(grad_end, state_in, values, states, value_slope, value_conv_in),
            conv_value,
            *cut(step_x, exp_cum_x, end_x, step_arg_t),
            decay_log,
            skip_gain,
            *cut(read, grad_scan, scaled_grad, gaps),
        ],
        [pltpu.VMEM((length + 2 * PAD, inner), F32)],
        steps=seqs,
    )
    state_part = hold(state_part, early_chain)
    early_chain.step(after=(value_in,))
    value_lines = width // blocks
    state_lines = part // blocks * (width // inner)
    state_grad_in, state_rows, step_rows, late = local(
        weight_kernel,
        [
            ((seqs, PAD + length, part), F32),
            ((taps + 1, part), F32),
            ((heads, width), F32),
            ((blocks, value_lines + state_lines, inner), BF16),
        ],
        [
            normed,
            value_in,
            grad_step_t,
            state_part,
            own_cols(state_slope, part),
            own_cols(state_conv_in, part),
            own_cols(conv_state, part),
        ],
        [pltpu.VMEM((length + 2 * PAD, part), F32)],
    )
    early_chain.step(after=(late,))
    early_chain = Gather(early_chain.finish(), "seq", near)
    early_chain.step()
    late = lax.all_to_all(late, "seq", 0, 0)
    over = jnp.concatenate([value_in[:, :PAD], state_grad_in[:, :PAD]], axis=2)
    over = shift(over, "seq", -1)
    late = hold(late, early_chain)
    early_chain.step()
    late_values, late_states = local(
        sum_kernel,
        [((blocks, value_lines, inner), BF16), ((state_lines, inner), BF16)],
        [late],
    )
    over = lax.optimization_barrier((over, late_values))[0]
    grad_value_proj = lax.all_to_all(late_values, "seq", 0, 0)
    keep, send, row_part, gain_sum = local(
        back_kernel,
        [
            *halves(head_devices, rows, col_width, BF16, 1),
            ((8, rows), F32, 1),
            ((1, width), F32),
        ],
        [
            own,
            (tokens, 0),
            norm_gain,
            *cut(value_in, state_grad_in, over[:, :, :inner], over[:, :, inner:]),
            value_proj,
            own_cols(state_proj, part),
            (grad_gate, 0),
            gate_proj,
            (grad_step_t, 0),
            step_proj_t,
        ],
        steps=seqs,
    )
    back_chain = Reduce(keep, send, "head", near_head)
    grad_value_proj = grad_value_proj.reshape(width, inner).astype(F32)
    grad_gate_proj, grad_out_proj = local(
        place_kernel,
        [
            ((blocks, value_lines, inner), F32),
            ((blocks, inner // blocks, width), F32),
        ],
        [own, *early_chain.finish()],
    )
    grad_gate_proj = grad_gate_proj.reshape(width, inner)
    grad_out_proj = grad_out_proj.reshape(inner, width)
    state_chain = Gather(late_states, "head", near_head)
    state_chain = Gather(jnp.concatenate(state_chain.finish(), axis=0), "seq", near)
    (grad_state_proj,) = local(
        place_state_kernel,
        [((width, 2 * nstate), F32)],
        [own, *state_chain.finish()],
        [pltpu.VMEM((blocks * head_devices, part // blocks, width), F32)],
    )
    branch = branch_chain.finish().astype(F32)
    own_source = own_cols(tokens.reshape(rows, width), col_width).astype(F32)
    mixed_rows = (own_source + branch).reshape(seqs, length, col_width)
    own_part = back_chain.finish().astype(F32)
    row_mean = sum_all(row_part, "head")[0][:, None] / width
    source = tokens.reshape(rows, width).astype(F32)
    own_scale = lax.rsqrt(jnp.mean(source * source, axis=-1, keepdims=True) + EPS)
    own_unit = own_source * own_scale
    grad_tokens = cot_rows + own_scale * (own_part - own_unit * row_mean)
    grad_tokens = grad_tokens.reshape(seqs, length, col_width)

    def padded(x, lines, lanes):
        return jnp.pad(x, ((0, lines - x.shape[0]), (0, lanes - x.shape[1])))

    state_rows = lax.dynamic_update_slice(
        jnp.zeros((taps + 1, 2 * nstate), F32), state_rows, (0, head_index * part)
    )
    lines = max(heads, taps + 1)
    lanes = max(width, channels + LANES)
    small = jnp.concatenate(
        [
            padded(step_rows, heads, lanes),
            padded(
                jnp.concatenate(
                    [
                        padded(value_rows, lines, inner),
                        padded(state_rows, lines, 2 * nstate),
                        padded(head_rows, lines, LANES),
                    ],
                    axis=1,
                ),
                lines,
                lanes,
            ),
            padded(inner_row, 1, lanes),
            padded(gain_sum, 1, lanes),
        ],
        axis=0,
    )
    small = sum_all(small, "seq")
    whole = sum_all(small[heads:], "head")
    conv_lines = small[heads : heads + lines]
    grad_heads = conv_lines[:heads, channels : channels + 2]
    grad_inner = small[heads + lines, : 2 * inner]
    return (
        mixed_rows,
        grad_tokens,
        whole[lines + 1, :width],
        grad_gate_proj,
        grad_value_proj,
        grad_state_proj,
        jnp.transpose(small[:heads, :width]),
        conv_lines[:taps, :inner],
        conv_lines[taps, :inner],
        whole[:taps, inner:channels],
        whole[taps, inner:channels],
        grad_heads[:, 0],
        grad_heads[:, 1],
        jnp.sum(grad_inner[inner:].reshape(heads, head_dim), axis=1),
        grad_inner[:inner],
        grad_out_proj,
    )


def solution(mesh):
    return jax.shard_map(
        on_device,
        mesh=mesh,
        in_specs=(
            P(None, "seq", None),
            P(),
            P(None, "head"),
            P(None, "head"),
            P(),
            P(None, "head"),
            P(None, "head"),
            P("head"),
            P(),
            P(),
            P("head"),
            P("head"),
            P("head"),
            P("head"),
            P("head", None),
            P(None, "seq", "head"),
        ),
        out_specs=(
            P(None, "seq", "head"),
            P(None, "seq", "head"),
            P(),
            P(None, "head"),
            P(None, "head"),
            P(),
            P(None, "head"),
            P(None, "head"),
            P("head"),
            P(),
            P(),
            P("head"),
            P("head"),
            P("head"),
            P("head"),
            P("head", None),
        ),
        check_vma=False,
    )
```

time: 553 us -> 225 us (0.41)
  waiting for transfers between devices: 328 us -> 54.2 us
  Pallas kernels: 0 us -> 66.1 us
  matrix products: 55.6 us -> 0 us
  blocking collectives: 59.2 us -> 8.6 us
  between operations: 15 us -> 1.1 us
  starting transfers between devices: 49 us -> 61.1 us
  other arithmetic: 18 us -> 11 us
    psum x3 -> x0, waiting for transfers between devices: 206 us -> none  [the longest x1 153 us: on_device(): lax.psum((grad_norm_gain, weight_grad(normed_low, grad_gate_low), weight_...]
    ppermute x16 -> x28, waiting for transfers between devices: 122 us -> 42.8 us  [the longest x26 41 us: swap(): return lax.ppermute(x, axis, [(i, i ^ mask) for i in range(devices)])]
    pallas_call x0 -> x15, Pallas kernels: none -> 66.1 us  [local(): pl.pallas_call(body, grid=(steps,), out_shape=[jax.ShapeDtypeStruct(shape...]
    dot_general x29 -> x0, matrix products: 55.6 us -> none  [the longest x14 32.3 us: fine_sum(): jnp.einsum(form, *operands, precision=HIGHEST, preferred_element_type=jnp...]
    psum x3 -> x0, blocking collectives: 50.2 us -> none  [the longest x1 38.2 us: on_device(): lax.psum((grad_norm_gain, weight_grad(normed_low, grad_gate_low), weight_...]
    all_to_all x0 -> x6, starting transfers between devices: none -> 26.3 us  [the longest x1 6.66 us: on_device(): got = lax.all_to_all(ends, 'seq', 0, 0)]
    ppermute x16 -> x28, starting transfers between devices: 48.6 us -> 34.8 us  [the longest x26 28.7 us: swap(): return lax.ppermute(x, axis, [(i, i ^ mask) for i in range(devices)])]
    all_to_all x0 -> x6, waiting for transfers between devices: none -> 11.4 us  [the longest x1 3.66 us: on_device(): got = lax.all_to_all(ends, 'seq', 0, 0)]
  transfers between devices with their start and end apart: 20 -> 34, of which waited for: 18 -> 16; matrix products, arithmetic and copies ran while one was open for 5% -> 10% of each run, Pallas kernels for 0% -> 21%
where the time goes in v1:
time: 225 us; the launch traced here: 224 us
  Pallas kernels  66.1 us (29%)
  starting transfers between devices  61.1 us (27%)
  waiting for transfers between devices  54.2 us (24%)
  local copies, waits for them, and re-layouts  21.5 us (10%)
  other arithmetic  11 us (5%)
  blocking collectives  8.6 us (4%)
    pallas_call x15, Pallas kernels, local(): pl.pallas_call(body, grid=(steps,), out_shape=[jax.ShapeDtypeStruct(shape...  66.1 us
    ppermute x26, waiting for transfers between devices, swap(): return lax.ppermute(x, axis, [(i, i ^ mask) for i in range(devices)])  41 us
    ppermute x26, starting transfers between devices, swap(): return lax.ppermute(x, axis, [(i, i ^ mask) for i in range(devices)])  28.7 us
    unnamed x74, local copies, waits for them, and re-layouts  8.89 us
    all_gather x1, blocking collectives, on_device(): cot_low = lax.all_gather(cot_low, 'head', axis=1, tiled=True)  8.6 us
    all_to_all x1, starting transfers between devices, on_device(): got = lax.all_to_all(ends, 'seq', 0, 0)  6.66 us
    ppermute x2, starting transfers between devices, shift(): return lax.ppermute(x, axis, pairs)  6.14 us
    all_to_all x1, starting transfers between devices, on_device(): late = lax.all_to_all(late, 'seq', 0, 0)  4.68 us
  transfers between devices with their start and end apart: 34, of which 16 were waited for; matrix products, arithmetic and copies ran while one was open for 10% of the time, Pallas kernels for 21%

profile of v1, /device:TPU:0, one launch (start us, length us, event | category | flops | bytes accessed | tf_op | source)
XLA Modules:
  0.0 223.7 jit_solution(14156039502997639593)
XLA Ops:
  1.5 4.9 %collective-permute-start = (bf16[2,16,768]{2,1,0:T(8,128)(2,1)S(1)}, bf16[2,16,768]{2,1,0:T(8,128)(2,1)S(1)}, u32[]{:S(2)}, u32[]{:S(2)}) collective-permute-start(bf16[2,16,768]{2,1,0:T(8,128)(2,1)S(1)} %slice.125), channel_id=1, source_target_pairs={{0,4},{4,8},{8,12},{12,16},{16,20},{20,24},{24,28},{1,5},{5,9},{9,... | collective-permute-start | bytes 147464 | tf_op jit(solution)/shard_map/ppermute | solution.py:23
  8.7 7.2 %shard_map.279 = (bf16[2,272,768]{2,1,0:T(8,128)(2,1)}, f32[2,272,384]{2,1,0:T(8,128)}, f32[2,272,256]{2,1,0:T(8,128)}, f32[2,256,384]{2,1,0:T(8,128)}, f32[2,25...) custom-call(bf16[2,256,768]{2,1,0:T(8,128)(2,1)} %tokens_ref.3, ...), custom_call_target="tpu_custom_call" | custom-call | flops 100000000 | bytes 460940 | tf_op jit(solution)/shard_map/pallas_call | solution.py:188
  15.9 6.7 %all-to-all-start = ((f32[8,40,384]{2,1,0:T(8,128)}), f32[8,40,384]{2,1,0:T(8,128)S(1)}, u32[]{:S(2)}, u32[]{:S(2)}) async-start(f32[8,40,384]{2,1,0:T(8,128)} %get-tuple-element.80), calls=%async_computation | async-start | bytes 983040 | tf_op jit(solution)/shard_map/all_to_all | solution.py:903
  22.9 8.6 %all_gather.3 = bf16[512,768]{0,1:T(8,128)(2,1)S(1)} all-gather(bf16[512,192]{0,1:T(8,128)(2,1)S(1)} %copy.39), channel_id=1, replica_groups=mesh['seq'=8,'head'=4] {'head'}, dimensions={1}, use_global_device_ids=true | all-gather | bytes 983040 | tf_op jit(solution)/shard_map/all_gather | solution.py:906
  31.5 3.7 %all-to-all-done.got_ref = f32[8,40,384]{2,1,0:T(8,128)S(1)} async-done(((f32[8,40,384]{2,1,0:T(8,128)}), f32[8,40,384]{2,1,0:T(8,128)S(1)}, u32[]{:S(2)}, u32[]{:S(2)}) %all-to-all-start) | async-done | bytes 491552 | tf_op jit(solution)/shard_map/all_to_all | solution.py:903
  37.8 3.7 %all-to-all-start.1 = ((f32[8,32,384]{2,1,0:T(8,128)}), f32[8,32,384]{2,1,0:T(8,128)S(1)}, u32[]{:S(2)}, u32[]{:S(2)}) async-start(f32[8,32,384]{2,1,0:T(8,128)} %shard_map.280), calls=%async_computation.1 | async-start | bytes 786432 | tf_op jit(solution)/shard_map/all_to_all | solution.py:909
  42.6 6.3 %shard_map.281 = (f32[2,256,384]{2,1,0:T(8,128)}, f32[2,256,384]{2,1,0:T(8,128)}, f32[2,256,384]{2,1,0:T(8,128)}) custom-call(bf16[2,272,768]{2,1,0:T(8,128)(2,1)} %get-tuple-element.85.normed_ref, bf16[768,384]{1,0:T(8,128)(2,1)} %gate_proj_ref.3, f32[2,256,384]{2,1,0:T(8,128)} %get-tuple-element.86.values_ref, ...), custom_call_target="tpu_custom_call" | custom-call | flops 100000000 | bytes 1230854 | tf_op jit(solution)/shard_map/pallas_call | solution.py:188
  48.9 3.5 %all-to-all-done.1 = f32[8,32,384]{2,1,0:T(8,128)S(1)} async-done(((f32[8,32,384]{2,1,0:T(8,128)}), f32[8,32,384]{2,1,0:T(8,128)S(1)}, u32[]{:S(2)}, u32[]{:S(2)}) %all-to-all-start.1) | async-done | bytes 393248 | tf_op jit(solution)/shard_map/all_to_all | solution.py:909
  53.2 3.6 %shard_map.282 = (f32[2,256,384]{2,1,0:T(8,128)}, f32[8,512]{1,0:T(8,128)}) custom-call(f32[2,128,384]{2,1,0:T(8,128)} %bitcast.39, f32[2,256,256]{2,1,0:T(8,128)} %get-tuple-element.83.states_ref, f32[2,256,384]{2,1,0:T(8,128)} %get-tuple-element.84.exp_cum_x_ref, f32[2,256,384]{2,1,0:T(8,128)} %get-tuple-element.91.base_ref, ...), custom_call_target="tpu_custom_call" | custom-call | flops 100000000 | bytes 1016192 | tf_op jit(solution)/shard_map/pallas_call | solution.py:188
  60.4 2.2 %collective-permute-done.2 = f32[8,512]{1,0:T(8,128)S(1)} collective-permute-done((f32[8,512]{1,0:T(8,128)S(1)}, f32[8,512]{1,0:T(8,128)S(1)}, u32[]{:S(2)}, u32[]{:S(2)}) %collective-permute-start.2) | collective-permute-done | bytes 16416 | tf_op jit(solution)/shard_map/ppermute | solution.py:28
  63.3 3.7 %shard_map.283 = (f32[2,256,384]{2,1,0:T(8,128)}, f32[8,32,384]{2,1,0:T(8,128)}) custom-call(f32[8,512]{1,0:T(8,128)} %add.109.sums_ref, f32[2,256,384]{2,1,0:T(8,128)} %get-tuple-element.95.read_ref, f32[2,256,384]{2,1,0:T(8,128)} %get-tuple-element.91.base_ref, f32[2,256,384]{2,1,0:T(8,128)} %get-tuple-element.92.gate_pre_ref, ...), custom_call_target="tpu_custom_call" | custom-call | flops 100000000 | bytes 1118592 | tf_op jit(solution)/shard_map/pallas_call | solution.py:188
  67.0 3.7 %all-to-all-start.2 = ((f32[8,32,384]{2,1,0:T(8,128)}), f32[8,32,384]{2,1,0:T(8,128)S(1)}, u32[]{:S(2)}, u32[]{:S(2)}) async-start(f32[8,32,384]{2,1,0:T(8,128)} %get-tuple-element.99), calls=%async_computation.2 | async-start | bytes 786432 | tf_op jit(solution)/shard_map/all_to_all | solution.py:940
  71.3 7.1 %shard_map.284 = (bf16[2,256,384]{2,1,0:T(8,128)(2,1)}, f32[1,768]{1,0:T(1,128)}, bf16[4,192,384]{2,1,0:T(8,128)(2,1)}, bf16[4,192,384]{2,1,0:T(8,128)(2,1)}, bf...) custom-call(s32[2]{0:T(128)} %pad_add_fusion.own_ref, f32[8,512]{1,0:T(8,128)} %add.109.sums_ref, ...), custom_call_target="tpu_custom_call" | custom-call | flops 100000000 | bytes 1737090 | tf_op jit(solution)/shard_map/pallas_call | solution.py:188
  78.4 3.1 %all-to-all-done.2.back_ref = f32[8,32,384]{2,1,0:T(8,128)S(1)} async-done(((f32[8,32,384]{2,1,0:T(8,128)}), f32[8,32,384]{2,1,0:T(8,128)S(1)}, u32[]{:S(2)}, u32[]{:S(2)}) %all-to-all-start.2) | async-done | bytes 393248 | tf_op jit(solution)/shard_map/all_to_all | solution.py:940
  84.2 3.7 %all-to-all-start.3 = ((f32[8,32,384]{2,1,0:T(8,128)}), f32[8,32,384]{2,1,0:T(8,128)S(1)}, u32[]{:S(2)}, u32[]{:S(2)}) async-start(f32[8,32,384]{2,1,0:T(8,128)} %shard_map.285), calls=%async_computation.3 | async-start | bytes 786432 | tf_op jit(solution)/shard_map/all_to_all | solution.py:983
  89.9 7.9 %shard_map.286 = (f32[2,256,384]{2,1,0:T(8,128)}, f32[2,256,128]{2,1,0:T(8,128)}, f32[2,256,128]{2,1,0:T(8,128)}, f32[2,6,256]{2,1,0:T(8,128)}) custom-call(f32[2,256,384]{2,1,0:T(8,128)} %get-tuple-element.86.values_ref, f32[2,256,256]{2,1,0:T(8,128)} %get-tuple-element.83.states_ref, f32[2,256,384]{2,1,0:T(8,128)} %get-tuple-element.87.step_x_ref, ...), custom_call_target="tpu_custom_call" | custom-call | flops 100000000 | bytes 1021952 | tf_op jit(solution)/shard_map/pallas_call | solution.py:188
  99.7 3.5 %shard_map.288 = (f32[2,512,64]{2,1,0:T(8,128)}, f32[2,512,64]{2,1,0:T(8,128)}) custom-call(s32[2]{0:T(128)} %pad_add_fusion.own_ref, f32[2,128,384]{2,1,0:T(8,128)} %bitcast.42, f32[2,256,384]{2,1,0:T(8,128)} %get-tuple-element.86.values_ref, f32[2,256,384]{2,1,0:T(8,128)} %get-tuple-element.87.step_x_ref, f32[2,256,384]{2,1,0:T(8,128)} %get-tuple-element.104.end_x_ref, ...), custom_call_target="tpu_custom_call" | custom-call | flops 100000000 | bytes 819202 | tf_op jit(solution)/shard_map/pallas_call | solution.py:188
  109.9 5.8 %shard_map.287 = (f32[2,272,384]{2,1,0:T(8,128)}, bf16[2,6,256]{2,1,0:T(8,128)(2,1)}, f32[5,384]{1,0:T(8,128)}, f32[6,128]{1,0:T(8,128)}) custom-call(f32[2,128,384]{2,1,0:T(8,128)} %bitcast.43, f32[2,128,384]{2,1,0:T(8,128)} %bitcast.41, f32[2,256,384]{2,1,0:T(8,128)} %get-tuple-element.86.values_ref, f32[2,256,256]{2,1,0:T(8,128)} %get-tuple-element.83.states_ref, ...), custom_call_target="tpu_custom_call" | custom-call | flops 100000000 | bytes 2117132 | tf_op jit(solution)/shard_map/pallas_call | solution.py:188
  116.5 3.7 %shard_map.289 = (f32[2,272,64]{2,1,0:T(8,128)}, f32[5,64]{1,0:T(8,128)}, f32[6,768]{1,0:T(8,128)}, bf16[8,112,384]{2,1,0:T(8,128)(2,1)}) custom-call(bf16[2,272,768]{2,1,0:T(8,128)(2,1)} %get-tuple-element.85.normed_ref, f32[2,272,384]{2,1,0:T(8,128)} %get-tuple-element.109.value_in_ref, bf16[2,6,256]{2,1,0:T(8,128)(2,1)} %get-tuple-element.110.grad_step_t_ref, ...), custom_call_target="tpu_custom_call" | custom-call | flops 100000000 | bytes 519936 | tf_op jit(solution)/shard_map/pallas_call | solution.py:188
  120.2 4.7 %all-to-all-start.4 = ((bf16[8,112,384]{2,1,0:T(8,128)(2,1)}), bf16[8,112,384]{2,1,0:T(8,128)(2,1)S(1)}, u32[]{:S(2)}, u32[]{:S(2)}) async-start(bf16[8,112,384]{2,1,0:T(8,128)(2,1)} %get-tuple-element.121), calls=%async_computation.4 | async-start | bytes 1376256 | tf_op jit(solution)/shard_map/all_to_all | solution.py:1053
  127.2 16.3 %collective-permute-done.9 = bf16[2,192,384]{2,1,0:T(8,128)(2,1)S(1)} collective-permute-done((bf16[2,192,384]{2,1,0:T(8,128)(2,1)}, bf16[2,192,384]{2,1,0:T(8,128)(2,1)S(1)}, u32[]{:S(2)}, u32[]{:S(2)}) %collective-permute-start.9) | collective-permute-done | bytes 294944 | tf_op jit(solution)/shard_map/ppermute | solution.py:28
  143.5 2.5 %collective-permute-start.10 = (bf16[1,192,384]{2,1,0:T(8,128)(2,1)S(1)}, bf16[1,192,384]{2,1,0:T(8,128)(2,1)S(1)}, u32[]{:S(2)}, u32[]{:S(2)}) collective-permute-start(bf16[1,192,384]{2,1,0:T(8,128)(2,1)S(1)} %add_convert_fusion.9), channel_id=1, source_target_pairs={{0,16},{4,20},{8,24},{12,28},{16,0},{20,4},{24,8},{28,12},{1,17},{... | collective-permute-start | bytes 442376 | tf_op jit(solution)/shard_map/ppermute | solution.py:28
  148.9 2.1 collective-permute-done.10
  154.7 6.5 %collective-permute-done.11 = bf16[1,192,384]{2,1,0:T(8,128)(2,1)S(1)} collective-permute-done((bf16[1,192,384]{2,1,0:T(8,128)(2,1)S(1)}, bf16[1,192,384]{2,1,0:T(8,128)(2,1)S(1)}, u32[]{:S(2)}, u32[]{:S(2)}) %collective-permute-start.11) | collective-permute-done | bytes 147488 | tf_op jit(solution)/shard_map/ppermute | solution.py:28
  164.0 3.9 %all-to-all-start.5 = ((bf16[8,96,384]{2,1,0:T(8,128)(2,1)}), bf16[8,96,384]{2,1,0:T(8,128)(2,1)S(1)}, u32[]{:S(2)}, u32[]{:S(2)}) async-start(bf16[8,96,384]{2,1,0:T(8,128)(2,1)} %get-tuple-element.127), calls=%async_computation.5 | async-start | bytes 1179648 | tf_op jit(solution)/shard_map/all_to_all | solution.py:1064
  169.7 6.4 %shard_map.291 = (bf16[2,512,192]{2,1,0:T(8,128)(2,1)}, bf16[2,512,192]{2,1,0:T(8,128)(2,1)}, f32[8,512]{1,0:T(8,128)}, f32[1,768]{1,0:T(1,128)}) custom-call(s32[2]{0:T(128)} %pad_add_fusion.own_ref, bf16[2,256,768]{2,1,0:T(8,128)(2,1)} %tokens_ref.3, f32[768]{0:T(1024)} %gain_ref.3, f32[2,272,384]{2,1,0:T(8,128)} %get-tuple-element.109.value_in_ref, ...), custom_call_target="tpu_custom_call" | custom-call | flops 100000000 | bytes 877058 | tf_op jit(solution)/shard_map/pallas_call | solution.py:188
  182.7 2.5 %collective-permute-start.25 = (bf16[1,4,16,384]{3,2,1,0:T(8,128)(2,1)S(1)}, bf16[1,4,16,384]{3,2,1,0:T(8,128)(2,1)S(1)}, u32[]{:S(2)}, u32[]{:S(2)}) collective-permute-start(bf16[1,4,16,384]{3,2,1,0:T(8,128)(2,1)S(1)} %maximum_bitcast_fusion), channel_id=1, source_target_pairs={{0,16},{4,20},{8,24},{12,28},{16,0},{20,4},{24,8},{28,12},{1,17},{... | collective-permute-start | bytes 147464 | tf_op jit(solution)/shard_map/ppermute | solution.py:28
  185.8 4.8 %collective-permute-done.17 = f32[14,768]{1,0:T(8,128)S(1)} collective-permute-done((f32[14,768]{1,0:T(8,128)S(1)}, f32[14,768]{1,0:T(8,128)S(1)}, u32[]{:S(2)}, u32[]{:S(2)}) %collective-permute-start.17) | collective-permute-done | bytes 43040 | tf_op jit(solution)/shard_map/ppermute | solution.py:28
  194.0 2.0 collective-permute-done.18
  208.1 2.2 shard_map.293
  214.8 4.1 %collective-permute-done.22.far_ref = bf16[4,192,384]{2,1,0:T(8,128)(2,1)S(1)} collective-permute-done((bf16[4,192,384]{2,1,0:T(8,128)(2,1)S(1)}, bf16[4,192,384]{2,1,0:T(8,128)(2,1)S(1)}, u32[]{:S(2)}, u32[]{:S(2)}) %collective-permute-start.22) | collective-permute-done | bytes 589856 | tf_op jit(solution)/shard_map/ppermute | solution.py:28
  219.7 2.8 %shard_map.292 = (f32[8,96,384]{2,1,0:T(8,128)}, f32[8,48,768]{2,1,0:T(8,128)}) custom-call(s32[2]{0:T(128)} %pad_add_fusion.own_ref, bf16[4,192,384]{2,1,0:T(8,128)(2,1)} %copy-done.6, bf16[4,192,384]{2,1,0:T(8,128)(2,1)} %copy-done.10), custom_call_target="tpu_custom_call" | custom-call | flops 100000000 | bytes 294914 | tf_op jit(solution)/shard_map/pallas_call | solution.py:188
  (179 shorter events, 69.1 us)
Async XLA Ops:
  1.5 6.6 %collective-permute-start = (bf16[2,16,768]{2,1,0:T(8,128)(2,1)S(1)}, bf16[2,16,768]{2,1,0:T(8,128)(2,1)S(1)}, u32[]{:S(2)}, u32[]{:S(2)}) collective-permute-start(bf16[2,16,768]{2,1,0:T(8,128)(2,1)S(1)} %slice.125), channel_id=1, source_target_pairs={{0,4},{4,8},{8,12},{12,16},{16,20},{20,24},{24,28},{1,5},{5,9},{9,... | collective-permute-start | bytes 147464 | tf_op jit(solution)/shard_map/ppermute | solution.py:23
  15.9 19.3 %all-to-all-start = ((f32[8,40,384]{2,1,0:T(8,128)}), f32[8,40,384]{2,1,0:T(8,128)S(1)}, u32[]{:S(2)}, u32[]{:S(2)}) async-start(f32[8,40,384]{2,1,0:T(8,128)} %get-tuple-element.80), calls=%async_computation | async-start | bytes 983040 | tf_op jit(solution)/shard_map/all_to_all | solution.py:903
  37.8 14.7 %all-to-all-start.1 = ((f32[8,32,384]{2,1,0:T(8,128)}), f32[8,32,384]{2,1,0:T(8,128)S(1)}, u32[]{:S(2)}, u32[]{:S(2)}) async-start(f32[8,32,384]{2,1,0:T(8,128)} %shard_map.280), calls=%async_computation.1 | async-start | bytes 786432 | tf_op jit(solution)/shard_map/all_to_all | solution.py:909
  58.9 3.7 %collective-permute-start.2 = (f32[8,512]{1,0:T(8,128)S(1)}, f32[8,512]{1,0:T(8,128)S(1)}, u32[]{:S(2)}, u32[]{:S(2)}) collective-permute-start(f32[8,512]{1,0:T(8,128)S(1)} %add.108), channel_id=1, source_target_pairs={{0,2},{1,3},{2,0},{3,1},{4,6},{5,7},{6,4},{7,5},{8,10},{9,11},{10,... | collective-permute-start | bytes 49160 | tf_op jit(solution)/shard_map/ppermute | solution.py:28
  67.0 14.6 %all-to-all-start.2 = ((f32[8,32,384]{2,1,0:T(8,128)}), f32[8,32,384]{2,1,0:T(8,128)S(1)}, u32[]{:S(2)}, u32[]{:S(2)}) async-start(f32[8,32,384]{2,1,0:T(8,128)} %get-tuple-element.99), calls=%async_computation.2 | async-start | bytes 786432 | tf_op jit(solution)/shard_map/all_to_all | solution.py:940
  84.2 14.8 %all-to-all-start.3 = ((f32[8,32,384]{2,1,0:T(8,128)}), f32[8,32,384]{2,1,0:T(8,128)S(1)}, u32[]{:S(2)}, u32[]{:S(2)}) async-start(f32[8,32,384]{2,1,0:T(8,128)} %shard_map.285), calls=%async_computation.3 | async-start | bytes 786432 | tf_op jit(solution)/shard_map/all_to_all | solution.py:983
  87.9 18.6 %collective-permute-start.7 = (bf16[4,192,384]{2,1,0:T(8,128)(2,1)}, bf16[4,192,384]{2,1,0:T(8,128)(2,1)S(1)}, u32[]{:S(2)}, u32[]{:S(2)}) collective-permute-start(bf16[4,192,384]{2,1,0:T(8,128)(2,1)} %get-tuple-element.100), channel_id=1, source_target_pairs={{0,4},{4,0},{8,12},{12,8},{16,20},{20,16},{24,28},{28,24},{1,5},{5... | collective-permute-start | bytes 1769480 | tf_op jit(solution)/shard_map/ppermute | solution.py:28
  103.3 3.2 %collective-permute-start.5 = (f32[2,512,64]{2,1,0:T(8,128)}, f32[2,512,64]{2,1,0:T(8,128)S(1)}, u32[]{:S(2)}, u32[]{:S(2)}) collective-permute-start(f32[2,512,64]{2,1,0:T(8,128)} %get-tuple-element.114), channel_id=1, source_target_pairs={{0,1},{1,0},{2,3},{3,2},{4,5},{5,4},{6,7},{7,6},{8,9},{9,8},{10,11... | collective-permute-start | bytes 786440 | tf_op jit(solution)/shard_map/ppermute | solution.py:28
  105.7 21.5 %collective-permute-start.3 = (bf16[2,512,192]{2,1,0:T(8,128)(2,1)}, bf16[2,512,192]{2,1,0:T(8,128)(2,1)S(1)}, u32[]{:S(2)}, u32[]{:S(2)}) collective-permute-start(bf16[2,512,192]{2,1,0:T(8,128)(2,1)} %get-tuple-element.98), channel_id=1, source_target_pairs={{0,1},{1,0},{2,3},{3,2},{4,5},{5,4},{6,7},{7,6},{8,9},{9,8},{10,11... | collective-permute-start | bytes 1179656 | tf_op jit(solution)/shard_map/ppermute | solution.py:28
  107.5 8.3 %collective-permute-start.6 = (f32[1,512,64]{2,1,0:T(8,128)S(1)}, f32[1,512,64]{2,1,0:T(8,128)S(1)}, u32[]{:S(2)}, u32[]{:S(2)}) collective-permute-start(f32[1,512,64]{2,1,0:T(8,128)S(1)} %slice_add_fusion), channel_id=1, source_target_pairs={{0,2},{1,3},{2,0},{3,1},{4,6},{5,7},{6,4},{7,5},{8,10},{9,11},{10,... | collective-permute-start | bytes 393224 | tf_op jit(solution)/shard_map/ppermute | solution.py:28
  120.2 41.0 %all-to-all-start.4 = ((bf16[8,112,384]{2,1,0:T(8,128)(2,1)}), bf16[8,112,384]{2,1,0:T(8,128)(2,1)S(1)}, u32[]{:S(2)}, u32[]{:S(2)}) async-start(bf16[8,112,384]{2,1,0:T(8,128)(2,1)} %get-tuple-element.121), calls=%async_computation.4 | async-start | bytes 1376256 | tf_op jit(solution)/shard_map/all_to_all | solution.py:1053
  124.9 18.6 %collective-permute-start.9 = (bf16[2,192,384]{2,1,0:T(8,128)(2,1)}, bf16[2,192,384]{2,1,0:T(8,128)(2,1)S(1)}, u32[]{:S(2)}, u32[]{:S(2)}) collective-permute-start(bf16[2,192,384]{2,1,0:T(8,128)(2,1)} %get-tuple-element.123), channel_id=1, source_target_pairs={{0,8},{4,12},{8,0},{12,4},{16,24},{20,28},{24,16},{28,20},{1,9},{5... | collective-permute-start | bytes 884744 | tf_op jit(solution)/shard_map/ppermute | solution.py:28
  143.5 7.6 %collective-permute-start.10 = (bf16[1,192,384]{2,1,0:T(8,128)(2,1)S(1)}, bf16[1,192,384]{2,1,0:T(8,128)(2,1)S(1)}, u32[]{:S(2)}, u32[]{:S(2)}) collective-permute-start(bf16[1,192,384]{2,1,0:T(8,128)(2,1)S(1)} %add_convert_fusion.9), channel_id=1, source_target_pairs={{0,16},{4,20},{8,24},{12,28},{16,0},{20,4},{24,8},{28,12},{1,17},{... | collective-permute-start | bytes 442376 | tf_op jit(solution)/shard_map/ppermute | solution.py:28
  146.8 7.6 %collective-permute-start.4 = (bf16[1,512,192]{2,1,0:T(8,128)(2,1)}, bf16[1,512,192]{2,1,0:T(8,128)(2,1)S(1)}, u32[]{:S(2)}, u32[]{:S(2)}) collective-permute-start(bf16[1,512,192]{2,1,0:T(8,128)(2,1)} %add_convert_fusion.6), channel_id=1, source_target_pairs={{0,2},{1,3},{2,0},{3,1},{4,6},{5,7},{6,4},{7,5},{8,10},{9,11},{10,... | collective-permute-start | bytes 589832 | tf_op jit(solution)/shard_map/ppermute | solution.py:28
  151.1 10.1 %collective-permute-start.11 = (bf16[1,192,384]{2,1,0:T(8,128)(2,1)S(1)}, bf16[1,192,384]{2,1,0:T(8,128)(2,1)S(1)}, u32[]{:S(2)}, u32[]{:S(2)}) collective-permute-start(bf16[1,192,384]{2,1,0:T(8,128)(2,1)S(1)} %add_convert_fusion.8), channel_id=1, source_target_pairs={{0,16},{4,20},{8,24},{12,28},{16,0},{20,4},{24,8},{28,12},{1,17},{... | collective-permute-start | bytes 442376 | tf_op jit(solution)/shard_map/ppermute | solution.py:28
  152.3 15.7 %collective-permute-start.8 = (f32[2,16,448]{2,1,0:T(8,128)S(1)}, f32[2,16,448]{2,1,0:T(8,128)S(1)}, u32[]{:S(2)}, u32[]{:S(2)}) collective-permute-start(f32[2,16,448]{2,1,0:T(8,128)S(1)} %pad_maximum_fusion.3), channel_id=1, source_target_pairs={{4,0},{8,4},{12,8},{16,12},{20,16},{24,20},{28,24},{5,1},{9,5},{13... | collective-permute-start | bytes 172040 | tf_op jit(solution)/shard_map/ppermute | solution.py:23
  164.0 58.5 %all-to-all-start.5 = ((bf16[8,96,384]{2,1,0:T(8,128)(2,1)}), bf16[8,96,384]{2,1,0:T(8,128)(2,1)S(1)}, u32[]{:S(2)}, u32[]{:S(2)}) async-start(bf16[8,96,384]{2,1,0:T(8,128)(2,1)} %get-tuple-element.127), calls=%async_computation.5 | async-start | bytes 1179648 | tf_op jit(solution)/shard_map/all_to_all | solution.py:1064
  169.2 11.1 %collective-permute-start.23 = (bf16[1,16,384]{2,1,0:T(8,128)(2,1)S(1)}, bf16[1,16,384]{2,1,0:T(8,128)(2,1)S(1)}, u32[]{:S(2)}, u32[]{:S(2)}) collective-permute-start(bf16[1,16,384]{2,1,0:T(8,128)(2,1)S(1)} %bitcast.46), channel_id=1, source_target_pairs={{0,2},{1,3},{2,0},{3,1},{4,6},{5,7},{6,4},{7,5},{8,10},{9,11},{10,... | collective-permute-start | bytes 36872 | tf_op jit(solution)/shard_map/ppermute | solution.py:28
  176.0 4.9 %collective-permute-start.14 = (f32[8,512]{1,0:T(8,128)}, f32[8,512]{1,0:T(8,128)S(1)}, u32[]{:S(2)}, u32[]{:S(2)}) collective-permute-start(f32[8,512]{1,0:T(8,128)} %get-tuple-element.132), channel_id=1, source_target_pairs={{0,1},{1,0},{2,3},{3,2},{4,5},{5,4},{6,7},{7,6},{8,9},{9,8},{10,11... | collective-permute-start | bytes 49160 | tf_op jit(solution)/shard_map/ppermute | solution.py:28
  176.9 8.3 %collective-permute-start.16 = (f32[14,768]{1,0:T(8,128)S(1)}, f32[14,768]{1,0:T(8,128)S(1)}, u32[]{:S(2)}, u32[]{:S(2)}) collective-permute-start(f32[14,768]{1,0:T(8,128)S(1)} %fusion.11), channel_id=1, source_target_pairs={{0,4},{4,0},{8,12},{12,8},{16,20},{20,16},{24,28},{28,24},{1,5},{5... | collective-permute-start | bytes 129032 | tf_op jit(solution)/shard_map/ppermute | solution.py:28
  178.8 22.0 %collective-permute-start.21 = (bf16[2,192,384]{2,1,0:T(8,128)(2,1)S(1)}, bf16[2,192,384]{2,1,0:T(8,128)(2,1)S(1)}, u32[]{:S(2)}, u32[]{:S(2)}) collective-permute-start(bf16[2,192,384]{2,1,0:T(8,128)(2,1)S(1)} %pad_maximum_fusion), channel_id=1, source_target_pairs={{0,8},{4,12},{8,0},{12,4},{16,24},{20,28},{24,16},{28,20},{1,9},{5... | collective-permute-start | bytes 884744 | tf_op jit(solution)/shard_map/ppermute | solution.py:28
  180.3 2.4 %collective-permute-start.24 = (bf16[2,16,384]{2,1,0:T(8,128)(2,1)S(1)}, bf16[2,16,384]{2,1,0:T(8,128)(2,1)S(1)}, u32[]{:S(2)}, u32[]{:S(2)}) collective-permute-start(bf16[2,16,384]{2,1,0:T(8,128)(2,1)S(1)} %pad_maximum_fusion.4), channel_id=1, source_target_pairs={{0,1},{1,0},{2,3},{3,2},{4,5},{5,4},{6,7},{7,6},{8,9},{9,8},{10,11... | collective-permute-start | bytes 73736 | tf_op jit(solution)/shard_map/ppermute | solution.py:28
  180.4 21.3 %collective-permute-start.12 = (bf16[2,512,192]{2,1,0:T(8,128)(2,1)S(1)}, bf16[2,512,192]{2,1,0:T(8,128)(2,1)S(1)}, u32[]{:S(2)}, u32[]{:S(2)}) collective-permute-start(bf16[2,512,192]{2,1,0:T(8,128)(2,1)S(1)} %copy-done.33), channel_id=1, source_target_pairs={{0,1},{1,0},{2,3},{3,2},{4,5},{5,4},{6,7},{7,6},{8,9},{9,8},{10,11... | collective-permute-start | bytes 1179656 | tf_op jit(solution)/shard_map/ppermute | solution.py:28
  181.0 4.8 %collective-permute-start.15 = (f32[8,512]{1,0:T(8,128)S(1)}, f32[8,512]{1,0:T(8,128)S(1)}, u32[]{:S(2)}, u32[]{:S(2)}) collective-permute-start(f32[8,512]{1,0:T(8,128)S(1)} %add.129), channel_id=1, source_target_pairs={{0,2},{1,3},{2,0},{3,1},{4,6},{5,7},{6,4},{7,5},{8,10},{9,11},{10,... | collective-permute-start | bytes 49160 | tf_op jit(solution)/shard_map/ppermute | solution.py:28
  182.7 9.7 %collective-permute-start.25 = (bf16[1,4,16,384]{3,2,1,0:T(8,128)(2,1)S(1)}, bf16[1,4,16,384]{3,2,1,0:T(8,128)(2,1)S(1)}, u32[]{:S(2)}, u32[]{:S(2)}) collective-permute-start(bf16[1,4,16,384]{3,2,1,0:T(8,128)(2,1)S(1)} %maximum_bitcast_fusion), channel_id=1, source_target_pairs={{0,16},{4,20},{8,24},{12,28},{16,0},{20,4},{24,8},{28,12},{1,17},{... | collective-permute-start | bytes 147464 | tf_op jit(solution)/shard_map/ppermute | solution.py:28
  185.2 5.5 %collective-permute-start.17 = (f32[14,768]{1,0:T(8,128)S(1)}, f32[14,768]{1,0:T(8,128)S(1)}, u32[]{:S(2)}, u32[]{:S(2)}) collective-permute-start(f32[14,768]{1,0:T(8,128)S(1)} %fusion.17), channel_id=1, source_target_pairs={{0,8},{4,12},{8,0},{12,4},{16,24},{20,28},{24,16},{28,20},{1,9},{5... | collective-permute-start | bytes 129032 | tf_op jit(solution)/shard_map/ppermute | solution.py:28
  190.7 5.4 %collective-permute-start.18 = (f32[14,768]{1,0:T(8,128)S(1)}, f32[14,768]{1,0:T(8,128)S(1)}, u32[]{:S(2)}, u32[]{:S(2)}) collective-permute-start(f32[14,768]{1,0:T(8,128)S(1)} %add.133), channel_id=1, source_target_pairs={{0,16},{4,20},{8,24},{12,28},{16,0},{20,4},{24,8},{28,12},{1,17},{... | collective-permute-start | bytes 129032 | tf_op jit(solution)/shard_map/ppermute | solution.py:28
  192.5 7.0 %collective-permute-start.26 = (bf16[2,4,16,384]{3,2,1,0:T(8,128)(2,1)S(1)}, bf16[2,4,16,384]{3,2,1,0:T(8,128)(2,1)S(1)}, u32[]{:S(2)}, u32[]{:S(2)}) collective-permute-start(bf16[2,4,16,384]{3,2,1,0:T(8,128)(2,1)S(1)} %pad_maximum_fusion.2), channel_id=1, source_target_pairs={{0,8},{4,12},{8,0},{12,4},{16,24},{20,28},{24,16},{28,20},{1,9},{5... | collective-permute-start | bytes 294920 | tf_op jit(solution)/shard_map/ppermute | solution.py:28
  197.9 7.2 %collective-permute-start.20 = (f32[8,768]{1,0:T(8,128)S(1)}, f32[8,768]{1,0:T(8,128)S(1)}, u32[]{:S(2)}, u32[]{:S(2)}) collective-permute-start(f32[8,768]{1,0:T(8,128)S(1)} %slice_add_fusion.3), channel_id=1, source_target_pairs={{0,2},{1,3},{2,0},{3,1},{4,6},{5,7},{6,4},{7,5},{8,10},{9,11},{10,... | collective-permute-start | bytes 73736 | tf_op jit(solution)/shard_map/ppermute | solution.py:28
  199.5 7.9 %collective-permute-start.27 = (bf16[4,4,16,384]{3,2,1,0:T(8,128)(2,1)S(1)}, bf16[4,4,16,384]{3,2,1,0:T(8,128)(2,1)S(1)}, u32[]{:S(2)}, u32[]{:S(2)}) collective-permute-start(bf16[4,4,16,384]{3,2,1,0:T(8,128)(2,1)S(1)} %pad_maximum_fusion.1.near_ref), channel_id=1, source_target_pairs={{0,4},{4,0},{8,12},{12,8},{16,20},{20,16},{24,28},{28,24},{1,5},{5... | collective-permute-start | bytes 589832 | tf_op jit(solution)/shard_map/ppermute | solution.py:28
  200.9 18.0 %collective-permute-start.22 = (bf16[4,192,384]{2,1,0:T(8,128)(2,1)S(1)}, bf16[4,192,384]{2,1,0:T(8,128)(2,1)S(1)}, u32[]{:S(2)}, u32[]{:S(2)}) collective-permute-start(bf16[4,192,384]{2,1,0:T(8,128)(2,1)S(1)} %constant_dynamic-update-slice_fusion.near_ref), channel_id=1, source_target_pairs={{0,4},{4,0},{8,12},{12,8},{16,20},{20,16},{24,28},{28,24},{1,5},{5... | collective-permute-start | bytes 1769480 | tf_op jit(solution)/shard_map/ppermute | solution.py:28
  202.7 7.7 %collective-permute-start.13 = (bf16[1,512,192]{2,1,0:T(8,128)(2,1)}, bf16[1,512,192]{2,1,0:T(8,128)(2,1)S(1)}, u32[]{:S(2)}, u32[]{:S(2)}) collective-permute-start(bf16[1,512,192]{2,1,0:T(8,128)(2,1)} %add_convert_fusion.3), channel_id=1, source_target_pairs={{0,2},{1,3},{2,0},{3,1},{4,6},{5,7},{6,4},{7,5},{8,10},{9,11},{10,... | collective-permute-start | bytes 589832 | tf_op jit(solution)/shard_map/ppermute | solution.py:28
  (36 other events, 284.9 us)

commit v2 on v1

--- a/solution.py
+++ b/solution.py
@@ -77,6 +77,15 @@
         while self.order:
             self.step()
         return self.keep
+
+
+def send_direct(keep, send, axis, order):
+    half = keep.shape[0]
+    pieces = [keep[p] for p in range(half)] + [send[p] for p in range(half)]
+    return [
+        swap(piece, axis, mask) if mask else piece
+        for piece, mask in zip(pieces, places(order))
+    ]
 
 
 class Gather:
@@ -244,6 +253,7 @@
     step_x_ref,
     exp_cum_x_ref,
     end_x_ref,
+    weighted_ref,
     cum_ref,
     cum_t_ref,
     step_arg_t_ref,
@@ -306,7 +316,9 @@
         values_ref,
         value_slope_ref,
     )
-    ends = dot_fine(states_ref[0, :, :nstate], end_x * step_x * values_ref[0], TN)
+    weighted = end_x * step_x * values_ref[0]
+    weighted_ref[0] = weighted
+    ends = dot_fine(states_ref[0, :, :nstate], weighted, TN)
     for block in range(blocks):
         ends_ref[block, 0:8] = jnp.broadcast_to(exp_cum_x[length - 1 :], (8, inner))
         ends_ref[block, 8:] = ends[block * share : (block + 1) * share]
@@ -436,7 +448,7 @@
 
         @pl.when((own ^ mask) == at)
         def _():
-            (keep_ref if p < half else send_ref)[p % half] = value
+            (keep_ref if p < half else send_ref)[p % half, :, : value.shape[1]] = value
 
 
 def low_kernel(
@@ -452,8 +464,10 @@
     normed_ref,
     cot_ref,
     out_proj_ref,
+    proj_ref,
     grad_gate_ref,
     rows_ref,
+    gain_row_ref,
     keep_ref,
     send_ref,
     branch_keep_ref,
@@ -492,6 +506,8 @@
         )
     rows_ref[:, :inner] = gain_sum
     rows_ref[:, inner:] = skip_sum
+    ones = jnp.ones((8, inner), BF16)
+    gain_row_ref[...] = dot_right(ones, total * proj_ref[...].astype(F32), NT)
     cut_lines(grad_gate_proj, total)
     cut_lines(grad_out_proj, dot(gate_low[...], cot_ref[...], TN))
     blocks = 2 * keep_ref.shape[0]
@@ -567,17 +583,14 @@
 def state_sum_kernel(
     own_ref,
     grad_end_ref,
-    values_ref,
-    step_x_ref,
-    end_x_ref,
+    weighted_ref,
     grad_b_ref,
     grad_c_ref,
     keep_ref,
     send_ref,
 ):
     pieces, part = 2 * keep_ref.shape[0], keep_ref.shape[2]
-    weighted = end_x_ref[0] * step_x_ref[0] * values_ref[0]
-    grad_b = grad_b_ref[0] + dot_fine(weighted, grad_end_ref[0], NT)
+    grad_b = grad_b_ref[0] + dot_fine(weighted_ref[0], grad_end_ref[0], NT)
     both = jnp.concatenate([grad_b, grad_c_ref[0]], axis=1)
     for piece in range(pieces):
         value = both[:, piece * part : (piece + 1) * part]
@@ -679,7 +692,12 @@
     accumulate(head_rows_ref, jnp.where(lane == 0, bias_sum, rate_sum * rate_t))
 
 
+def small_places(heads, taps, lanes):
+    return lanes - LANES, heads + max(heads, taps)
+
+
 def weight_kernel(
+    own_ref,
     normed_ref,
     value_in_ref,
     grad_step_t_ref,
@@ -687,13 +705,34 @@
     slope_ref,
     conv_in_ref,
     conv_weight_ref,
+    gain_ref,
+    gate_gain_row_ref,
+    value_proj_ref,
+    state_proj_t_ref,
+    step_proj_t_ref,
+    value_rows_ref,
+    head_rows_ref,
+    inner_row_ref,
     state_in_ref,
-    conv_rows_ref,
-    step_rows_ref,
     late_ref,
     around,
+    small,
+    slope,
+    conv_in,
+    conv_weight,
+    *,
+    pieces,
 ):
-    seqs, length, _ = slope_ref.shape
+    seqs, length, part = slope.shape
+    for piece in range(pieces):
+
+        @pl.when(own_ref[1] == piece)
+        def _():
+            lanes = slice(piece * part, (piece + 1) * part)
+            slope[...] = slope_ref[:, :, lanes]
+            conv_in[...] = conv_in_ref[:, :, lanes]
+            conv_weight[...] = conv_weight_ref[:, lanes]
+
     width = normed_ref.shape[2]
     blocks, _, inner = late_ref.shape
     value_total = state_total = step_total = conv_total = None
@@ -704,33 +743,62 @@
     clear_edges(around)
     for seq in range(seqs):
         normed = normed_ref[seq]
-        grad = state_grad_ref[seq * length : (seq + 1) * length] * slope_ref[seq]
-        grad_in, conv_rows = conv_back(grad, conv_in_ref, conv_weight_ref, seq, around)
+        grad = state_grad_ref[seq * length : (seq + 1) * length] * slope[seq]
+        grad_in, conv_rows = conv_back(grad, conv_in, conv_weight, seq, around)
         state_in_ref[seq] = grad_in
         conv_total = add(conv_total, conv_rows)
         value_total = add(value_total, dot(normed, value_in_ref[seq].astype(BF16), TN))
         state_total = add(state_total, dot(grad_in.astype(BF16), normed, TN))
         step_total = add(step_total, dot(grad_step_t_ref[seq], normed_ref[seq, PAD:]))
-    conv_rows_ref[...] = conv_total
-    step_rows_ref[...] = step_total
+    ones = jnp.ones((8, inner), BF16)
+    gain_row = gate_gain_row_ref[...] + dot_right(
+        ones, value_total * value_proj_ref[...].astype(F32), NT
+    )
+    gain_row = (
+        gain_row[0:1]
+        + jnp.sum(state_total * state_proj_t_ref[...].astype(F32), axis=0, keepdims=True)
+        + jnp.sum(step_total * step_proj_t_ref[...].astype(F32), axis=0, keepdims=True)
+    )
+    heads, taps = step_total.shape[0], value_rows_ref.shape[0]
+    heads_at, last = small_places(heads, taps, small.shape[1])
+    small[...] = jnp.zeros(small.shape, F32)
+    small[:heads, :width] = step_total
+    small[heads : heads + taps, :inner] = value_rows_ref[...]
+    for piece in range(pieces):
+
+        @pl.when(own_ref[1] == piece)
+        def _():
+            first = inner + piece * part
+            small[heads : heads + taps, first : first + part] = conv_total
+
+    small[heads : 2 * heads, heads_at:] = head_rows_ref[...]
+    small[last : last + 1, : 2 * inner] = inner_row_ref[...]
+    small[last + 1 : last + 2, :width] = gain_row / as_row(gain_ref)
+    small_rows = jnp.concatenate(stacked(small[...], inner), axis=0)
+    small_lines = small_rows.shape[0] // blocks
     value_lines = width // blocks
     state_lines = state_total.shape[0] // blocks
     for block in range(blocks):
         value = value_total[block * value_lines : (block + 1) * value_lines]
         state = state_total[block * state_lines : (block + 1) * state_lines]
-        value = jnp.concatenate([value, *stacked(state, inner)], axis=0)
-        late_ref[block] = value.astype(BF16)
-
-
-def sum_kernel(got_ref, value_ref, state_ref):
+        lines = small_rows[block * small_lines : (block + 1) * small_lines]
+        value = [value, *stacked(state, inner), *[x.astype(F32) for x in parts(lines, 2)]]
+        spare = late_ref.shape[1] - sum(x.shape[0] for x in value)
+        if spare:
+            value.append(jnp.zeros((spare, inner), F32))
+        late_ref[block] = jnp.concatenate(value, axis=0).astype(BF16)
+
+
+def sum_kernel(got_ref, out_ref, *, first, lines):
     total = got_ref[0].astype(F32)
     for block in range(1, got_ref.shape[0]):
         total = total + got_ref[block].astype(F32)
-    total = total.astype(BF16)
-    lines = value_ref.shape[1]
-    for block in range(value_ref.shape[0]):
-        value_ref[block] = total[:lines]
-    state_ref[...] = total[lines:]
+    small = total[first : first + lines] + total[first + lines : first + 2 * lines]
+    small = [x.astype(F32) for x in parts(small, 2)]
+    spare = [total[first + 2 * lines :]] if total.shape[0] > first + 2 * lines else []
+    total = jnp.concatenate([total[:first], *small, *spare], axis=0).astype(BF16)
+    for block in range(out_ref.shape[0]):
+        out_ref[block] = total
 
 
 def place_kernel(own_ref, near_ref, far_ref, gate_ref, out_ref):
@@ -746,21 +814,6 @@
             out_ref[at, :, group * inner : (group + 1) * inner] = value[first : first + count]
 
 
-def place_state_kernel(own_ref, near_ref, far_ref, out_ref, held):
-    half, pieces, _, inner = near_ref.shape
-    _, each, width = held.shape
-    for p, mask in enumerate(places(orders(2 * half)[0])):
-        ref = near_ref if p < half else far_ref
-        for q, head_mask in enumerate(places(orders(pieces)[0])):
-            value = ref[p % half, q].astype(F32)
-            at = (own_ref[1] ^ head_mask) * 2 * half + (own_ref[0] ^ mask)
-            for group in range(width // inner):
-                held[at, :, group * inner : (group + 1) * inner] = value[
-                    group * each : (group + 1) * each
-                ]
-    out_ref[...] = jnp.transpose(held[...].reshape(-1, width))
-
-
 def back_kernel(
     own_ref,
     tokens_ref,
@@ -770,19 +823,18 @@
     value_over_ref,
     state_over_ref,
     value_proj_ref,
-    state_proj_ref,
+    state_proj_t_ref,
     grad_gate_ref,
     gate_proj_ref,
     grad_step_t_ref,
     step_proj_t_ref,
     keep_ref,
     send_ref,
-    sums_ref,
-    gain_sum_ref,
+    *,
+    col_width,
 ):
     _, length, width = tokens_ref.shape
-    pieces, col_width = 2 * keep_ref.shape[0], keep_ref.shape[2]
-    ones = jnp.ones((8, width), BF16)
+    pieces = 2 * keep_ref.shape[0]
     def whole(in_ref, over_ref, seq):
         return jnp.concatenate(
             [
@@ -796,16 +848,83 @@
     unit = x * lax.rsqrt(jnp.mean(x * x, axis=-1, keepdims=True) + EPS)
     normed_grad = (
         dot(whole(value_in_ref, value_over_ref, 0), value_proj_ref[...], NT)
-        + dot(whole(state_in_ref, state_over_ref, 0), state_proj_ref[...], NT)
+        + dot(whole(state_in_ref, state_over_ref, 0), state_proj_t_ref[...])
         + dot(grad_gate_ref[0], gate_proj_ref[...], NT)
         + dot(grad_step_t_ref[0], step_proj_t_ref[...], TN)
     )
-    accumulate(gain_sum_ref, jnp.sum(normed_grad * unit, axis=0, keepdims=True))
     unit_grad = normed_grad * as_row(gain_ref)
-    sums_ref[...] = dot_right(ones, unit_grad * unit, NT)
+    row_sum = jnp.sum(unit_grad * unit, axis=-1, keepdims=True).astype(BF16)
+    row_sum = jnp.broadcast_to(row_sum, (length, LANES))
+    for half_ref in (keep_ref, send_ref):
+        for p in range(pieces // 2):
+            half_ref[p, :, half_ref.shape[2] - LANES :] = row_sum
     for piece in range(pieces):
         value = unit_grad[:, piece * col_width : (piece + 1) * col_width].astype(BF16)
         ordered_piece(own_ref[1], piece, value, keep_ref, send_ref)
+
+
+def last_kernel(
+    own_ref,
+    near_ref,
+    far_ref,
+    state_proj_ref,
+    norm_gain_ref,
+    step_proj_ref,
+    conv_value_ref,
+    conv_value_bias_ref,
+    conv_state_ref,
+    conv_state_bias_ref,
+    step_bias_ref,
+    decay_log_ref,
+    skip_gain_ref,
+    out_gain_ref,
+    held,
+    smalls,
+):
+    half, blocks, _, inner = near_ref.shape
+    pieces, _, each, width = held.shape
+    _, lines, lanes = smalls.shape
+    state_lines = each * width // inner
+    small_lines = lines * lanes // inner // blocks
+    for p, mask in enumerate(places(orders(2 * half)[0])):
+        ref = near_ref if p < half else far_ref
+        at = own_ref[1] ^ mask
+        small = []
+        for block in range(blocks):
+            value = ref[p % half, block].astype(F32)
+            for group in range(width // inner):
+                held[at, block, :, group * inner : (group + 1) * inner] = value[
+                    group * each : (group + 1) * each
+                ]
+            high = value[state_lines : state_lines + small_lines]
+            small.append(high + value[state_lines + small_lines : state_lines + 2 * small_lines])
+        small = jnp.concatenate(small, axis=0)
+        smalls[at] = jnp.concatenate(
+            [small[first : first + lines] for first in range(0, small.shape[0], lines)], axis=1
+        )
+    state_proj_ref[...] = jnp.transpose(held[...].reshape(-1, width))
+    whole = smalls[0]
+    for piece in range(1, pieces):
+        whole = whole + smalls[piece]
+    small = smalls[own_ref[1]]
+    heads = step_proj_ref.shape[0]
+    taps = conv_value_ref.shape[0]
+    channels = inner + conv_state_ref.shape[1]
+    heads_at, last = small_places(heads, taps + 1, lanes)
+    norm_gain_ref[...] = whole[last + 1, :width]
+    step_proj_ref[...] = small[:heads, :width]
+    conv_value_ref[...] = small[heads : heads + taps, :inner]
+    conv_value_bias_ref[...] = small[heads + taps, :inner]
+    conv_state_ref[...] = whole[heads : heads + taps, inner:channels]
+    conv_state_bias_ref[...] = whole[heads + taps, inner:channels]
+    sums = small[heads : 2 * heads, heads_at : heads_at + 2]
+    eye = iota((heads, heads), 0) == iota((heads, heads), 1)
+    step_bias_ref[...] = jnp.sum(jnp.where(eye, sums[:, 0:1], 0.0), axis=0)
+    decay_log_ref[...] = jnp.sum(jnp.where(eye, sums[:, 1:2], 0.0), axis=0)
+    row = small[last : last + 1, : 2 * inner]
+    out_gain_ref[...] = row[0, :inner]
+    skip = dot_left(row[:, inner:], spread(heads, inner), NT, 3)
+    skip_gain_ref[...] = skip.reshape(heads)
 
 
 def on_device(
@@ -852,6 +971,8 @@
 
     edge_tokens = shift(tokens[:, length - PAD :, :], "seq", 1)
     step_proj_t = jnp.transpose(step_proj)
+    state_proj_t = jnp.transpose(state_proj)
+    state_proj_t = lax.dynamic_slice_in_dim(state_proj_t, head_index * part, part, 0)
     (
         normed,
         value_conv_in,
@@ -863,6 +984,7 @@
         step_x,
         exp_cum_x,
         end_x,
+        weighted,
         cum,
         cum_t,
         step_arg_t,
@@ -877,6 +999,7 @@
             ((seqs, length, 2 * nstate), F32, 0),
             (full, F32, 0),
             ((seqs, length, 2 * nstate), F32, 0),
+            (full, F32, 0),
             (full, F32, 0),
             (full, F32, 0),
             (full, F32, 0),
@@ -945,6 +1068,7 @@
     (
         grad_gate,
         inner_row,
+        gate_gain_row,
         early_keep,
         early_send,
         branch_keep,
@@ -954,6 +1078,7 @@
         [
             (full, BF16),
             ((1, 2 * inner), F32),
+            ((8, width), F32),
             *halves(blocks, 2 * (width // blocks), inner),
             *halves(head_devices, rows, col_width),
         ],
@@ -970,6 +1095,7 @@
             normed,
             cot_low,
             out_proj,
+            gate_proj,
         ],
         [
             pltpu.VMEM((rows, inner), BF16),
@@ -983,7 +1109,7 @@
     grad_end = lax.all_to_all(leaving, "seq", 0, 0).reshape(seqs, nstate, inner)
     near = orders(blocks)[0]
     near_head = orders(head_devices)[0]
-    early_chain = Reduce(early_keep, early_send, "seq", near)
+    even = places(near)[: blocks // 2]
     branch_chain = Reduce(branch_keep, branch_send, "head", near_head)
     grad_scan = lax.optimization_barrier((grad_scan, leaving))[0]
     scaled_grad, grad_b, grad_c, gaps = local(
@@ -997,14 +1123,20 @@
         cut(values, states, step_x, exp_cum_x, cum, cum_t, grad_scan, state_in),
         steps=seqs,
     )
-    early_chain.step(after=(gaps, grad_end))
+    early = lax.optimization_barrier((swap(early_send, "seq", 1), gaps))[0]
+    early = add_wide(early_keep, early)
+    grad_end, early = lax.optimization_barrier((grad_end, early))
+    early = [
+        swap(early[p], "seq", mask) if mask else early[p] for p, mask in enumerate(even)
+    ]
     state_keep, state_send = local(
         state_sum_kernel,
         halves(head_devices, rows, part, F32, 1),
-        [own, *cut(grad_end, values, step_x, end_x, grad_b, grad_c)],
+        [own, *cut(grad_end, weighted, grad_b, grad_c)],
         steps=seqs,
     )
-    state_part = Reduce(state_keep, state_send, "head", near_head).finish()
+    state_part = send_direct(state_keep, state_send, "head", near_head)
+    state_part = sum(state_part[1:], state_part[0])
     value_in, grad_step_t, value_rows, head_rows = local(
         value_kernel,
         [
@@ -1024,50 +1156,58 @@
         [pltpu.VMEM((length + 2 * PAD, inner), F32)],
         steps=seqs,
     )
-    state_part = hold(state_part, early_chain)
-    early_chain.step(after=(value_in,))
     value_lines = width // blocks
     state_lines = part // blocks * (width // inner)
-    state_grad_in, state_rows, step_rows, late = local(
-        weight_kernel,
+    small_lanes = max(width, channels + LANES)
+    small_rows = -(-(heads + max(heads, taps + 1) + 2) // 8) * 8
+    small_lines = small_rows * (small_lanes // inner) // blocks
+    late_lines = -(-(value_lines + state_lines + 2 * small_lines) // 16) * 16
+    state_grad_in, late = local(
+        functools.partial(weight_kernel, pieces=head_devices),
         [
             ((seqs, PAD + length, part), F32),
-            ((taps + 1, part), F32),
-            ((heads, width), F32),
-            ((blocks, value_lines + state_lines, inner), BF16),
-        ],
-        [
+            ((blocks, late_lines, inner), BF16),
+        ],
+        [
+            own,
             normed,
             value_in,
             grad_step_t,
             state_part,
-            own_cols(state_slope, part),
-            own_cols(state_conv_in, part),
-            own_cols(conv_state, part),
-        ],
-        [pltpu.VMEM((length + 2 * PAD, part), F32)],
-    )
-    early_chain.step(after=(late,))
-    early_chain = Gather(early_chain.finish(), "seq", near)
-    early_chain.step()
+            state_slope,
+            state_conv_in,
+            conv_state,
+            norm_gain,
+            gate_gain_row,
+            value_proj,
+            state_proj_t,
+            step_proj_t,
+            value_rows,
+            head_rows,
+            inner_row,
+        ],
+        [
+            pltpu.VMEM((length + 2 * PAD, part), F32),
+            pltpu.VMEM((small_rows, small_lanes), F32),
+            pltpu.VMEM((seqs, length, part), F32),
+            pltpu.VMEM((seqs, PAD + length, part), F32),
+            pltpu.VMEM((taps, part), F32),
+        ],
+    )
+    late, early = lax.optimization_barrier((late, early))
+    early = sum(x.astype(F32) for x in early).astype(BF16)
+    early = [swap(early, "seq", mask) if mask else early for mask in even]
     late = lax.all_to_all(late, "seq", 0, 0)
     over = jnp.concatenate([value_in[:, :PAD], state_grad_in[:, :PAD]], axis=2)
     over = shift(over, "seq", -1)
-    late = hold(late, early_chain)
-    early_chain.step()
-    late_values, late_states = local(
-        sum_kernel,
-        [((blocks, value_lines, inner), BF16), ((state_lines, inner), BF16)],
-        [late],
-    )
-    over = lax.optimization_barrier((over, late_values))[0]
-    grad_value_proj = lax.all_to_all(late_values, "seq", 0, 0)
-    keep, send, row_part, gain_sum = local(
-        back_kernel,
-        [
-            *halves(head_devices, rows, col_width, BF16, 1),
-            ((8, rows), F32, 1),
-            ((1, width), F32),
+    branch = branch_chain.finish().astype(F32)
+    own_source = own_cols(tokens.reshape(rows, width), col_width).astype(F32)
+    mixed_rows = jnp.swapaxes((own_source + branch).reshape(seqs, length, col_width), 1, 2)
+    back_width = -(-(col_width + 1) // LANES) * LANES
+    keep, send = local(
+        functools.partial(back_kernel, col_width=col_width),
+        [
+            *halves(head_devices, rows, back_width, BF16, 1),
         ],
         [
             own,
@@ -1075,7 +1215,7 @@
             norm_gain,
             *cut(value_in, state_grad_in, over[:, :, :inner], over[:, :, inner:]),
             value_proj,
-            own_cols(state_proj, part),
+            state_proj_t,
             (grad_gate, 0),
             gate_proj,
             (grad_step_t, 0),
@@ -1083,86 +1223,93 @@
         ],
         steps=seqs,
     )
-    back_chain = Reduce(keep, send, "head", near_head)
-    grad_value_proj = grad_value_proj.reshape(width, inner).astype(F32)
-    grad_gate_proj, grad_out_proj = local(
-        place_kernel,
-        [
-            ((blocks, value_lines, inner), F32),
-            ((blocks, inner // blocks, width), F32),
-        ],
-        [own, *early_chain.finish()],
-    )
-    grad_gate_proj = grad_gate_proj.reshape(width, inner)
-    grad_out_proj = grad_out_proj.reshape(inner, width)
-    state_chain = Gather(late_states, "head", near_head)
-    state_chain = Gather(jnp.concatenate(state_chain.finish(), axis=0), "seq", near)
-    (grad_state_proj,) = local(
-        place_state_kernel,
-        [((width, 2 * nstate), F32)],
-        [own, *state_chain.finish()],
-        [pltpu.VMEM((blocks * head_devices, part // blocks, width), F32)],
-    )
-    branch = branch_chain.finish().astype(F32)
-    own_source = own_cols(tokens.reshape(rows, width), col_width).astype(F32)
-    mixed_rows = (own_source + branch).reshape(seqs, length, col_width)
-    own_part = back_chain.finish().astype(F32)
-    row_mean = sum_all(row_part, "head")[0][:, None] / width
+    early = jnp.stack(early)
+    late, mixed_rows, early, keep, send = lax.optimization_barrier(
+        (late, mixed_rows, early, keep, send)
+    )
+    early_far = swap(early, "seq", 1)
+    (late_values,) = local(
+        functools.partial(
+            sum_kernel, first=value_lines + state_lines, lines=small_lines
+        ),
+        [((blocks, late_lines, inner), BF16)],
+        [late],
+    )
+    late = lax.all_to_all(late_values, "seq", 0, 0)
+    own_part = send_direct(keep, send, "head", near_head)
+    own_part = sum(x.astype(F32) for x in own_part)
+    row_mean = own_part[:, back_width - 1 :] / width
+    own_part = own_part[:, :col_width]
     source = tokens.reshape(rows, width).astype(F32)
     own_scale = lax.rsqrt(jnp.mean(source * source, axis=-1, keepdims=True) + EPS)
     own_unit = own_source * own_scale
     grad_tokens = cot_rows + own_scale * (own_part - own_unit * row_mean)
-    grad_tokens = grad_tokens.reshape(seqs, length, col_width)
-
-    def padded(x, lines, lanes):
-        return jnp.pad(x, ((0, lines - x.shape[0]), (0, lanes - x.shape[1])))
-
-    state_rows = lax.dynamic_update_slice(
-        jnp.zeros((taps + 1, 2 * nstate), F32), state_rows, (0, head_index * part)
-    )
-    lines = max(heads, taps + 1)
-    lanes = max(width, channels + LANES)
-    small = jnp.concatenate(
-        [
-            padded(step_rows, heads, lanes),
-            padded(
-                jnp.concatenate(
-                    [
-                        padded(value_rows, lines, inner),
-                        padded(state_rows, lines, 2 * nstate),
-                        padded(head_rows, lines, LANES),
-                    ],
-                    axis=1,
-                ),
-                lines,
-                lanes,
-            ),
-            padded(inner_row, 1, lanes),
-            padded(gain_sum, 1, lanes),
-        ],
-        axis=0,
-    )
-    small = sum_all(small, "seq")
-    whole = sum_all(small[heads:], "head")
-    conv_lines = small[heads : heads + lines]
-    grad_heads = conv_lines[:heads, channels : channels + 2]
-    grad_inner = small[heads + lines, : 2 * inner]
+    grad_tokens = jnp.swapaxes(grad_tokens.reshape(seqs, length, col_width), 1, 2)
+    late, grad_tokens = lax.optimization_barrier((late, grad_tokens))
+    grad_value_proj = late[:, :value_lines].reshape(width, inner).astype(F32)
+    grad_gate_proj, grad_out_proj = local(
+        place_kernel,
+        [
+            ((blocks, value_lines, inner), F32),
+            ((blocks, inner // blocks, width), F32),
+        ],
+        [own, early, early_far],
+    )
+    grad_gate_proj = grad_gate_proj.reshape(width, inner)
+    grad_out_proj = grad_out_proj.reshape(inner, width)
+    state_chain = Gather(late[:, value_lines:], "head", near_head)
+    state_chain.step()
+    done = (grad_gate_proj, grad_out_proj, mixed_rows, grad_tokens)
+    grad_gate_proj, grad_out_proj, mixed_rows, grad_tokens = hold(done, state_chain)
+    (
+        grad_state_proj,
+        grad_norm_gain,
+        grad_step_proj,
+        grad_conv_value,
+        grad_conv_value_bias,
+        grad_conv_state,
+        grad_conv_state_bias,
+        grad_step_bias,
+        grad_decay_log,
+        grad_skip_gain,
+        grad_out_gain,
+    ) = local(
+        last_kernel,
+        [
+            ((width, 2 * nstate), F32),
+            ((width,), F32),
+            ((heads, width), F32),
+            ((taps, inner), F32),
+            ((inner,), F32),
+            ((taps, 2 * nstate), F32),
+            ((2 * nstate,), F32),
+            ((heads,), F32),
+            ((heads,), F32),
+            ((heads,), F32),
+            ((inner,), F32),
+        ],
+        [own, *state_chain.finish()],
+        [
+            pltpu.VMEM((head_devices, blocks, part // blocks, width), F32),
+            pltpu.VMEM((head_devices, small_rows, small_lanes), F32),
+        ],
+    )
     return (
-        mixed_rows,
-        grad_tokens,
-        whole[lines + 1, :width],
+        jnp.swapaxes(mixed_rows, 1, 2),
+        jnp.swapaxes(grad_tokens, 1, 2),
+        grad_norm_gain,
         grad_gate_proj,
         grad_value_proj,
         grad_state_proj,
-        jnp.transpose(small[:heads, :width]),
-        conv_lines[:taps, :inner],
-        conv_lines[taps, :inner],
-        whole[:taps, inner:channels],
-        whole[taps, inner:channels],
-        grad_heads[:, 0],
-        grad_heads[:, 1],
-        jnp.sum(grad_inner[inner:].reshape(heads, head_dim), axis=1),
-        grad_inner[:inner],
+        jnp.transpose(grad_step_proj),
+        grad_conv_value,
+        grad_conv_value_bias,
+        grad_conv_state,
+        grad_conv_state_bias,
+        grad_step_bias,
+        grad_decay_log,
+        grad_skip_gain,
+        grad_out_gain,
         grad_out_proj,
     )
 

time: 225 us -> 205 us (0.911)
  waiting for transfers between devices: 54.2 us -> 44.6 us
  local copies, waits for them, and re-layouts: 21.5 us -> 17.5 us
  starting transfers between devices: 61.1 us -> 57.4 us
  other arithmetic: 11 us -> 8.41 us
    ppermute x26 -> x20, waiting for transfers between devices: 41 us -> 31.3 us  [swap(): return lax.ppermute(x, axis, [(i, i ^ mask) for i in range(devices)])]
    ppermute x26 -> x20, starting transfers between devices: 28.7 us -> 24 us  [swap(): return lax.ppermute(x, axis, [(i, i ^ mask) for i in range(devices)])]
    slice x7 -> x1, local copies, waits for them, and re-layouts: 3.67 us -> 0.06 us  [on_device(): grad_value_proj = late[:, :value_lines].reshape(width, inner).astype(F32)]
    dynamic_slice x4 -> x0, local copies, waits for them, and re-layouts: 3.15 us -> none  [own_cols(): return lax.dynamic_slice_in_dim(x, head_index * size, size, x.ndim - 1)]
    squeeze x0 -> x5, local copies, waits for them, and re-layouts: none -> 2.69 us  [the longest x4 1.9 us: send_direct(): pieces = [keep[p] for p in range(half)] + [send[p] for p in range(half)]]
    all_to_all x1, waiting for transfers between devices: 3.12 us -> 0.44 us  [on_device(): got_back = lax.all_to_all(back, 'seq', 0, 0)]
    convert_element_type x5 -> x2, other arithmetic: 2.58 us -> 0.21 us  [add_wide(): return (left.astype(F32) + right.astype(F32)).astype(left.dtype)]
    all_to_all x1, waiting for transfers between devices: 0.01 us -> 2.31 us  [on_device(): late = lax.all_to_all(late_values, 'seq', 0, 0)]
  transfers between devices with their start and end apart: 34 -> 28, of which waited for: 16 -> 15; matrix products, arithmetic and copies ran while one was open for 10% -> 8% of each run, Pallas kernels for 21% -> 22%
where the time goes in v2:
time: 205 us; the launch traced here: 204 us
  Pallas kernels  66.5 us (32%)
  starting transfers between devices  57.4 us (28%)
  waiting for transfers between devices  44.6 us (22%)
  local copies, waits for them, and re-layouts  17.5 us (9%)
  blocking collectives  8.6 us (4%)
  other arithmetic  8.41 us (4%)
    pallas_call x15, Pallas kernels, local(): pl.pallas_call(body, grid=(steps,), out_shape=[jax.ShapeDtypeStruct(shape...  66.5 us
    ppermute x20, waiting for transfers between devices, swap(): return lax.ppermute(x, axis, [(i, i ^ mask) for i in range(devices)])  31.3 us
    ppermute x20, starting transfers between devices, swap(): return lax.ppermute(x, axis, [(i, i ^ mask) for i in range(devices)])  24 us
    all_gather x1, blocking collectives, on_device(): cot_low = lax.all_gather(cot_low, 'head', axis=1, tiled=True)  8.6 us
    unnamed x44, local copies, waits for them, and re-layouts  7.88 us
    all_to_all x1, starting transfers between devices, on_device(): got = lax.all_to_all(ends, 'seq', 0, 0)  6.66 us
    ppermute x2, starting transfers between devices, shift(): return lax.ppermute(x, axis, pairs)  6.15 us
    all_to_all x1, starting transfers between devices, on_device(): late = lax.all_to_all(late, 'seq', 0, 0)  4.62 us
  transfers between devices with their start and end apart: 28, of which 15 were waited for; matrix products, arithmetic and copies ran while one was open for 8% of the time, Pallas kernels for 22%

profile of v2, /device:TPU:0, one launch (start us, length us, event | category | flops | bytes accessed | tf_op | source)
XLA Modules:
  0.0 204.1 jit_solution(7699984690800724958)
XLA Ops:
  1.5 4.9 %collective-permute-start = (bf16[2,16,768]{2,1,0:T(8,128)(2,1)S(1)}, bf16[2,16,768]{2,1,0:T(8,128)(2,1)S(1)}, u32[]{:S(2)}, u32[]{:S(2)}) collective-permute-start(bf16[2,16,768]{2,1,0:T(8,128)(2,1)S(1)} %slice.75), channel_id=1, source_target_pairs={{0,4},{4,8},{8,12},{12,16},{16,20},{20,24},{24,28},{1,5},{5,9},{9,... | collective-permute-start | bytes 147464 | tf_op jit(solution)/shard_map/ppermute | solution.py:23
  8.7 7.3 %shard_map.279 = (bf16[2,272,768]{2,1,0:T(8,128)(2,1)}, f32[2,272,384]{2,1,0:T(8,128)}, f32[2,272,256]{2,1,0:T(8,128)}, f32[2,256,384]{2,1,0:T(8,128)}, f32[2,25...) custom-call(bf16[2,256,768]{2,1,0:T(8,128)(2,1)} %tokens_ref.3, ...), custom_call_target="tpu_custom_call" | custom-call | flops 100000000 | bytes 460940 | tf_op jit(solution)/shard_map/pallas_call | solution.py:197
  16.0 6.7 %all-to-all-start = ((f32[8,40,384]{2,1,0:T(8,128)}), f32[8,40,384]{2,1,0:T(8,128)S(1)}, u32[]{:S(2)}, u32[]{:S(2)}) async-start(f32[8,40,384]{2,1,0:T(8,128)} %get-tuple-element.99), calls=%async_computation | async-start | bytes 983040 | tf_op jit(solution)/shard_map/all_to_all | solution.py:1026
  23.1 8.6 %all_gather.3 = bf16[512,768]{0,1:T(8,128)(2,1)S(1)} all-gather(bf16[512,192]{0,1:T(8,128)(2,1)S(1)} %copy.41), channel_id=1, replica_groups=mesh['seq'=8,'head'=4] {'head'}, dimensions={1}, use_global_device_ids=true | all-gather | bytes 983040 | tf_op jit(solution)/shard_map/all_gather | solution.py:1029
  31.7 3.7 %all-to-all-done.got_ref = f32[8,40,384]{2,1,0:T(8,128)S(1)} async-done(((f32[8,40,384]{2,1,0:T(8,128)}), f32[8,40,384]{2,1,0:T(8,128)S(1)}, u32[]{:S(2)}, u32[]{:S(2)}) %all-to-all-start) | async-done | bytes 491552 | tf_op jit(solution)/shard_map/all_to_all | solution.py:1026
  37.9 3.7 %all-to-all-start.1 = ((f32[8,32,384]{2,1,0:T(8,128)}), f32[8,32,384]{2,1,0:T(8,128)S(1)}, u32[]{:S(2)}, u32[]{:S(2)}) async-start(f32[8,32,384]{2,1,0:T(8,128)} %shard_map.280), calls=%async_computation.1 | async-start | bytes 786432 | tf_op jit(solution)/shard_map/all_to_all | solution.py:1032
  42.8 6.3 %shard_map.281 = (f32[2,256,384]{2,1,0:T(8,128)}, f32[2,256,384]{2,1,0:T(8,128)}, f32[2,256,384]{2,1,0:T(8,128)}) custom-call(bf16[2,272,768]{2,1,0:T(8,128)(2,1)} %get-tuple-element.98.normed_ref, bf16[768,384]{1,0:T(8,128)(2,1)} %gate_proj_ref.3, f32[2,256,384]{2,1,0:T(8,128)} %get-tuple-element.104.values_ref, ...), custom_call_target="tpu_custom_call" | custom-call | flops 100000000 | bytes 1230854 | tf_op jit(solution)/shard_map/pallas_call | solution.py:197
  49.1 3.5 %all-to-all-done.1 = f32[8,32,384]{2,1,0:T(8,128)S(1)} async-done(((f32[8,32,384]{2,1,0:T(8,128)}), f32[8,32,384]{2,1,0:T(8,128)S(1)}, u32[]{:S(2)}, u32[]{:S(2)}) %all-to-all-start.1) | async-done | bytes 393248 | tf_op jit(solution)/shard_map/all_to_all | solution.py:1032
  53.4 3.4 %shard_map.282 = (f32[2,256,384]{2,1,0:T(8,128)}, f32[8,512]{1,0:T(8,128)}) custom-call(f32[2,128,384]{2,1,0:T(8,128)} %bitcast.67, f32[2,256,256]{2,1,0:T(8,128)} %get-tuple-element.102.states_ref, f32[2,256,384]{2,1,0:T(8,128)} %get-tuple-element.103.exp_cum_x_ref, f32[2,256,384]{2,1,0:T(8,128)} %get-tuple-element.109.base_ref, ...), custom_call_target="tpu_custom_call" | custom-call | flops 100000000 | bytes 1016192 | tf_op jit(solution)/shard_map/pallas_call | solution.py:197
  60.4 2.3 %collective-permute-done.2 = f32[8,512]{1,0:T(8,128)S(1)} collective-permute-done((f32[8,512]{1,0:T(8,128)S(1)}, f32[8,512]{1,0:T(8,128)S(1)}, u32[]{:S(2)}, u32[]{:S(2)}) %collective-permute-start.2) | collective-permute-done | bytes 16416 | tf_op jit(solution)/shard_map/ppermute | solution.py:28
  63.3 3.8 %shard_map.283 = (f32[2,256,384]{2,1,0:T(8,128)}, f32[8,32,384]{2,1,0:T(8,128)}) custom-call(f32[8,512]{1,0:T(8,128)} %add.71.sums_ref, f32[2,256,384]{2,1,0:T(8,128)} %get-tuple-element.113.read_ref, f32[2,256,384]{2,1,0:T(8,128)} %get-tuple-element.109.base_ref, f32[2,256,384]{2,1,0:T(8,128)} %get-tuple-element.110.gate_pre_ref, ...), custom_call_target="tpu_custom_call" | custom-call | flops 100000000 | bytes 1118592 | tf_op jit(solution)/shard_map/pallas_call | solution.py:197
  67.1 3.7 %all-to-all-start.2 = ((f32[8,32,384]{2,1,0:T(8,128)}), f32[8,32,384]{2,1,0:T(8,128)S(1)}, u32[]{:S(2)}, u32[]{:S(2)}) async-start(f32[8,32,384]{2,1,0:T(8,128)} %get-tuple-element.114), calls=%async_computation.2 | async-start | bytes 786432 | tf_op jit(solution)/shard_map/all_to_all | solution.py:1063
  71.4 7.7 %shard_map.284 = (bf16[2,256,384]{2,1,0:T(8,128)(2,1)}, f32[1,768]{1,0:T(1,128)}, f32[8,768]{1,0:T(8,128)}, bf16[4,192,384]{2,1,0:T(8,128)(2,1)}, bf16[4,192,384...) custom-call(s32[2]{0:T(128)} %pad_add_fusion.own_ref, f32[8,512]{1,0:T(8,128)} %add.71.sums_ref, ...), custom_call_target="tpu_custom_call" | custom-call | flops 100000000 | bytes 1884546 | tf_op jit(solution)/shard_map/pallas_call | solution.py:197
  79.1 2.1 %collective-permute-start.3 = (bf16[4,192,384]{2,1,0:T(8,128)(2,1)}, bf16[4,192,384]{2,1,0:T(8,128)(2,1)S(1)}, u32[]{:S(2)}, u32[]{:S(2)}) collective-permute-start(bf16[4,192,384]{2,1,0:T(8,128)(2,1)} %get-tuple-element.116), channel_id=1, source_target_pairs={{0,4},{4,0},{8,12},{12,8},{16,20},{20,16},{24,28},{28,24},{1,5},{5... | collective-permute-start | bytes 1769480 | tf_op jit(solution)/shard_map/ppermute | solution.py:28
  84.3 4.1 %all-to-all-start.3 = ((f32[8,32,384]{2,1,0:T(8,128)}), f32[8,32,384]{2,1,0:T(8,128)S(1)}, u32[]{:S(2)}, u32[]{:S(2)}) async-start(f32[8,32,384]{2,1,0:T(8,128)} %shard_map.285), calls=%async_computation.3 | async-start | bytes 786432 | tf_op jit(solution)/shard_map/all_to_all | solution.py:1109
  89.3 8.0 %shard_map.286 = (f32[2,256,384]{2,1,0:T(8,128)}, f32[2,256,128]{2,1,0:T(8,128)}, f32[2,256,128]{2,1,0:T(8,128)}, f32[2,6,256]{2,1,0:T(8,128)}) custom-call(f32[2,256,384]{2,1,0:T(8,128)} %get-tuple-element.104.values_ref, f32[2,256,256]{2,1,0:T(8,128)} %get-tuple-element.102.states_ref, f32[2,256,384]{2,1,0:T(8,128)} %get-tuple-element.105.step_x_ref, ...), custom_call_target="tpu_custom_call" | custom-call | flops 100000000 | bytes 1021952 | tf_op jit(solution)/shard_map/pallas_call | solution.py:197
  99.9 3.2 %shard_map.288 = (f32[2,512,64]{2,1,0:T(8,128)}, f32[2,512,64]{2,1,0:T(8,128)}) custom-call(s32[2]{0:T(128)} %pad_add_fusion.own_ref, f32[2,128,384]{2,1,0:T(8,128)} %bitcast.70, f32[2,256,384]{2,1,0:T(8,128)} %get-tuple-element.130.weighted_ref, f32[2,256,128]{2,1,0:T(8,128)} %get-tuple-element.131.grad_b_ref, f32[2,256,128]{2,1,0:T(8,128)} %get-tuple-element.132.grad_c_ref), custom_call_target="tpu_custom_call" | custom-call | flops 100000000 | bytes 425986 | tf_op jit(solution)/shard_map/pallas_call | solution.py:197
  109.3 5.8 %shard_map.287 = (f32[2,272,384]{2,1,0:T(8,128)}, bf16[2,6,256]{2,1,0:T(8,128)(2,1)}, f32[5,384]{1,0:T(8,128)}, f32[6,128]{1,0:T(8,128)}) custom-call(f32[2,128,384]{2,1,0:T(8,128)} %bitcast.71, f32[2,128,384]{2,1,0:T(8,128)} %bitcast.69, f32[2,256,384]{2,1,0:T(8,128)} %get-tuple-element.104.values_ref, f32[2,256,256]{2,1,0:T(8,128)} %get-tuple-element.102.states_ref, ...), custom_call_target="tpu_custom_call" | custom-call | flops 100000000 | bytes 2117132 | tf_op jit(solution)/shard_map/pallas_call | solution.py:197
  120.2 4.7 %shard_map.289 = (f32[2,272,64]{2,1,0:T(8,128)}, bf16[8,128,384]{2,1,0:T(8,128)(2,1)}) custom-call(s32[2]{0:T(128)} %pad_add_fusion.own_ref, bf16[2,272,768]{2,1,0:T(8,128)(2,1)} %get-tuple-element.98.normed_ref, f32[2,272,384]{2,1,0:T(8,128)} %get-tuple-element.128.value_in_ref, bf16[2,6,256]{2,1,0:T(8,128)(2,1)} %get-tuple-element.129.grad_step_t_ref, ...), custom_call_target="tpu_custom_call" | custom-call | flops 100000000 | bytes 908162 | tf_op jit(solution)/shard_map/pallas_call | solution.py:197
  125.6 4.6 %all-to-all-start.4 = ((bf16[8,128,384]{2,1,0:T(8,128)(2,1)}), bf16[8,128,384]{2,1,0:T(8,128)(2,1)S(1)}, u32[]{:S(2)}, u32[]{:S(2)}) async-start(bf16[8,128,384]{2,1,0:T(8,128)(2,1)} %get-tuple-element.143), calls=%async_computation.4 | async-start | bytes 1572864 | tf_op jit(solution)/shard_map/all_to_all | solution.py:1200
  131.9 6.0 %collective-permute-done.11 = bf16[1,512,192]{2,1,0:T(8,128)(2,1)S(1)} collective-permute-done((bf16[1,512,192]{2,1,0:T(8,128)(2,1)S(1)}, bf16[1,512,192]{2,1,0:T(8,128)(2,1)S(1)}, u32[]{:S(2)}, u32[]{:S(2)}) %collective-permute-start.11) | collective-permute-done | bytes 196640 | tf_op jit(solution)/shard_map/ppermute | solution.py:28
  141.7 5.6 %collective-permute-start.14 = (bf16[192,384]{1,0:T(8,128)(2,1)S(1)}, bf16[192,384]{1,0:T(8,128)(2,1)}, u32[]{:S(2)}, u32[]{:S(2)}) collective-permute-start(bf16[192,384]{1,0:T(8,128)(2,1)S(1)} %add_convert_fusion.4), channel_id=1, source_target_pairs={{0,24},{4,28},{8,16},{12,20},{16,8},{20,12},{24,0},{28,4},{1,25},{... | collective-permute-start | bytes 442376 | tf_op jit(solution)/shard_map/ppermute | solution.py:28
  151.4 5.0 %shard_map.290 = (bf16[2,512,256]{2,1,0:T(8,128)(2,1)}, bf16[2,512,256]{2,1,0:T(8,128)(2,1)}) custom-call(s32[2]{0:T(128)} %pad_add_fusion.own_ref, bf16[2,256,768]{2,1,0:T(8,128)(2,1)} %tokens_ref.3, f32[768]{0:T(1024)} %gain_ref.5, f32[2,272,384]{2,1,0:T(8,128)} %get-tuple-element.128.value_in_ref, f32[2,272,64]{2,1,0:T(8,128)} %get-tuple-element.150.state_in_ref, ...), custom_call_target="tpu_custom_call" | custom-call | flops 100000000 | bytes 877058 | tf_op jit(solution)/shard_map/pallas_call | solution.py:197
  156.4 7.9 %collective-permute-done.12 = bf16[192,384]{1,0:T(8,128)(2,1)} collective-permute-done((bf16[192,384]{1,0:T(8,128)(2,1)S(1)}, bf16[192,384]{1,0:T(8,128)(2,1)}, u32[]{:S(2)}, u32[]{:S(2)}) %collective-permute-start.12) | collective-permute-done | bytes 147488 | tf_op jit(solution)/shard_map/ppermute | solution.py:28
  166.4 2.1 %shard_map.292 = bf16[8,128,384]{2,1,0:T(8,128)(2,1)} custom-call(bf16[8,128,384]{2,1,0:T(8,128)(2,1)} %copy-done.4), custom_call_target="tpu_custom_call" | custom-call | flops 100000000 | bytes 196608 | tf_op jit(solution)/shard_map/pallas_call | solution.py:197
  168.5 4.4 %all-to-all-start.5 = ((bf16[8,128,384]{2,1,0:T(8,128)(2,1)}), bf16[8,128,384]{2,1,0:T(8,128)(2,1)S(1)}, u32[]{:S(2)}, u32[]{:S(2)}) async-start(bf16[8,128,384]{2,1,0:T(8,128)(2,1)} %shard_map.292), calls=%async_computation.5 | async-start | bytes 1572864 | tf_op jit(solution)/shard_map/all_to_all | solution.py:1238
  177.7 4.0 %collective-permute-done.19 = bf16[512,256]{1,0:T(8,128)(2,1)S(1)} collective-permute-done((bf16[512,256]{1,0:T(8,128)(2,1)S(1)}, bf16[512,256]{1,0:T(8,128)(2,1)S(1)}, u32[]{:S(2)}, u32[]{:S(2)}) %collective-permute-start.19) | collective-permute-done | bytes 262176 | tf_op jit(solution)/shard_map/ppermute | solution.py:28
  181.7 5.7 %collective-permute-done.17 = bf16[512,256]{1,0:T(8,128)(2,1)S(1)} collective-permute-done((bf16[512,256]{1,0:T(8,128)(2,1)S(1)}, bf16[512,256]{1,0:T(8,128)(2,1)S(1)}, u32[]{:S(2)}, u32[]{:S(2)}) %collective-permute-start.17) | collective-permute-done | bytes 262176 | tf_op jit(solution)/shard_map/ppermute | solution.py:28
  188.9 2.3 %all-to-all-done.5 = bf16[8,128,384]{2,1,0:T(8,128)(2,1)S(1)} async-done(((bf16[8,128,384]{2,1,0:T(8,128)(2,1)}), bf16[8,128,384]{2,1,0:T(8,128)(2,1)S(1)}, u32[]{:S(2)}, u32[]{:S(2)}) %all-to-all-start.5) | async-done | bytes 786464 | tf_op jit(solution)/shard_map/all_to_all | solution.py:1238
  192.8 2.4 %collective-permute-done.16.far_ref = bf16[4,192,384]{2,1,0:T(8,128)(2,1)S(1)} collective-permute-done((bf16[4,192,384]{2,1,0:T(8,128)(2,1)S(1)}, bf16[4,192,384]{2,1,0:T(8,128)(2,1)S(1)}, u32[]{:S(2)}, u32[]{:S(2)}) %collective-permute-start.16) | collective-permute-done | bytes 589856 | tf_op jit(solution)/shard_map/ppermute | solution.py:28
  196.1 2.8 %shard_map.291 = (f32[8,96,384]{2,1,0:T(8,128)}, f32[8,48,768]{2,1,0:T(8,128)}) custom-call(s32[2]{0:T(128)} %pad_add_fusion.own_ref, bf16[4,192,384]{2,1,0:T(8,128)(2,1)} %copy-done.5, bf16[4,192,384]{2,1,0:T(8,128)(2,1)} %copy-done.10), custom_call_target="tpu_custom_call" | custom-call | flops 100000000 | bytes 294914 | tf_op jit(solution)/shard_map/pallas_call | solution.py:197
  201.5 2.4 %shard_map.293 = (f32[768,256]{1,0:T(8,128)}, f32[768]{0:T(1024)}, f32[6,768]{1,0:T(8,128)}, f32[4,384]{1,0:T(4,128)}, f32[384]{0:T(512)}, /*index=5*/f32[4,256]...) custom-call(s32[2]{0:T(128)} %pad_add_fusion.own_ref, ...), custom_call_target="tpu_custom_call" | custom-call | flops 100000000 | bytes 196610 | tf_op jit(solution)/shard_map/pallas_call | solution.py:197
  (119 shorter events, 54.1 us)
Async XLA Ops:
  1.5 6.6 %collective-permute-start = (bf16[2,16,768]{2,1,0:T(8,128)(2,1)S(1)}, bf16[2,16,768]{2,1,0:T(8,128)(2,1)S(1)}, u32[]{:S(2)}, u32[]{:S(2)}) collective-permute-start(bf16[2,16,768]{2,1,0:T(8,128)(2,1)S(1)} %slice.75), channel_id=1, source_target_pairs={{0,4},{4,8},{8,12},{12,16},{16,20},{20,24},{24,28},{1,5},{5,9},{9,... | collective-permute-start | bytes 147464 | tf_op jit(solution)/shard_map/ppermute | solution.py:23
  8.7 14.0 %copy-start.15 = (f32[2,256,192]{1,2,0:T(8,128)S(1)}, f32[2,256,192]{1,2,0:T(8,128)}, u32[]{:S(2)}) copy-start(f32[2,256,192]{1,2,0:T(8,128)} %param.31) | copy-start | bytes 1179652
  16.0 19.3 %all-to-all-start = ((f32[8,40,384]{2,1,0:T(8,128)}), f32[8,40,384]{2,1,0:T(8,128)S(1)}, u32[]{:S(2)}, u32[]{:S(2)}) async-start(f32[8,40,384]{2,1,0:T(8,128)} %get-tuple-element.99), calls=%async_computation | async-start | bytes 983040 | tf_op jit(solution)/shard_map/all_to_all | solution.py:1026
  37.9 14.7 %all-to-all-start.1 = ((f32[8,32,384]{2,1,0:T(8,128)}), f32[8,32,384]{2,1,0:T(8,128)S(1)}, u32[]{:S(2)}, u32[]{:S(2)}) async-start(f32[8,32,384]{2,1,0:T(8,128)} %shard_map.280), calls=%async_computation.1 | async-start | bytes 786432 | tf_op jit(solution)/shard_map/all_to_all | solution.py:1032
  56.8 1.4 collective-permute-start.1
  58.9 3.7 %collective-permute-start.2 = (f32[8,512]{1,0:T(8,128)S(1)}, f32[8,512]{1,0:T(8,128)S(1)}, u32[]{:S(2)}, u32[]{:S(2)}) collective-permute-start(f32[8,512]{1,0:T(8,128)S(1)} %add.70), channel_id=1, source_target_pairs={{0,2},{1,3},{2,0},{3,1},{4,6},{5,7},{6,4},{7,5},{8,10},{9,11},{10,... | collective-permute-start | bytes 49160 | tf_op jit(solution)/shard_map/ppermute | solution.py:28
  67.1 14.6 %all-to-all-start.2 = ((f32[8,32,384]{2,1,0:T(8,128)}), f32[8,32,384]{2,1,0:T(8,128)S(1)}, u32[]{:S(2)}, u32[]{:S(2)}) async-start(f32[8,32,384]{2,1,0:T(8,128)} %get-tuple-element.114), calls=%async_computation.2 | async-start | bytes 786432 | tf_op jit(solution)/shard_map/all_to_all | solution.py:1063
  79.1 9.3 %copy-start.7 = (bf16[768,256]{1,0:T(8,128)(2,1)S(1)}, bf16[768,256]{1,0:T(8,128)(2,1)}, u32[]{:S(2)}) copy-start(bf16[768,256]{1,0:T(8,128)(2,1)} %state_proj_ref.1) | copy-start | bytes 1179652
  79.1 18.2 %collective-permute-start.3 = (bf16[4,192,384]{2,1,0:T(8,128)(2,1)}, bf16[4,192,384]{2,1,0:T(8,128)(2,1)S(1)}, u32[]{:S(2)}, u32[]{:S(2)}) collective-permute-start(bf16[4,192,384]{2,1,0:T(8,128)(2,1)} %get-tuple-element.116), channel_id=1, source_target_pairs={{0,4},{4,0},{8,12},{12,8},{16,20},{20,16},{24,28},{28,24},{1,5},{5... | collective-permute-start | bytes 1769480 | tf_op jit(solution)/shard_map/ppermute | solution.py:28
  84.3 14.8 %all-to-all-start.3 = ((f32[8,32,384]{2,1,0:T(8,128)}), f32[8,32,384]{2,1,0:T(8,128)S(1)}, u32[]{:S(2)}, u32[]{:S(2)}) async-start(f32[8,32,384]{2,1,0:T(8,128)} %shard_map.285), calls=%async_computation.3 | async-start | bytes 786432 | tf_op jit(solution)/shard_map/all_to_all | solution.py:1109
  89.3 8.0 %copy-start.9 = (bf16[4,192,384]{2,1,0:T(8,128)(2,1)S(1)}, bf16[4,192,384]{2,1,0:T(8,128)(2,1)}, u32[]{:S(2)}) copy-start(bf16[4,192,384]{2,1,0:T(8,128)(2,1)} %get-tuple-element.118) | copy-start | bytes 1769476
  89.3 40.9 %collective-permute-start.10 = (bf16[2,512,192]{2,1,0:T(8,128)(2,1)}, bf16[2,512,192]{2,1,0:T(8,128)(2,1)S(1)}, u32[]{:S(2)}, u32[]{:S(2)}) collective-permute-start(bf16[2,512,192]{2,1,0:T(8,128)(2,1)} %get-tuple-element.145), channel_id=1, source_target_pairs={{0,1},{1,0},{2,3},{3,2},{4,5},{5,4},{6,7},{7,6},{8,9},{9,8},{10,11... | collective-permute-start | bytes 1179656 | tf_op jit(solution)/shard_map/ppermute | solution.py:28
  105.0 10.1 %collective-permute-start.6 = (f32[512,64]{1,0:T(8,128)}, f32[512,64]{1,0:T(8,128)S(1)}, u32[]{:S(2)}, u32[]{:S(2)}) collective-permute-start(f32[512,64]{1,0:T(8,128)} %get-tuple-element.187), channel_id=1, source_target_pairs={{0,3},{1,2},{2,1},{3,0},{4,7},{5,6},{6,5},{7,4},{8,11},{9,10},{10,... | collective-permute-start | bytes 393224 | tf_op jit(solution)/shard_map/ppermute | solution.py:28
  105.0 11.6 %collective-permute-start.5 = (f32[512,64]{1,0:T(8,128)S(1)}, f32[512,64]{1,0:T(8,128)S(1)}, u32[]{:S(2)}, u32[]{:S(2)}) collective-permute-start(f32[512,64]{1,0:T(8,128)S(1)} %get-tuple-element.186), channel_id=1, source_target_pairs={{0,1},{1,0},{2,3},{3,2},{4,5},{5,4},{6,7},{7,6},{8,9},{9,8},{10,11... | collective-permute-start | bytes 393224 | tf_op jit(solution)/shard_map/ppermute | solution.py:28
  106.6 12.8 %collective-permute-start.4 = (f32[512,64]{1,0:T(8,128)S(1)}, f32[512,64]{1,0:T(8,128)S(1)}, u32[]{:S(2)}, u32[]{:S(2)}) collective-permute-start(f32[512,64]{1,0:T(8,128)S(1)} %slice_bitcast_fusion.5), channel_id=1, source_target_pairs={{0,2},{1,3},{2,0},{3,1},{4,6},{5,7},{6,4},{7,5},{8,10},{9,11},{10,... | collective-permute-start | bytes 393224 | tf_op jit(solution)/shard_map/ppermute | solution.py:28
  108.0 16.9 %collective-permute-start.7 = (bf16[192,384]{1,0:T(8,128)(2,1)}, bf16[192,384]{1,0:T(8,128)(2,1)S(1)}, u32[]{:S(2)}, u32[]{:S(2)}) collective-permute-start(bf16[192,384]{1,0:T(8,128)(2,1)} %get-tuple-element.182), channel_id=1, source_target_pairs={{0,16},{4,20},{8,24},{12,28},{16,0},{20,4},{24,8},{28,12},{1,17},{... | collective-permute-start | bytes 442376 | tf_op jit(solution)/shard_map/ppermute | solution.py:28
  115.1 9.8 %collective-permute-start.8 = (bf16[192,384]{1,0:T(8,128)(2,1)}, bf16[192,384]{1,0:T(8,128)(2,1)S(1)}, u32[]{:S(2)}, u32[]{:S(2)}) collective-permute-start(bf16[192,384]{1,0:T(8,128)(2,1)} %get-tuple-element.181), channel_id=1, source_target_pairs={{0,8},{4,12},{8,0},{12,4},{16,24},{20,28},{24,16},{28,20},{1,9},{5... | collective-permute-start | bytes 442376 | tf_op jit(solution)/shard_map/ppermute | solution.py:28
  116.6 8.3 %collective-permute-start.9 = (bf16[192,384]{1,0:T(8,128)(2,1)S(1)}, bf16[192,384]{1,0:T(8,128)(2,1)S(1)}, u32[]{:S(2)}, u32[]{:S(2)}) collective-permute-start(bf16[192,384]{1,0:T(8,128)(2,1)S(1)} %get-tuple-element.180), channel_id=1, source_target_pairs={{0,24},{4,28},{8,16},{12,20},{16,8},{20,12},{24,0},{28,4},{1,25},{... | collective-permute-start | bytes 442376 | tf_op jit(solution)/shard_map/ppermute | solution.py:28
  125.6 39.9 %all-to-all-start.4 = ((bf16[8,128,384]{2,1,0:T(8,128)(2,1)}), bf16[8,128,384]{2,1,0:T(8,128)(2,1)S(1)}, u32[]{:S(2)}, u32[]{:S(2)}) async-start(bf16[8,128,384]{2,1,0:T(8,128)(2,1)} %get-tuple-element.143), calls=%async_computation.4 | async-start | bytes 1572864 | tf_op jit(solution)/shard_map/all_to_all | solution.py:1200
  130.3 7.5 %collective-permute-start.11 = (bf16[1,512,192]{2,1,0:T(8,128)(2,1)S(1)}, bf16[1,512,192]{2,1,0:T(8,128)(2,1)S(1)}, u32[]{:S(2)}, u32[]{:S(2)}) collective-permute-start(bf16[1,512,192]{2,1,0:T(8,128)(2,1)S(1)} %add_convert_fusion.2), channel_id=1, source_target_pairs={{0,2},{1,3},{2,0},{3,1},{4,6},{5,7},{6,4},{7,5},{8,10},{9,11},{10,... | collective-permute-start | bytes 589832 | tf_op jit(solution)/shard_map/ppermute | solution.py:28
  139.4 10.7 %collective-permute-start.15 = (f32[2,16,448]{2,1,0:T(8,128)S(1)}, f32[2,16,448]{2,1,0:T(8,128)S(1)}, u32[]{:S(2)}, u32[]{:S(2)}) collective-permute-start(f32[2,16,448]{2,1,0:T(8,128)S(1)} %pad_maximum_fusion.1), channel_id=1, source_target_pairs={{4,0},{8,4},{12,8},{16,12},{20,16},{24,20},{28,24},{5,1},{9,5},{13... | collective-permute-start | bytes 172040 | tf_op jit(solution)/shard_map/ppermute | solution.py:23
  141.7 14.7 %collective-permute-start.14 = (bf16[192,384]{1,0:T(8,128)(2,1)S(1)}, bf16[192,384]{1,0:T(8,128)(2,1)}, u32[]{:S(2)}, u32[]{:S(2)}) collective-permute-start(bf16[192,384]{1,0:T(8,128)(2,1)S(1)} %add_convert_fusion.4), channel_id=1, source_target_pairs={{0,24},{4,28},{8,16},{12,20},{16,8},{20,12},{24,0},{28,4},{1,25},{... | collective-permute-start | bytes 442376 | tf_op jit(solution)/shard_map/ppermute | solution.py:28
  147.4 9.0 %collective-permute-start.13 = (bf16[192,384]{1,0:T(8,128)(2,1)S(1)}, bf16[192,384]{1,0:T(8,128)(2,1)}, u32[]{:S(2)}, u32[]{:S(2)}) collective-permute-start(bf16[192,384]{1,0:T(8,128)(2,1)S(1)} %add_convert_fusion.4), channel_id=1, source_target_pairs={{0,8},{4,12},{8,0},{12,4},{16,24},{20,28},{24,16},{28,20},{1,9},{5... | collective-permute-start | bytes 442376 | tf_op jit(solution)/shard_map/ppermute | solution.py:28
  147.4 16.9 %collective-permute-start.12 = (bf16[192,384]{1,0:T(8,128)(2,1)S(1)}, bf16[192,384]{1,0:T(8,128)(2,1)}, u32[]{:S(2)}, u32[]{:S(2)}) collective-permute-start(bf16[192,384]{1,0:T(8,128)(2,1)S(1)} %add_convert_fusion.4), channel_id=1, source_target_pairs={{0,16},{4,20},{8,24},{12,28},{16,0},{20,4},{24,8},{28,12},{1,17},{... | collective-permute-start | bytes 442376 | tf_op jit(solution)/shard_map/ppermute | solution.py:28
  165.5 22.0 %copy-start.5 = (bf16[4,192,384]{2,1,0:T(8,128)(2,1)}, bf16[4,192,384]{2,1,0:T(8,128)(2,1)S(1)}, u32[]{:S(2)}) copy-start(bf16[4,192,384]{2,1,0:T(8,128)(2,1)S(1)} %pad_maximum_fusion.near_ref) | copy-start | bytes 1769476
  168.5 22.7 %all-to-all-start.5 = ((bf16[8,128,384]{2,1,0:T(8,128)(2,1)}), bf16[8,128,384]{2,1,0:T(8,128)(2,1)S(1)}, u32[]{:S(2)}, u32[]{:S(2)}) async-start(bf16[8,128,384]{2,1,0:T(8,128)(2,1)} %shard_map.292), calls=%async_computation.5 | async-start | bytes 1572864 | tf_op jit(solution)/shard_map/all_to_all | solution.py:1238
  173.0 8.6 %collective-permute-start.19 = (bf16[512,256]{1,0:T(8,128)(2,1)S(1)}, bf16[512,256]{1,0:T(8,128)(2,1)S(1)}, u32[]{:S(2)}, u32[]{:S(2)}) collective-permute-start(bf16[512,256]{1,0:T(8,128)(2,1)S(1)} %get-tuple-element.185), channel_id=1, source_target_pairs={{0,3},{1,2},{2,1},{3,0},{4,7},{5,6},{6,5},{7,4},{8,11},{9,10},{10,... | collective-permute-start | bytes 786440 | tf_op jit(solution)/shard_map/ppermute | solution.py:28
  173.1 8.5 %collective-permute-start.18 = (bf16[512,256]{1,0:T(8,128)(2,1)S(1)}, bf16[512,256]{1,0:T(8,128)(2,1)S(1)}, u32[]{:S(2)}, u32[]{:S(2)}) collective-permute-start(bf16[512,256]{1,0:T(8,128)(2,1)S(1)} %get-tuple-element.184), channel_id=1, source_target_pairs={{0,1},{1,0},{2,3},{3,2},{4,5},{5,4},{6,7},{7,6},{8,9},{9,8},{10,11... | collective-permute-start | bytes 786440 | tf_op jit(solution)/shard_map/ppermute | solution.py:28
  174.7 12.6 %collective-permute-start.17 = (bf16[512,256]{1,0:T(8,128)(2,1)S(1)}, bf16[512,256]{1,0:T(8,128)(2,1)S(1)}, u32[]{:S(2)}, u32[]{:S(2)}) collective-permute-start(bf16[512,256]{1,0:T(8,128)(2,1)S(1)} %slice_bitcast_fusion.2), channel_id=1, source_target_pairs={{0,2},{1,3},{2,0},{3,1},{4,6},{5,7},{6,4},{7,5},{8,10},{9,11},{10,... | collective-permute-start | bytes 786440 | tf_op jit(solution)/shard_map/ppermute | solution.py:28
  175.6 19.7 %collective-permute-start.16 = (bf16[4,192,384]{2,1,0:T(8,128)(2,1)S(1)}, bf16[4,192,384]{2,1,0:T(8,128)(2,1)S(1)}, u32[]{:S(2)}, u32[]{:S(2)}) collective-permute-start(bf16[4,192,384]{2,1,0:T(8,128)(2,1)S(1)} %pad_maximum_fusion.near_ref), channel_id=1, source_target_pairs={{0,4},{4,0},{8,12},{12,8},{16,20},{20,16},{24,28},{28,24},{1,5},{5... | collective-permute-start | bytes 1769480 | tf_op jit(solution)/shard_map/ppermute | solution.py:28
  191.3 7.6 %collective-permute-start.20 = (bf16[1,8,32,384]{3,2,1,0:T(8,128)(2,1)S(1)}, bf16[1,8,32,384]{3,2,1,0:T(8,128)(2,1)S(1)}, u32[]{:S(2)}, u32[]{:S(2)}) collective-permute-start(bf16[1,8,32,384]{3,2,1,0:T(8,128)(2,1)S(1)} %slice_bitcast_fusion.6), channel_id=1, source_target_pairs={{0,2},{1,3},{2,0},{3,1},{4,6},{5,7},{6,4},{7,5},{8,10},{9,11},{10,... | collective-permute-start | bytes 589832 | tf_op jit(solution)/shard_map/ppermute | solution.py:28
  199.0 1.8 collective-permute-start.21
  (16 other events, 30.6 us)

commit v3 on v2

--- a/solution.py
+++ b/solution.py
@@ -714,12 +714,14 @@
     head_rows_ref,
     inner_row_ref,
     state_in_ref,
-    late_ref,
+    keep_ref,
+    send_ref,
     around,
     small,
     slope,
     conv_in,
     conv_weight,
+    late,
     *,
     pieces,
 ):
@@ -734,7 +736,7 @@
             conv_weight[...] = conv_weight_ref[:, lanes]
 
     width = normed_ref.shape[2]
-    blocks, _, inner = late_ref.shape
+    blocks, _, inner = late.shape
     value_total = state_total = step_total = conv_total = None
 
     def add(total, part):
@@ -783,22 +785,34 @@
         state = state_total[block * state_lines : (block + 1) * state_lines]
         lines = small_rows[block * small_lines : (block + 1) * small_lines]
         value = [value, *stacked(state, inner), *[x.astype(F32) for x in parts(lines, 2)]]
-        spare = late_ref.shape[1] - sum(x.shape[0] for x in value)
+        spare = late.shape[1] - sum(x.shape[0] for x in value)
         if spare:
             value.append(jnp.zeros((spare, inner), F32))
-        late_ref[block] = jnp.concatenate(value, axis=0).astype(BF16)
-
-
-def sum_kernel(got_ref, out_ref, *, first, lines):
-    total = got_ref[0].astype(F32)
-    for block in range(1, got_ref.shape[0]):
-        total = total + got_ref[block].astype(F32)
+        late[block] = jnp.concatenate(value, axis=0).astype(BF16)
+    for p, mask in enumerate(places(orders(blocks)[0])):
+        ref = keep_ref if p < blocks // 2 else send_ref
+        ref[p % (blocks // 2)] = late[own_ref[0] ^ mask]
+
+
+def sum_terms(terms, first, lines):
+    total = terms[0].astype(F32)
+    for term in terms[1:]:
+        total = total + term.astype(F32)
     small = total[first : first + lines] + total[first + lines : first + 2 * lines]
     small = [x.astype(F32) for x in parts(small, 2)]
     spare = [total[first + 2 * lines :]] if total.shape[0] > first + 2 * lines else []
-    total = jnp.concatenate([total[:first], *small, *spare], axis=0).astype(BF16)
+    return jnp.concatenate([total[:first], *small, *spare], axis=0).astype(BF16)
+
+
+def pair_kernel(keep_ref, got_ref, out_ref, **small):
     for block in range(out_ref.shape[0]):
-        out_ref[block] = total
+        out_ref[block] = sum_terms([keep_ref[block], got_ref[block]], **small)
+
+
+def sum_kernel(*refs, **small):
+    total = sum_terms([ref[...] for ref in refs[:-1]], **small)
+    for block in range(refs[-1].shape[0]):
+        refs[-1][block] = total
 
 
 def place_kernel(own_ref, near_ref, far_ref, gate_ref, out_ref):
@@ -1162,11 +1176,11 @@
     small_rows = -(-(heads + max(heads, taps + 1) + 2) // 8) * 8
     small_lines = small_rows * (small_lanes // inner) // blocks
     late_lines = -(-(value_lines + state_lines + 2 * small_lines) // 16) * 16
-    state_grad_in, late = local(
+    state_grad_in, late_keep, late_send = local(
         functools.partial(weight_kernel, pieces=head_devices),
         [
             ((seqs, PAD + length, part), F32),
-            ((blocks, late_lines, inner), BF16),
+            *halves(blocks, late_lines, inner),
         ],
         [
             own,
@@ -1192,17 +1206,23 @@
             pltpu.VMEM((seqs, length, part), F32),
             pltpu.VMEM((seqs, PAD + length, part), F32),
             pltpu.VMEM((taps, part), F32),
-        ],
-    )
-    late, early = lax.optimization_barrier((late, early))
+            pltpu.VMEM((blocks, late_lines, inner), BF16),
+        ],
+    )
+    late_send, early = lax.optimization_barrier((late_send, early))
+    late = swap(late_send, "seq", 1)
     early = sum(x.astype(F32) for x in early).astype(BF16)
     early = [swap(early, "seq", mask) if mask else early for mask in even]
-    late = lax.all_to_all(late, "seq", 0, 0)
+    late_small = dict(first=value_lines + state_lines, lines=small_lines)
+    (late,) = local(
+        functools.partial(pair_kernel, **late_small),
+        [((blocks // 2, late_lines, inner), BF16)],
+        [late_keep, late],
+    )
+    late = [swap(late[p], "seq", mask) if mask else late[p] for p, mask in enumerate(even)]
     over = jnp.concatenate([value_in[:, :PAD], state_grad_in[:, :PAD]], axis=2)
     over = shift(over, "seq", -1)
-    branch = branch_chain.finish().astype(F32)
     own_source = own_cols(tokens.reshape(rows, width), col_width).astype(F32)
-    mixed_rows = jnp.swapaxes((own_source + branch).reshape(seqs, length, col_width), 1, 2)
     back_width = -(-(col_width + 1) // LANES) * LANES
     keep, send = local(
         functools.partial(back_kernel, col_width=col_width),
@@ -1223,17 +1243,19 @@
         ],
         steps=seqs,
     )
+    branch_chain.step()
+    branch_chain.step(after=(keep,))
+    branch = branch_chain.finish().astype(F32)
+    mixed_rows = jnp.swapaxes((own_source + branch).reshape(seqs, length, col_width), 1, 2)
     early = jnp.stack(early)
     late, mixed_rows, early, keep, send = lax.optimization_barrier(
         (late, mixed_rows, early, keep, send)
     )
     early_far = swap(early, "seq", 1)
     (late_values,) = local(
-        functools.partial(
-            sum_kernel, first=value_lines + state_lines, lines=small_lines
-        ),
+        functools.partial(sum_kernel, **late_small),
         [((blocks, late_lines, inner), BF16)],
-        [late],
+        late,
     )
     late = lax.all_to_all(late_values, "seq", 0, 0)
     own_part = send_direct(keep, send, "head", near_head)

time: 205 us -> 198 us (0.966)
  waiting for transfers between devices: 44.6 us -> 36.8 us
    ppermute x20 -> x24, waiting for transfers between devices: 31.3 us -> 22.6 us  [swap(): return lax.ppermute(x, axis, [(i, i ^ mask) for i in range(devices)])]
    all_to_all x1 -> x0, starting transfers between devices: 4.62 us -> none  [on_device(): late = lax.all_to_all(late, 'seq', 0, 0)]
    ppermute x20 -> x24, starting transfers between devices: 24 us -> 28.2 us  [swap(): return lax.ppermute(x, axis, [(i, i ^ mask) for i in range(devices)])]
    all_to_all x1, waiting for transfers between devices: 2.31 us -> 4.64 us  [on_device(): late = lax.all_to_all(late_values, 'seq', 0, 0)]
    pallas_call x15 -> x16, Pallas kernels: 66.5 us -> 68.3 us  [local(): pl.pallas_call(body, grid=(steps,), out_shape=[jax.ShapeDtypeStruct(shape...]
    unnamed x44 -> x46, local copies, waits for them, and re-layouts: 7.88 us -> 6.83 us
  transfers between devices with their start and end apart: 28 -> 31, of which waited for: 15 -> 15; matrix products, arithmetic and copies ran while one was open for 8% -> 9% of each run, Pallas kernels for 22% -> 24%
where the time goes in v3:
time: 198 us; the launch traced here: 197 us
  Pallas kernels  68.3 us (34%)
  starting transfers between devices  57 us (29%)
  waiting for transfers between devices  36.8 us (19%)
  local copies, waits for them, and re-layouts  17.4 us (9%)
  blocking collectives  8.6 us (4%)
  other arithmetic  7.37 us (4%)
    pallas_call x16, Pallas kernels, local(): pl.pallas_call(body, grid=(steps,), out_shape=[jax.ShapeDtypeStruct(shape...  68.3 us
    ppermute x24, starting transfers between devices, swap(): return lax.ppermute(x, axis, [(i, i ^ mask) for i in range(devices)])  28.2 us
    ppermute x24, waiting for transfers between devices, swap(): return lax.ppermute(x, axis, [(i, i ^ mask) for i in range(devices)])  22.6 us
    all_gather x1, blocking collectives, on_device(): cot_low = lax.all_gather(cot_low, 'head', axis=1, tiled=True)  8.6 us
    unnamed x46, local copies, waits for them, and re-layouts  6.83 us
    all_to_all x1, starting transfers between devices, on_device(): got = lax.all_to_all(ends, 'seq', 0, 0)  6.66 us
    ppermute x2, starting transfers between devices, shift(): return lax.ppermute(x, axis, pairs)  6.15 us
    all_to_all x1, waiting for transfers between devices, on_device(): late = lax.all_to_all(late_values, 'seq', 0, 0)  4.64 us
  transfers between devices with their start and end apart: 31, of which 15 were waited for; matrix products, arithmetic and copies ran while one was open for 9% of the time, Pallas kernels for 24%

profile of v3, /device:TPU:0, one launch (start us, length us, event | category | flops | bytes accessed | tf_op | source)
XLA Modules:
  0.0 196.7 jit_solution(17237941747782861777)
XLA Ops:
  1.5 4.9 %collective-permute-start = (bf16[2,16,768]{2,1,0:T(8,128)(2,1)S(1)}, bf16[2,16,768]{2,1,0:T(8,128)(2,1)S(1)}, u32[]{:S(2)}, u32[]{:S(2)}) collective-permute-start(bf16[2,16,768]{2,1,0:T(8,128)(2,1)S(1)} %slice.87), channel_id=1, source_target_pairs={{0,4},{4,8},{8,12},{12,16},{16,20},{20,24},{24,28},{1,5},{5,9},{9,... | collective-permute-start | bytes 147464 | tf_op jit(solution)/shard_map/ppermute | solution.py:23
  8.7 7.3 %shard_map.279 = (bf16[2,272,768]{2,1,0:T(8,128)(2,1)}, f32[2,272,384]{2,1,0:T(8,128)}, f32[2,272,256]{2,1,0:T(8,128)}, f32[2,256,384]{2,1,0:T(8,128)}, f32[2,25...) custom-call(bf16[2,256,768]{2,1,0:T(8,128)(2,1)} %tokens_ref.3, ...), custom_call_target="tpu_custom_call" | custom-call | flops 100000000 | bytes 460940 | tf_op jit(solution)/shard_map/pallas_call | solution.py:197
  16.0 6.7 %all-to-all-start = ((f32[8,40,384]{2,1,0:T(8,128)}), f32[8,40,384]{2,1,0:T(8,128)S(1)}, u32[]{:S(2)}, u32[]{:S(2)}) async-start(f32[8,40,384]{2,1,0:T(8,128)} %get-tuple-element.104), calls=%async_computation | async-start | bytes 983040 | tf_op jit(solution)/shard_map/all_to_all | solution.py:1040
  23.1 8.6 %all_gather.3 = bf16[512,768]{0,1:T(8,128)(2,1)S(1)} all-gather(bf16[512,192]{0,1:T(8,128)(2,1)S(1)} %copy.41), channel_id=1, replica_groups=mesh['seq'=8,'head'=4] {'head'}, dimensions={1}, use_global_device_ids=true | all-gather | bytes 983040 | tf_op jit(solution)/shard_map/all_gather | solution.py:1043
  31.7 3.7 %all-to-all-done.got_ref = f32[8,40,384]{2,1,0:T(8,128)S(1)} async-done(((f32[8,40,384]{2,1,0:T(8,128)}), f32[8,40,384]{2,1,0:T(8,128)S(1)}, u32[]{:S(2)}, u32[]{:S(2)}) %all-to-all-start) | async-done | bytes 491552 | tf_op jit(solution)/shard_map/all_to_all | solution.py:1040
  37.9 3.7 %all-to-all-start.1 = ((f32[8,32,384]{2,1,0:T(8,128)}), f32[8,32,384]{2,1,0:T(8,128)S(1)}, u32[]{:S(2)}, u32[]{:S(2)}) async-start(f32[8,32,384]{2,1,0:T(8,128)} %shard_map.280), calls=%async_computation.1 | async-start | bytes 786432 | tf_op jit(solution)/shard_map/all_to_all | solution.py:1046
  42.8 6.3 %shard_map.281 = (f32[2,256,384]{2,1,0:T(8,128)}, f32[2,256,384]{2,1,0:T(8,128)}, f32[2,256,384]{2,1,0:T(8,128)}) custom-call(bf16[2,272,768]{2,1,0:T(8,128)(2,1)} %get-tuple-element.103.normed_ref, bf16[768,384]{1,0:T(8,128)(2,1)} %gate_proj_ref.3, f32[2,256,384]{2,1,0:T(8,128)} %get-tuple-element.109.values_ref, ...), custom_call_target="tpu_custom_call" | custom-call | flops 100000000 | bytes 1230854 | tf_op jit(solution)/shard_map/pallas_call | solution.py:197
  49.1 3.5 %all-to-all-done.1 = f32[8,32,384]{2,1,0:T(8,128)S(1)} async-done(((f32[8,32,384]{2,1,0:T(8,128)}), f32[8,32,384]{2,1,0:T(8,128)S(1)}, u32[]{:S(2)}, u32[]{:S(2)}) %all-to-all-start.1) | async-done | bytes 393248 | tf_op jit(solution)/shard_map/all_to_all | solution.py:1046
  53.3 3.4 %shard_map.282 = (f32[2,256,384]{2,1,0:T(8,128)}, f32[8,512]{1,0:T(8,128)}) custom-call(f32[2,128,384]{2,1,0:T(8,128)} %bitcast.75, f32[2,256,256]{2,1,0:T(8,128)} %get-tuple-element.107.states_ref, f32[2,256,384]{2,1,0:T(8,128)} %get-tuple-element.108.exp_cum_x_ref, f32[2,256,384]{2,1,0:T(8,128)} %get-tuple-element.114.base_ref, ...), custom_call_target="tpu_custom_call" | custom-call | flops 100000000 | bytes 1016192 | tf_op jit(solution)/shard_map/pallas_call | solution.py:197
  60.4 2.3 %collective-permute-done.2 = f32[8,512]{1,0:T(8,128)S(1)} collective-permute-done((f32[8,512]{1,0:T(8,128)S(1)}, f32[8,512]{1,0:T(8,128)S(1)}, u32[]{:S(2)}, u32[]{:S(2)}) %collective-permute-start.2) | collective-permute-done | bytes 16416 | tf_op jit(solution)/shard_map/ppermute | solution.py:28
  63.2 3.8 %shard_map.283 = (f32[2,256,384]{2,1,0:T(8,128)}, f32[8,32,384]{2,1,0:T(8,128)}) custom-call(f32[8,512]{1,0:T(8,128)} %add.71.sums_ref, f32[2,256,384]{2,1,0:T(8,128)} %get-tuple-element.118.read_ref, f32[2,256,384]{2,1,0:T(8,128)} %get-tuple-element.114.base_ref, f32[2,256,384]{2,1,0:T(8,128)} %get-tuple-element.115.gate_pre_ref, ...), custom_call_target="tpu_custom_call" | custom-call | flops 100000000 | bytes 1118592 | tf_op jit(solution)/shard_map/pallas_call | solution.py:197
  67.0 3.7 %all-to-all-start.2 = ((f32[8,32,384]{2,1,0:T(8,128)}), f32[8,32,384]{2,1,0:T(8,128)S(1)}, u32[]{:S(2)}, u32[]{:S(2)}) async-start(f32[8,32,384]{2,1,0:T(8,128)} %get-tuple-element.119), calls=%async_computation.2 | async-start | bytes 786432 | tf_op jit(solution)/shard_map/all_to_all | solution.py:1077
  71.4 7.7 %shard_map.284 = (bf16[2,256,384]{2,1,0:T(8,128)(2,1)}, f32[1,768]{1,0:T(1,128)}, f32[8,768]{1,0:T(8,128)}, bf16[4,192,384]{2,1,0:T(8,128)(2,1)}, bf16[4,192,384...) custom-call(s32[2]{0:T(128)} %pad_add_fusion.own_ref, f32[8,512]{1,0:T(8,128)} %add.71.sums_ref, ...), custom_call_target="tpu_custom_call" | custom-call | flops 100000000 | bytes 1884546 | tf_op jit(solution)/shard_map/pallas_call | solution.py:197
  79.1 2.1 %collective-permute-start.3 = (bf16[4,192,384]{2,1,0:T(8,128)(2,1)}, bf16[4,192,384]{2,1,0:T(8,128)(2,1)S(1)}, u32[]{:S(2)}, u32[]{:S(2)}) collective-permute-start(bf16[4,192,384]{2,1,0:T(8,128)(2,1)} %get-tuple-element.121), channel_id=1, source_target_pairs={{0,4},{4,0},{8,12},{12,8},{16,20},{20,16},{24,28},{28,24},{1,5},{5... | collective-permute-start | bytes 1769480 | tf_op jit(solution)/shard_map/ppermute | solution.py:28
  84.2 4.2 %all-to-all-start.3 = ((f32[8,32,384]{2,1,0:T(8,128)}), f32[8,32,384]{2,1,0:T(8,128)S(1)}, u32[]{:S(2)}, u32[]{:S(2)}) async-start(f32[8,32,384]{2,1,0:T(8,128)} %shard_map.285), calls=%async_computation.3 | async-start | bytes 786432 | tf_op jit(solution)/shard_map/all_to_all | solution.py:1123
  91.9 7.9 %shard_map.286 = (f32[2,256,384]{2,1,0:T(8,128)}, f32[2,256,128]{2,1,0:T(8,128)}, f32[2,256,128]{2,1,0:T(8,128)}, f32[2,6,256]{2,1,0:T(8,128)}) custom-call(f32[2,256,384]{2,1,0:T(8,128)} %get-tuple-element.109.values_ref, f32[2,256,256]{2,1,0:T(8,128)} %get-tuple-element.107.states_ref, f32[2,256,384]{2,1,0:T(8,128)} %get-tuple-element.110.step_x_ref, ...), custom_call_target="tpu_custom_call" | custom-call | flops 100000000 | bytes 1021952 | tf_op jit(solution)/shard_map/pallas_call | solution.py:197
  101.2 3.2 %shard_map.288 = (f32[2,512,64]{2,1,0:T(8,128)}, f32[2,512,64]{2,1,0:T(8,128)}) custom-call(s32[2]{0:T(128)} %pad_add_fusion.own_ref, f32[2,128,384]{2,1,0:T(8,128)} %bitcast.78, f32[2,256,384]{2,1,0:T(8,128)} %get-tuple-element.135.weighted_ref, f32[2,256,128]{2,1,0:T(8,128)} %get-tuple-element.136.grad_b_ref, f32[2,256,128]{2,1,0:T(8,128)} %get-tuple-element.137.grad_c_ref), custom_call_target="tpu_custom_call" | custom-call | flops 100000000 | bytes 425986 | tf_op jit(solution)/shard_map/pallas_call | solution.py:197
  108.5 2.5 %collective-permute-start.7 = (bf16[192,384]{1,0:T(8,128)(2,1)}, bf16[192,384]{1,0:T(8,128)(2,1)S(1)}, u32[]{:S(2)}, u32[]{:S(2)}) collective-permute-start(bf16[192,384]{1,0:T(8,128)(2,1)} %get-tuple-element.192), channel_id=1, source_target_pairs={{0,16},{4,20},{8,24},{12,28},{16,0},{20,4},{24,8},{28,12},{1,17},{... | collective-permute-start | bytes 442376 | tf_op jit(solution)/shard_map/ppermute | solution.py:28
  111.1 5.8 %shard_map.287 = (f32[2,272,384]{2,1,0:T(8,128)}, bf16[2,6,256]{2,1,0:T(8,128)(2,1)}, f32[5,384]{1,0:T(8,128)}, f32[6,128]{1,0:T(8,128)}) custom-call(f32[2,128,384]{2,1,0:T(8,128)} %bitcast.79, f32[2,128,384]{2,1,0:T(8,128)} %bitcast.77, f32[2,256,384]{2,1,0:T(8,128)} %get-tuple-element.109.values_ref, f32[2,256,256]{2,1,0:T(8,128)} %get-tuple-element.107.states_ref, ...), custom_call_target="tpu_custom_call" | custom-call | flops 100000000 | bytes 2117132 | tf_op jit(solution)/shard_map/pallas_call | solution.py:197
  120.6 4.7 %shard_map.289 = (f32[2,272,64]{2,1,0:T(8,128)}, bf16[4,128,384]{2,1,0:T(8,128)(2,1)}, bf16[4,128,384]{2,1,0:T(8,128)(2,1)}) custom-call(s32[2]{0:T(128)} %pad_add_fusion.own_ref, bf16[2,272,768]{2,1,0:T(8,128)(2,1)} %get-tuple-element.103.normed_ref, f32[2,272,384]{2,1,0:T(8,128)} %get-tuple-element.133.value_in_ref, ...), custom_call_target="tpu_custom_call" | custom-call | flops 100000000 | bytes 908162 | tf_op jit(solution)/shard_map/pallas_call | solution.py:197
  127.4 2.7 %collective-permute-start.10 = (bf16[4,128,384]{2,1,0:T(8,128)(2,1)}, bf16[4,128,384]{2,1,0:T(8,128)(2,1)S(1)}, u32[]{:S(2)}, u32[]{:S(2)}) collective-permute-start(bf16[4,128,384]{2,1,0:T(8,128)(2,1)} %get-tuple-element.149), channel_id=1, source_target_pairs={{0,4},{4,0},{8,12},{12,8},{16,20},{20,16},{24,28},{28,24},{1,5},{5... | collective-permute-start | bytes 1179656 | tf_op jit(solution)/shard_map/ppermute | solution.py:28
  130.2 3.2 %collective-permute-start.19 = (bf16[192,384]{1,0:T(8,128)(2,1)S(1)}, bf16[192,384]{1,0:T(8,128)(2,1)S(1)}, u32[]{:S(2)}, u32[]{:S(2)}) collective-permute-start(bf16[192,384]{1,0:T(8,128)(2,1)S(1)} %add_convert_fusion.4), channel_id=1, source_target_pairs={{0,24},{4,28},{8,16},{12,20},{16,8},{20,12},{24,0},{28,4},{1,25},{... | collective-permute-start | bytes 442376 | tf_op jit(solution)/shard_map/ppermute | solution.py:28
  135.9 5.1 %shard_map.291 = (bf16[2,512,256]{2,1,0:T(8,128)(2,1)}, bf16[2,512,256]{2,1,0:T(8,128)(2,1)}) custom-call(s32[2]{0:T(128)} %pad_add_fusion.own_ref, bf16[2,256,768]{2,1,0:T(8,128)(2,1)} %tokens_ref.3, f32[768]{0:T(1024)} %gain_ref.5, f32[2,272,384]{2,1,0:T(8,128)} %get-tuple-element.133.value_in_ref, f32[2,272,64]{2,1,0:T(8,128)} %get-tuple-element.152.state_in_ref, ...), custom_call_target="tpu_custom_call" | custom-call | flops 100000000 | bytes 877058 | tf_op jit(solution)/shard_map/pallas_call | solution.py:197
  152.1 4.3 %collective-permute-done.11.refs_1_ = bf16[128,384]{1,0:T(8,128)(2,1)S(1)} collective-permute-done((bf16[128,384]{1,0:T(8,128)(2,1)S(1)}, bf16[128,384]{1,0:T(8,128)(2,1)S(1)}, u32[]{:S(2)}, u32[]{:S(2)}) %collective-permute-start.11) | collective-permute-done | bytes 98336 | tf_op jit(solution)/shard_map/ppermute | solution.py:28
  160.5 4.5 %all-to-all-start.4 = ((bf16[8,128,384]{2,1,0:T(8,128)(2,1)}), bf16[8,128,384]{2,1,0:T(8,128)(2,1)S(1)}, u32[]{:S(2)}, u32[]{:S(2)}) async-start(bf16[8,128,384]{2,1,0:T(8,128)(2,1)} %shard_map.293), calls=%async_computation.4 | async-start | bytes 1572864 | tf_op jit(solution)/shard_map/all_to_all | solution.py:1260
  167.6 2.1 %collective-permute-start.20 = (bf16[4,192,384]{2,1,0:T(8,128)(2,1)S(1)}, bf16[4,192,384]{2,1,0:T(8,128)(2,1)}, u32[]{:S(2)}, u32[]{:S(2)}) collective-permute-start(bf16[4,192,384]{2,1,0:T(8,128)(2,1)S(1)} %pad_maximum_fusion.near_ref), channel_id=1, source_target_pairs={{0,4},{4,0},{8,12},{12,8},{16,20},{20,16},{24,28},{28,24},{1,5},{5... | collective-permute-start | bytes 1769480 | tf_op jit(solution)/shard_map/ppermute | solution.py:28
  169.7 4.0 %collective-permute-done.23 = bf16[512,256]{1,0:T(8,128)(2,1)S(1)} collective-permute-done((bf16[512,256]{1,0:T(8,128)(2,1)S(1)}, bf16[512,256]{1,0:T(8,128)(2,1)S(1)}, u32[]{:S(2)}, u32[]{:S(2)}) %collective-permute-start.23) | collective-permute-done | bytes 262176 | tf_op jit(solution)/shard_map/ppermute | solution.py:28
  173.6 4.7 %collective-permute-done.21 = bf16[512,256]{1,0:T(8,128)(2,1)S(1)} collective-permute-done((bf16[512,256]{1,0:T(8,128)(2,1)S(1)}, bf16[512,256]{1,0:T(8,128)(2,1)S(1)}, u32[]{:S(2)}, u32[]{:S(2)}) %collective-permute-start.21) | collective-permute-done | bytes 262176 | tf_op jit(solution)/shard_map/ppermute | solution.py:28
  180.0 4.6 %all-to-all-done.4 = bf16[8,128,384]{2,1,0:T(8,128)(2,1)S(1)} async-done(((bf16[8,128,384]{2,1,0:T(8,128)(2,1)}), bf16[8,128,384]{2,1,0:T(8,128)(2,1)S(1)}, u32[]{:S(2)}, u32[]{:S(2)}) %all-to-all-start.4) | async-done | bytes 786464 | tf_op jit(solution)/shard_map/all_to_all | solution.py:1260
  185.0 3.7 %collective-permute-done.20.far_ref = bf16[4,192,384]{2,1,0:T(8,128)(2,1)} collective-permute-done((bf16[4,192,384]{2,1,0:T(8,128)(2,1)S(1)}, bf16[4,192,384]{2,1,0:T(8,128)(2,1)}, u32[]{:S(2)}, u32[]{:S(2)}) %collective-permute-start.20) | collective-permute-done | bytes 589856 | tf_op jit(solution)/shard_map/ppermute | solution.py:28
  188.7 2.8 %shard_map.292 = (f32[8,96,384]{2,1,0:T(8,128)}, f32[8,48,768]{2,1,0:T(8,128)}) custom-call(s32[2]{0:T(128)} %pad_add_fusion.own_ref, bf16[4,192,384]{2,1,0:T(8,128)(2,1)} %copy-done.4, bf16[4,192,384]{2,1,0:T(8,128)(2,1)} %collective-permute-done.20.far_ref), custom_call_target="tpu_custom_call" | custom-call | flops 100000000 | bytes 294914 | tf_op jit(solution)/shard_map/pallas_call | solution.py:197
  194.1 2.4 %shard_map.294 = (f32[768,256]{1,0:T(8,128)}, f32[768]{0:T(1024)}, f32[6,768]{1,0:T(8,128)}, f32[4,384]{1,0:T(4,128)}, f32[384]{0:T(512)}, /*index=5*/f32[4,256]...) custom-call(s32[2]{0:T(128)} %pad_add_fusion.own_ref, ...), custom_call_target="tpu_custom_call" | custom-call | flops 100000000 | bytes 196610 | tf_op jit(solution)/shard_map/pallas_call | solution.py:197
  (129 shorter events, 55.6 us)
Async XLA Ops:
  1.5 6.6 %collective-permute-start = (bf16[2,16,768]{2,1,0:T(8,128)(2,1)S(1)}, bf16[2,16,768]{2,1,0:T(8,128)(2,1)S(1)}, u32[]{:S(2)}, u32[]{:S(2)}) collective-permute-start(bf16[2,16,768]{2,1,0:T(8,128)(2,1)S(1)} %slice.87), channel_id=1, source_target_pairs={{0,4},{4,8},{8,12},{12,16},{16,20},{20,24},{24,28},{1,5},{5,9},{9,... | collective-permute-start | bytes 147464 | tf_op jit(solution)/shard_map/ppermute | solution.py:23
  16.0 19.3 %all-to-all-start = ((f32[8,40,384]{2,1,0:T(8,128)}), f32[8,40,384]{2,1,0:T(8,128)S(1)}, u32[]{:S(2)}, u32[]{:S(2)}) async-start(f32[8,40,384]{2,1,0:T(8,128)} %get-tuple-element.104), calls=%async_computation | async-start | bytes 983040 | tf_op jit(solution)/shard_map/all_to_all | solution.py:1040
  37.9 14.7 %all-to-all-start.1 = ((f32[8,32,384]{2,1,0:T(8,128)}), f32[8,32,384]{2,1,0:T(8,128)S(1)}, u32[]{:S(2)}, u32[]{:S(2)}) async-start(f32[8,32,384]{2,1,0:T(8,128)} %shard_map.280), calls=%async_computation.1 | async-start | bytes 786432 | tf_op jit(solution)/shard_map/all_to_all | solution.py:1046
  56.8 1.4 collective-permute-start.1
  58.9 3.7 %collective-permute-start.2 = (f32[8,512]{1,0:T(8,128)S(1)}, f32[8,512]{1,0:T(8,128)S(1)}, u32[]{:S(2)}, u32[]{:S(2)}) collective-permute-start(f32[8,512]{1,0:T(8,128)S(1)} %add.70), channel_id=1, source_target_pairs={{0,2},{1,3},{2,0},{3,1},{4,6},{5,7},{6,4},{7,5},{8,10},{9,11},{10,... | collective-permute-start | bytes 49160 | tf_op jit(solution)/shard_map/ppermute | solution.py:28
  67.0 14.5 %all-to-all-start.2 = ((f32[8,32,384]{2,1,0:T(8,128)}), f32[8,32,384]{2,1,0:T(8,128)S(1)}, u32[]{:S(2)}, u32[]{:S(2)}) async-start(f32[8,32,384]{2,1,0:T(8,128)} %get-tuple-element.119), calls=%async_computation.2 | async-start | bytes 786432 | tf_op jit(solution)/shard_map/all_to_all | solution.py:1077
  79.0 10.3 %collective-permute-start.14 = (bf16[2,512,192]{2,1,0:T(8,128)(2,1)}, bf16[2,512,192]{2,1,0:T(8,128)(2,1)}, u32[]{:S(2)}, u32[]{:S(2)}) collective-permute-start(bf16[2,512,192]{2,1,0:T(8,128)(2,1)} %get-tuple-element.151), channel_id=1, source_target_pairs={{0,1},{1,0},{2,3},{3,2},{4,5},{5,4},{6,7},{7,6},{8,9},{9,8},{10,11... | collective-permute-start | bytes 1179656 | tf_op jit(solution)/shard_map/ppermute | solution.py:28
  79.1 20.7 %collective-permute-start.3 = (bf16[4,192,384]{2,1,0:T(8,128)(2,1)}, bf16[4,192,384]{2,1,0:T(8,128)(2,1)S(1)}, u32[]{:S(2)}, u32[]{:S(2)}) collective-permute-start(bf16[4,192,384]{2,1,0:T(8,128)(2,1)} %get-tuple-element.121), channel_id=1, source_target_pairs={{0,4},{4,0},{8,12},{12,8},{16,20},{20,16},{24,28},{28,24},{1,5},{5... | collective-permute-start | bytes 1769480 | tf_op jit(solution)/shard_map/ppermute | solution.py:28
  84.2 16.2 %all-to-all-start.3 = ((f32[8,32,384]{2,1,0:T(8,128)}), f32[8,32,384]{2,1,0:T(8,128)S(1)}, u32[]{:S(2)}, u32[]{:S(2)}) async-start(f32[8,32,384]{2,1,0:T(8,128)} %shard_map.285), calls=%async_computation.3 | async-start | bytes 786432 | tf_op jit(solution)/shard_map/all_to_all | solution.py:1123
  90.4 50.6 %collective-permute-start.15 = (bf16[1,512,192]{2,1,0:T(8,128)(2,1)S(1)}, bf16[1,512,192]{2,1,0:T(8,128)(2,1)}, u32[]{:S(2)}, u32[]{:S(2)}) collective-permute-start(bf16[1,512,192]{2,1,0:T(8,128)(2,1)S(1)} %add_convert_fusion.2), channel_id=1, source_target_pairs={{0,2},{1,3},{2,0},{3,1},{4,6},{5,7},{6,4},{7,5},{8,10},{9,11},{10,... | collective-permute-start | bytes 589832 | tf_op jit(solution)/shard_map/ppermute | solution.py:28
  105.5 12.1 %collective-permute-start.6 = (f32[512,64]{1,0:T(8,128)S(1)}, f32[512,64]{1,0:T(8,128)S(1)}, u32[]{:S(2)}, u32[]{:S(2)}) collective-permute-start(f32[512,64]{1,0:T(8,128)S(1)} %get-tuple-element.197), channel_id=1, source_target_pairs={{0,3},{1,2},{2,1},{3,0},{4,7},{5,6},{6,5},{7,4},{8,11},{9,10},{10,... | collective-permute-start | bytes 393224 | tf_op jit(solution)/shard_map/ppermute | solution.py:28
  105.7 13.4 %collective-permute-start.5 = (f32[512,64]{1,0:T(8,128)S(1)}, f32[512,64]{1,0:T(8,128)S(1)}, u32[]{:S(2)}, u32[]{:S(2)}) collective-permute-start(f32[512,64]{1,0:T(8,128)S(1)} %get-tuple-element.196), channel_id=1, source_target_pairs={{0,1},{1,0},{2,3},{3,2},{4,5},{5,4},{6,7},{7,6},{8,9},{9,8},{10,11... | collective-permute-start | bytes 393224 | tf_op jit(solution)/shard_map/ppermute | solution.py:28
  107.2 12.6 %collective-permute-start.4 = (f32[512,64]{1,0:T(8,128)S(1)}, f32[512,64]{1,0:T(8,128)S(1)}, u32[]{:S(2)}, u32[]{:S(2)}) collective-permute-start(f32[512,64]{1,0:T(8,128)S(1)} %slice_bitcast_fusion.5), channel_id=1, source_target_pairs={{0,2},{1,3},{2,0},{3,1},{4,6},{5,7},{6,4},{7,5},{8,10},{9,11},{10,... | collective-permute-start | bytes 393224 | tf_op jit(solution)/shard_map/ppermute | solution.py:28
  108.5 18.8 %collective-permute-start.7 = (bf16[192,384]{1,0:T(8,128)(2,1)}, bf16[192,384]{1,0:T(8,128)(2,1)S(1)}, u32[]{:S(2)}, u32[]{:S(2)}) collective-permute-start(bf16[192,384]{1,0:T(8,128)(2,1)} %get-tuple-element.192), channel_id=1, source_target_pairs={{0,16},{4,20},{8,24},{12,28},{16,0},{20,4},{24,8},{28,12},{1,17},{... | collective-permute-start | bytes 442376 | tf_op jit(solution)/shard_map/ppermute | solution.py:28
  117.7 9.7 %collective-permute-start.8 = (bf16[192,384]{1,0:T(8,128)(2,1)S(1)}, bf16[192,384]{1,0:T(8,128)(2,1)S(1)}, u32[]{:S(2)}, u32[]{:S(2)}) collective-permute-start(bf16[192,384]{1,0:T(8,128)(2,1)S(1)} %get-tuple-element.191), channel_id=1, source_target_pairs={{0,8},{4,12},{8,0},{12,4},{16,24},{20,28},{24,16},{28,20},{1,9},{5... | collective-permute-start | bytes 442376 | tf_op jit(solution)/shard_map/ppermute | solution.py:28
  119.1 8.3 %collective-permute-start.9 = (bf16[192,384]{1,0:T(8,128)(2,1)S(1)}, bf16[192,384]{1,0:T(8,128)(2,1)S(1)}, u32[]{:S(2)}, u32[]{:S(2)}) collective-permute-start(bf16[192,384]{1,0:T(8,128)(2,1)S(1)} %get-tuple-element.190), channel_id=1, source_target_pairs={{0,24},{4,28},{8,16},{12,20},{16,8},{20,12},{24,0},{28,4},{1,25},{... | collective-permute-start | bytes 442376 | tf_op jit(solution)/shard_map/ppermute | solution.py:28
  126.1 7.3 %collective-permute-start.16 = (f32[2,16,448]{2,1,0:T(8,128)S(1)}, f32[2,16,448]{2,1,0:T(8,128)S(1)}, u32[]{:S(2)}, u32[]{:S(2)}) collective-permute-start(f32[2,16,448]{2,1,0:T(8,128)S(1)} %pad_maximum_fusion.1), channel_id=1, source_target_pairs={{4,0},{8,4},{12,8},{16,12},{20,16},{24,20},{28,24},{5,1},{9,5},{13... | collective-permute-start | bytes 172040 | tf_op jit(solution)/shard_map/ppermute | solution.py:23
  127.4 15.8 %collective-permute-start.10 = (bf16[4,128,384]{2,1,0:T(8,128)(2,1)}, bf16[4,128,384]{2,1,0:T(8,128)(2,1)S(1)}, u32[]{:S(2)}, u32[]{:S(2)}) collective-permute-start(bf16[4,128,384]{2,1,0:T(8,128)(2,1)} %get-tuple-element.149), channel_id=1, source_target_pairs={{0,4},{4,0},{8,12},{12,8},{16,20},{20,16},{24,28},{28,24},{1,5},{5... | collective-permute-start | bytes 1179656 | tf_op jit(solution)/shard_map/ppermute | solution.py:28
  130.2 21.1 %collective-permute-start.19 = (bf16[192,384]{1,0:T(8,128)(2,1)S(1)}, bf16[192,384]{1,0:T(8,128)(2,1)S(1)}, u32[]{:S(2)}, u32[]{:S(2)}) collective-permute-start(bf16[192,384]{1,0:T(8,128)(2,1)S(1)} %add_convert_fusion.4), channel_id=1, source_target_pairs={{0,24},{4,28},{8,16},{12,20},{16,8},{20,12},{24,0},{28,4},{1,25},{... | collective-permute-start | bytes 442376 | tf_op jit(solution)/shard_map/ppermute | solution.py:28
  133.3 18.6 %collective-permute-start.18 = (bf16[192,384]{1,0:T(8,128)(2,1)S(1)}, bf16[192,384]{1,0:T(8,128)(2,1)S(1)}, u32[]{:S(2)}, u32[]{:S(2)}) collective-permute-start(bf16[192,384]{1,0:T(8,128)(2,1)S(1)} %add_convert_fusion.4), channel_id=1, source_target_pairs={{0,8},{4,12},{8,0},{12,4},{16,24},{20,28},{24,16},{28,20},{1,9},{5... | collective-permute-start | bytes 442376 | tf_op jit(solution)/shard_map/ppermute | solution.py:28
  133.4 18.6 %collective-permute-start.17 = (bf16[192,384]{1,0:T(8,128)(2,1)S(1)}, bf16[192,384]{1,0:T(8,128)(2,1)S(1)}, u32[]{:S(2)}, u32[]{:S(2)}) collective-permute-start(bf16[192,384]{1,0:T(8,128)(2,1)S(1)} %add_convert_fusion.4), channel_id=1, source_target_pairs={{0,16},{4,20},{8,24},{12,28},{16,0},{20,4},{24,8},{28,12},{1,17},{... | collective-permute-start | bytes 442376 | tf_op jit(solution)/shard_map/ppermute | solution.py:28
  147.6 8.8 %collective-permute-start.11 = (bf16[128,384]{1,0:T(8,128)(2,1)S(1)}, bf16[128,384]{1,0:T(8,128)(2,1)S(1)}, u32[]{:S(2)}, u32[]{:S(2)}) collective-permute-start(bf16[128,384]{1,0:T(8,128)(2,1)S(1)} %get-tuple-element.200), channel_id=1, source_target_pairs={{0,16},{4,20},{8,24},{12,28},{16,0},{20,4},{24,8},{28,12},{1,17},{... | collective-permute-start | bytes 294920 | tf_op jit(solution)/shard_map/ppermute | solution.py:28
  149.2 7.1 %collective-permute-start.12 = (bf16[128,384]{1,0:T(8,128)(2,1)S(1)}, bf16[128,384]{1,0:T(8,128)(2,1)S(1)}, u32[]{:S(2)}, u32[]{:S(2)}) collective-permute-start(bf16[128,384]{1,0:T(8,128)(2,1)S(1)} %get-tuple-element.199), channel_id=1, source_target_pairs={{0,8},{4,12},{8,0},{12,4},{16,24},{20,28},{24,16},{28,20},{1,9},{5... | collective-permute-start | bytes 294920 | tf_op jit(solution)/shard_map/ppermute | solution.py:28
  151.3 6.5 %collective-permute-start.13 = (bf16[128,384]{1,0:T(8,128)(2,1)S(1)}, bf16[128,384]{1,0:T(8,128)(2,1)S(1)}, u32[]{:S(2)}, u32[]{:S(2)}) collective-permute-start(bf16[128,384]{1,0:T(8,128)(2,1)S(1)} %get-tuple-element.198), channel_id=1, source_target_pairs={{0,24},{4,28},{8,16},{12,20},{16,8},{20,12},{24,0},{28,4},{1,25},{... | collective-permute-start | bytes 294920 | tf_op jit(solution)/shard_map/ppermute | solution.py:28
  152.1 15.5 %copy-start.4 = (bf16[4,192,384]{2,1,0:T(8,128)(2,1)}, bf16[4,192,384]{2,1,0:T(8,128)(2,1)S(1)}, u32[]{:S(2)}) copy-start(bf16[4,192,384]{2,1,0:T(8,128)(2,1)S(1)} %pad_maximum_fusion.near_ref) | copy-start | bytes 1769476
  160.5 24.1 %all-to-all-start.4 = ((bf16[8,128,384]{2,1,0:T(8,128)(2,1)}), bf16[8,128,384]{2,1,0:T(8,128)(2,1)S(1)}, u32[]{:S(2)}, u32[]{:S(2)}) async-start(bf16[8,128,384]{2,1,0:T(8,128)(2,1)} %shard_map.293), calls=%async_computation.4 | async-start | bytes 1572864 | tf_op jit(solution)/shard_map/all_to_all | solution.py:1260
  165.0 8.6 %collective-permute-start.23 = (bf16[512,256]{1,0:T(8,128)(2,1)S(1)}, bf16[512,256]{1,0:T(8,128)(2,1)S(1)}, u32[]{:S(2)}, u32[]{:S(2)}) collective-permute-start(bf16[512,256]{1,0:T(8,128)(2,1)S(1)} %get-tuple-element.195), channel_id=1, source_target_pairs={{0,3},{1,2},{2,1},{3,0},{4,7},{5,6},{6,5},{7,4},{8,11},{9,10},{10,... | collective-permute-start | bytes 786440 | tf_op jit(solution)/shard_map/ppermute | solution.py:28
  165.1 8.5 %collective-permute-start.22 = (bf16[512,256]{1,0:T(8,128)(2,1)S(1)}, bf16[512,256]{1,0:T(8,128)(2,1)S(1)}, u32[]{:S(2)}, u32[]{:S(2)}) collective-permute-start(bf16[512,256]{1,0:T(8,128)(2,1)S(1)} %get-tuple-element.194), channel_id=1, source_target_pairs={{0,1},{1,0},{2,3},{3,2},{4,5},{5,4},{6,7},{7,6},{8,9},{9,8},{10,11... | collective-permute-start | bytes 786440 | tf_op jit(solution)/shard_map/ppermute | solution.py:28
  166.2 12.2 %collective-permute-start.21 = (bf16[512,256]{1,0:T(8,128)(2,1)S(1)}, bf16[512,256]{1,0:T(8,128)(2,1)S(1)}, u32[]{:S(2)}, u32[]{:S(2)}) collective-permute-start(bf16[512,256]{1,0:T(8,128)(2,1)S(1)} %slice_bitcast_fusion.2), channel_id=1, source_target_pairs={{0,2},{1,3},{2,0},{3,1},{4,6},{5,7},{6,4},{7,5},{8,10},{9,11},{10,... | collective-permute-start | bytes 786440 | tf_op jit(solution)/shard_map/ppermute | solution.py:28
  167.6 21.1 %collective-permute-start.20 = (bf16[4,192,384]{2,1,0:T(8,128)(2,1)S(1)}, bf16[4,192,384]{2,1,0:T(8,128)(2,1)}, u32[]{:S(2)}, u32[]{:S(2)}) collective-permute-start(bf16[4,192,384]{2,1,0:T(8,128)(2,1)S(1)} %pad_maximum_fusion.near_ref), channel_id=1, source_target_pairs={{0,4},{4,0},{8,12},{12,8},{16,20},{20,16},{24,28},{28,24},{1,5},{5... | collective-permute-start | bytes 1769480 | tf_op jit(solution)/shard_map/ppermute | solution.py:28
  184.6 6.9 %collective-permute-start.24 = (bf16[1,8,32,384]{3,2,1,0:T(8,128)(2,1)S(1)}, bf16[1,8,32,384]{3,2,1,0:T(8,128)(2,1)S(1)}, u32[]{:S(2)}, u32[]{:S(2)}) collective-permute-start(bf16[1,8,32,384]{3,2,1,0:T(8,128)(2,1)S(1)} %slice_bitcast_fusion.6), channel_id=1, source_target_pairs={{0,2},{1,3},{2,0},{3,1},{4,6},{5,7},{6,4},{7,5},{8,10},{9,11},{10,... | collective-permute-start | bytes 589832 | tf_op jit(solution)/shard_map/ppermute | solution.py:28
  191.6 1.8 collective-permute-start.25
  (20 other events, 73.9 us)

commit v4 on v3

--- a/solution.py
+++ b/solution.py
@@ -804,9 +804,9 @@
     return jnp.concatenate([total[:first], *small, *spare], axis=0).astype(BF16)
 
 
-def pair_kernel(keep_ref, got_ref, out_ref, **small):
-    for block in range(out_ref.shape[0]):
-        out_ref[block] = sum_terms([keep_ref[block], got_ref[block]], **small)
+def pair_kernel(keep_ref, got_ref, *out_refs, **small):
+    for block, out_ref in enumerate(out_refs):
+        out_ref[...] = sum_terms([keep_ref[block], got_ref[block]], **small)
 
 
 def sum_kernel(*refs, **small):
@@ -1214,12 +1214,12 @@
     early = sum(x.astype(F32) for x in early).astype(BF16)
     early = [swap(early, "seq", mask) if mask else early for mask in even]
     late_small = dict(first=value_lines + state_lines, lines=small_lines)
-    (late,) = local(
+    late = local(
         functools.partial(pair_kernel, **late_small),
-        [((blocks // 2, late_lines, inner), BF16)],
+        [((late_lines, inner), BF16)] * (blocks // 2),
         [late_keep, late],
     )
-    late = [swap(late[p], "seq", mask) if mask else late[p] for p, mask in enumerate(even)]
+    late = [swap(x, "seq", mask) if mask else x for x, mask in zip(late, even)]
     over = jnp.concatenate([value_in[:, :PAD], state_grad_in[:, :PAD]], axis=2)
     over = shift(over, "seq", -1)
     own_source = own_cols(tokens.reshape(rows, width), col_width).astype(F32)

time: 198 us -> 198 us (level)
    unnamed x46 -> x52, local copies, waits for them, and re-layouts: 6.83 us -> 7.5 us
  transfers between devices with their start and end apart: 31 -> 31, of which waited for: 15 -> 15; matrix products, arithmetic and copies ran while one was open for 9% -> 8% of each run, Pallas kernels for 24% -> 24%
where the time goes in v4:
time: 198 us; the launch traced here: 196 us
  Pallas kernels  68.3 us (34%)
  starting transfers between devices  57.4 us (29%)
  waiting for transfers between devices  36.3 us (18%)
  local copies, waits for them, and re-layouts  16.4 us (8%)
  blocking collectives  8.6 us (4%)
  other arithmetic  8.26 us (4%)
    pallas_call x16, Pallas kernels, local(): pl.pallas_call(body, grid=(steps,), out_shape=[jax.ShapeDtypeStruct(shape...  68.3 us
    ppermute x24, starting transfers between devices, swap(): return lax.ppermute(x, axis, [(i, i ^ mask) for i in range(devices)])  29 us
    ppermute x24, waiting for transfers between devices, swap(): return lax.ppermute(x, axis, [(i, i ^ mask) for i in range(devices)])  22.5 us
    all_gather x1, blocking collectives, on_device(): cot_low = lax.all_gather(cot_low, 'head', axis=1, tiled=True)  8.6 us
    unnamed x52, local copies, waits for them, and re-layouts  7.5 us
    all_to_all x1, starting transfers between devices, on_device(): got = lax.all_to_all(ends, 'seq', 0, 0)  6.66 us
    ppermute x2, starting transfers between devices, shift(): return lax.ppermute(x, axis, pairs)  6.15 us
    all_to_all x1, waiting for transfers between devices, on_device(): late = lax.all_to_all(late_values, 'seq', 0, 0)  4.12 us
  transfers between devices with their start and end apart: 31, of which 15 were waited for; matrix products, arithmetic and copies ran while one was open for 8% of the time, Pallas kernels for 24%

profile of v4, /device:TPU:0, one launch (start us, length us, event | category | flops | bytes accessed | tf_op | source)
XLA Modules:
  0.0 196.4 jit_solution(12480670664013119047)
XLA Ops:
  1.5 4.9 %collective-permute-start = (bf16[2,16,768]{2,1,0:T(8,128)(2,1)S(1)}, bf16[2,16,768]{2,1,0:T(8,128)(2,1)S(1)}, u32[]{:S(2)}, u32[]{:S(2)}) collective-permute-start(bf16[2,16,768]{2,1,0:T(8,128)(2,1)S(1)} %slice.75), channel_id=1, source_target_pairs={{0,4},{4,8},{8,12},{12,16},{16,20},{20,24},{24,28},{1,5},{5,9},{9,... | collective-permute-start | bytes 147464 | tf_op jit(solution)/shard_map/ppermute | solution.py:23
  8.7 7.4 %shard_map.279 = (bf16[2,272,768]{2,1,0:T(8,128)(2,1)}, f32[2,272,384]{2,1,0:T(8,128)}, f32[2,272,256]{2,1,0:T(8,128)}, f32[2,256,384]{2,1,0:T(8,128)}, f32[2,25...) custom-call(bf16[2,256,768]{2,1,0:T(8,128)(2,1)} %tokens_ref.3, ...), custom_call_target="tpu_custom_call" | custom-call | flops 100000000 | bytes 460940 | tf_op jit(solution)/shard_map/pallas_call | solution.py:197
  16.0 6.7 %all-to-all-start = ((f32[8,40,384]{2,1,0:T(8,128)}), f32[8,40,384]{2,1,0:T(8,128)S(1)}, u32[]{:S(2)}, u32[]{:S(2)}) async-start(f32[8,40,384]{2,1,0:T(8,128)} %get-tuple-element.108), calls=%async_computation | async-start | bytes 983040 | tf_op jit(solution)/shard_map/all_to_all | solution.py:1040
  23.1 8.6 %all_gather.3 = bf16[512,768]{0,1:T(8,128)(2,1)S(1)} all-gather(bf16[512,192]{0,1:T(8,128)(2,1)S(1)} %copy.41), channel_id=1, replica_groups=mesh['seq'=8,'head'=4] {'head'}, dimensions={1}, use_global_device_ids=true | all-gather | bytes 983040 | tf_op jit(solution)/shard_map/all_gather | solution.py:1043
  31.7 3.7 %all-to-all-done.got_ref = f32[8,40,384]{2,1,0:T(8,128)S(1)} async-done(((f32[8,40,384]{2,1,0:T(8,128)}), f32[8,40,384]{2,1,0:T(8,128)S(1)}, u32[]{:S(2)}, u32[]{:S(2)}) %all-to-all-start) | async-done | bytes 491552 | tf_op jit(solution)/shard_map/all_to_all | solution.py:1040
  38.0 3.7 %all-to-all-start.1 = ((f32[8,32,384]{2,1,0:T(8,128)}), f32[8,32,384]{2,1,0:T(8,128)S(1)}, u32[]{:S(2)}, u32[]{:S(2)}) async-start(f32[8,32,384]{2,1,0:T(8,128)} %shard_map.280), calls=%async_computation.1 | async-start | bytes 786432 | tf_op jit(solution)/shard_map/all_to_all | solution.py:1046
  42.8 6.3 %shard_map.281 = (f32[2,256,384]{2,1,0:T(8,128)}, f32[2,256,384]{2,1,0:T(8,128)}, f32[2,256,384]{2,1,0:T(8,128)}) custom-call(bf16[2,272,768]{2,1,0:T(8,128)(2,1)} %get-tuple-element.107.normed_ref, bf16[768,384]{1,0:T(8,128)(2,1)} %gate_proj_ref.3, f32[2,256,384]{2,1,0:T(8,128)} %get-tuple-element.113.values_ref, ...), custom_call_target="tpu_custom_call" | custom-call | flops 100000000 | bytes 1230854 | tf_op jit(solution)/shard_map/pallas_call | solution.py:197
  49.1 3.5 %all-to-all-done.1 = f32[8,32,384]{2,1,0:T(8,128)S(1)} async-done(((f32[8,32,384]{2,1,0:T(8,128)}), f32[8,32,384]{2,1,0:T(8,128)S(1)}, u32[]{:S(2)}, u32[]{:S(2)}) %all-to-all-start.1) | async-done | bytes 393248 | tf_op jit(solution)/shard_map/all_to_all | solution.py:1046
  53.4 3.4 %shard_map.282 = (f32[2,256,384]{2,1,0:T(8,128)}, f32[8,512]{1,0:T(8,128)}) custom-call(f32[2,128,384]{2,1,0:T(8,128)} %bitcast.67, f32[2,256,256]{2,1,0:T(8,128)} %get-tuple-element.111.states_ref, f32[2,256,384]{2,1,0:T(8,128)} %get-tuple-element.112.exp_cum_x_ref, f32[2,256,384]{2,1,0:T(8,128)} %get-tuple-element.118.base_ref, ...), custom_call_target="tpu_custom_call" | custom-call | flops 100000000 | bytes 1016192 | tf_op jit(solution)/shard_map/pallas_call | solution.py:197
  60.4 2.2 %collective-permute-done.2 = f32[8,512]{1,0:T(8,128)S(1)} collective-permute-done((f32[8,512]{1,0:T(8,128)S(1)}, f32[8,512]{1,0:T(8,128)S(1)}, u32[]{:S(2)}, u32[]{:S(2)}) %collective-permute-start.2) | collective-permute-done | bytes 16416 | tf_op jit(solution)/shard_map/ppermute | solution.py:28
  63.3 3.8 %shard_map.283 = (f32[2,256,384]{2,1,0:T(8,128)}, f32[8,32,384]{2,1,0:T(8,128)}) custom-call(f32[8,512]{1,0:T(8,128)} %add.71.sums_ref, f32[2,256,384]{2,1,0:T(8,128)} %get-tuple-element.122.read_ref, f32[2,256,384]{2,1,0:T(8,128)} %get-tuple-element.118.base_ref, f32[2,256,384]{2,1,0:T(8,128)} %get-tuple-element.119.gate_pre_ref, ...), custom_call_target="tpu_custom_call" | custom-call | flops 100000000 | bytes 1118592 | tf_op jit(solution)/shard_map/pallas_call | solution.py:197
  67.1 3.7 %all-to-all-start.2 = ((f32[8,32,384]{2,1,0:T(8,128)}), f32[8,32,384]{2,1,0:T(8,128)S(1)}, u32[]{:S(2)}, u32[]{:S(2)}) async-start(f32[8,32,384]{2,1,0:T(8,128)} %get-tuple-element.123), calls=%async_computation.2 | async-start | bytes 786432 | tf_op jit(solution)/shard_map/all_to_all | solution.py:1077
  71.3 7.7 %shard_map.284 = (bf16[2,256,384]{2,1,0:T(8,128)(2,1)}, f32[1,768]{1,0:T(1,128)}, f32[8,768]{1,0:T(8,128)}, bf16[4,192,384]{2,1,0:T(8,128)(2,1)}, bf16[4,192,384...) custom-call(s32[2]{0:T(128)} %pad_add_fusion.own_ref, f32[8,512]{1,0:T(8,128)} %add.71.sums_ref, ...), custom_call_target="tpu_custom_call" | custom-call | flops 100000000 | bytes 1884546 | tf_op jit(solution)/shard_map/pallas_call | solution.py:197
  79.1 2.1 %collective-permute-start.3 = (bf16[4,192,384]{2,1,0:T(8,128)(2,1)}, bf16[4,192,384]{2,1,0:T(8,128)(2,1)S(1)}, u32[]{:S(2)}, u32[]{:S(2)}) collective-permute-start(bf16[4,192,384]{2,1,0:T(8,128)(2,1)} %get-tuple-element.125), channel_id=1, source_target_pairs={{0,4},{4,0},{8,12},{12,8},{16,20},{20,16},{24,28},{28,24},{1,5},{5... | collective-permute-start | bytes 1769480 | tf_op jit(solution)/shard_map/ppermute | solution.py:28
  84.3 4.1 %all-to-all-start.3 = ((f32[8,32,384]{2,1,0:T(8,128)}), f32[8,32,384]{2,1,0:T(8,128)S(1)}, u32[]{:S(2)}, u32[]{:S(2)}) async-start(f32[8,32,384]{2,1,0:T(8,128)} %shard_map.285), calls=%async_computation.3 | async-start | bytes 786432 | tf_op jit(solution)/shard_map/all_to_all | solution.py:1123
  91.9 7.9 %shard_map.286 = (f32[2,256,384]{2,1,0:T(8,128)}, f32[2,256,128]{2,1,0:T(8,128)}, f32[2,256,128]{2,1,0:T(8,128)}, f32[2,6,256]{2,1,0:T(8,128)}) custom-call(f32[2,256,384]{2,1,0:T(8,128)} %get-tuple-element.113.values_ref, f32[2,256,256]{2,1,0:T(8,128)} %get-tuple-element.111.states_ref, f32[2,256,384]{2,1,0:T(8,128)} %get-tuple-element.114.step_x_ref, ...), custom_call_target="tpu_custom_call" | custom-call | flops 100000000 | bytes 1021952 | tf_op jit(solution)/shard_map/pallas_call | solution.py:197
  101.1 3.2 %shard_map.288 = (f32[2,512,64]{2,1,0:T(8,128)}, f32[2,512,64]{2,1,0:T(8,128)}) custom-call(s32[2]{0:T(128)} %pad_add_fusion.own_ref, f32[2,128,384]{2,1,0:T(8,128)} %bitcast.70, f32[2,256,384]{2,1,0:T(8,128)} %get-tuple-element.139.weighted_ref, f32[2,256,128]{2,1,0:T(8,128)} %get-tuple-element.140.grad_b_ref, f32[2,256,128]{2,1,0:T(8,128)} %get-tuple-element.141.grad_c_ref), custom_call_target="tpu_custom_call" | custom-call | flops 100000000 | bytes 425986 | tf_op jit(solution)/shard_map/pallas_call | solution.py:197
  108.5 2.5 %collective-permute-start.7 = (bf16[192,384]{1,0:T(8,128)(2,1)}, bf16[192,384]{1,0:T(8,128)(2,1)S(1)}, u32[]{:S(2)}, u32[]{:S(2)}) collective-permute-start(bf16[192,384]{1,0:T(8,128)(2,1)} %get-tuple-element.200), channel_id=1, source_target_pairs={{0,16},{4,20},{8,24},{12,28},{16,0},{20,4},{24,8},{28,12},{1,17},{... | collective-permute-start | bytes 442376 | tf_op jit(solution)/shard_map/ppermute | solution.py:28
  111.1 5.8 %shard_map.287 = (f32[2,272,384]{2,1,0:T(8,128)}, bf16[2,6,256]{2,1,0:T(8,128)(2,1)}, f32[5,384]{1,0:T(8,128)}, f32[6,128]{1,0:T(8,128)}) custom-call(f32[2,128,384]{2,1,0:T(8,128)} %bitcast.71, f32[2,128,384]{2,1,0:T(8,128)} %bitcast.69, f32[2,256,384]{2,1,0:T(8,128)} %get-tuple-element.113.values_ref, f32[2,256,256]{2,1,0:T(8,128)} %get-tuple-element.111.states_ref, ...), custom_call_target="tpu_custom_call" | custom-call | flops 100000000 | bytes 2117132 | tf_op jit(solution)/shard_map/pallas_call | solution.py:197
  120.5 4.7 %shard_map.289 = (f32[2,272,64]{2,1,0:T(8,128)}, bf16[4,128,384]{2,1,0:T(8,128)(2,1)}, bf16[4,128,384]{2,1,0:T(8,128)(2,1)}) custom-call(s32[2]{0:T(128)} %pad_add_fusion.own_ref, bf16[2,272,768]{2,1,0:T(8,128)(2,1)} %get-tuple-element.107.normed_ref, f32[2,272,384]{2,1,0:T(8,128)} %get-tuple-element.137.value_in_ref, ...), custom_call_target="tpu_custom_call" | custom-call | flops 100000000 | bytes 908162 | tf_op jit(solution)/shard_map/pallas_call | solution.py:197
  128.0 2.6 %collective-permute-start.10 = (bf16[4,128,384]{2,1,0:T(8,128)(2,1)}, bf16[4,128,384]{2,1,0:T(8,128)(2,1)S(1)}, u32[]{:S(2)}, u32[]{:S(2)}) collective-permute-start(bf16[4,128,384]{2,1,0:T(8,128)(2,1)} %get-tuple-element.153), channel_id=1, source_target_pairs={{0,4},{4,0},{8,12},{12,8},{16,20},{20,16},{24,28},{28,24},{1,5},{5... | collective-permute-start | bytes 1179656 | tf_op jit(solution)/shard_map/ppermute | solution.py:28
  131.7 3.4 %collective-permute-start.19 = (bf16[192,384]{1,0:T(8,128)(2,1)S(1)}, bf16[192,384]{1,0:T(8,128)(2,1)S(1)}, u32[]{:S(2)}, u32[]{:S(2)}) collective-permute-start(bf16[192,384]{1,0:T(8,128)(2,1)S(1)} %add_convert_fusion.4), channel_id=1, source_target_pairs={{0,24},{4,28},{8,16},{12,20},{16,8},{20,12},{24,0},{28,4},{1,25},{... | collective-permute-start | bytes 442376 | tf_op jit(solution)/shard_map/ppermute | solution.py:28
  137.4 5.1 %shard_map.291 = (bf16[2,512,256]{2,1,0:T(8,128)(2,1)}, bf16[2,512,256]{2,1,0:T(8,128)(2,1)}) custom-call(s32[2]{0:T(128)} %pad_add_fusion.own_ref, bf16[2,256,768]{2,1,0:T(8,128)(2,1)} %tokens_ref.3, f32[768]{0:T(1024)} %gain_ref.5, f32[2,272,384]{2,1,0:T(8,128)} %get-tuple-element.137.value_in_ref, f32[2,272,64]{2,1,0:T(8,128)} %get-tuple-element.160.state_in_ref, ...), custom_call_target="tpu_custom_call" | custom-call | flops 100000000 | bytes 877058 | tf_op jit(solution)/shard_map/pallas_call | solution.py:197
  151.8 4.4 %collective-permute-done.11.refs_1_ = bf16[128,384]{1,0:T(8,128)(2,1)S(1)} collective-permute-done((bf16[128,384]{1,0:T(8,128)(2,1)}, bf16[128,384]{1,0:T(8,128)(2,1)S(1)}, u32[]{:S(2)}, u32[]{:S(2)}) %collective-permute-start.11) | collective-permute-done | bytes 98336 | tf_op jit(solution)/shard_map/ppermute | solution.py:28
  160.6 4.1 %all-to-all-start.4 = ((bf16[8,128,384]{2,1,0:T(8,128)(2,1)}), bf16[8,128,384]{2,1,0:T(8,128)(2,1)S(1)}, u32[]{:S(2)}, u32[]{:S(2)}) async-start(bf16[8,128,384]{2,1,0:T(8,128)(2,1)} %shard_map.293), calls=%async_computation.4 | async-start | bytes 1572864 | tf_op jit(solution)/shard_map/all_to_all | solution.py:1260
  167.3 2.1 %collective-permute-start.20 = (bf16[4,192,384]{2,1,0:T(8,128)(2,1)S(1)}, bf16[4,192,384]{2,1,0:T(8,128)(2,1)}, u32[]{:S(2)}, u32[]{:S(2)}) collective-permute-start(bf16[4,192,384]{2,1,0:T(8,128)(2,1)S(1)} %pad_maximum_fusion.near_ref), channel_id=1, source_target_pairs={{0,4},{4,0},{8,12},{12,8},{16,20},{20,16},{24,28},{28,24},{1,5},{5... | collective-permute-start | bytes 1769480 | tf_op jit(solution)/shard_map/ppermute | solution.py:28
  169.4 4.0 %collective-permute-done.23 = bf16[512,256]{1,0:T(8,128)(2,1)S(1)} collective-permute-done((bf16[512,256]{1,0:T(8,128)(2,1)S(1)}, bf16[512,256]{1,0:T(8,128)(2,1)S(1)}, u32[]{:S(2)}, u32[]{:S(2)}) %collective-permute-start.23) | collective-permute-done | bytes 262176 | tf_op jit(solution)/shard_map/ppermute | solution.py:28
  173.5 5.2 %collective-permute-done.21 = bf16[512,256]{1,0:T(8,128)(2,1)S(1)} collective-permute-done((bf16[512,256]{1,0:T(8,128)(2,1)S(1)}, bf16[512,256]{1,0:T(8,128)(2,1)S(1)}, u32[]{:S(2)}, u32[]{:S(2)}) %collective-permute-start.21) | collective-permute-done | bytes 262176 | tf_op jit(solution)/shard_map/ppermute | solution.py:28
  180.2 4.1 %all-to-all-done.4 = bf16[8,128,384]{2,1,0:T(8,128)(2,1)S(1)} async-done(((bf16[8,128,384]{2,1,0:T(8,128)(2,1)}), bf16[8,128,384]{2,1,0:T(8,128)(2,1)S(1)}, u32[]{:S(2)}, u32[]{:S(2)}) %all-to-all-start.4) | async-done | bytes 786464 | tf_op jit(solution)/shard_map/all_to_all | solution.py:1260
  185.6 2.9 %collective-permute-done.20.far_ref = bf16[4,192,384]{2,1,0:T(8,128)(2,1)} collective-permute-done((bf16[4,192,384]{2,1,0:T(8,128)(2,1)S(1)}, bf16[4,192,384]{2,1,0:T(8,128)(2,1)}, u32[]{:S(2)}, u32[]{:S(2)}) %collective-permute-start.20) | collective-permute-done | bytes 589856 | tf_op jit(solution)/shard_map/ppermute | solution.py:28
  188.5 2.8 %shard_map.292 = (f32[8,96,384]{2,1,0:T(8,128)}, f32[8,48,768]{2,1,0:T(8,128)}) custom-call(s32[2]{0:T(128)} %pad_add_fusion.own_ref, bf16[4,192,384]{2,1,0:T(8,128)(2,1)} %copy-done.4, bf16[4,192,384]{2,1,0:T(8,128)(2,1)} %collective-permute-done.20.far_ref), custom_call_target="tpu_custom_call" | custom-call | flops 100000000 | bytes 294914 | tf_op jit(solution)/shard_map/pallas_call | solution.py:197
  193.9 2.4 %shard_map.294 = (f32[768,256]{1,0:T(8,128)}, f32[768]{0:T(1024)}, f32[6,768]{1,0:T(8,128)}, f32[4,384]{1,0:T(4,128)}, f32[384]{0:T(512)}, /*index=5*/f32[4,256]...) custom-call(s32[2]{0:T(128)} %pad_add_fusion.own_ref, ...), custom_call_target="tpu_custom_call" | custom-call | flops 100000000 | bytes 196610 | tf_op jit(solution)/shard_map/pallas_call | solution.py:197
  (134 shorter events, 56.2 us)
Async XLA Ops:
  1.5 6.6 %collective-permute-start = (bf16[2,16,768]{2,1,0:T(8,128)(2,1)S(1)}, bf16[2,16,768]{2,1,0:T(8,128)(2,1)S(1)}, u32[]{:S(2)}, u32[]{:S(2)}) collective-permute-start(bf16[2,16,768]{2,1,0:T(8,128)(2,1)S(1)} %slice.75), channel_id=1, source_target_pairs={{0,4},{4,8},{8,12},{12,16},{16,20},{20,24},{24,28},{1,5},{5,9},{9,... | collective-permute-start | bytes 147464 | tf_op jit(solution)/shard_map/ppermute | solution.py:23
  16.0 19.3 %all-to-all-start = ((f32[8,40,384]{2,1,0:T(8,128)}), f32[8,40,384]{2,1,0:T(8,128)S(1)}, u32[]{:S(2)}, u32[]{:S(2)}) async-start(f32[8,40,384]{2,1,0:T(8,128)} %get-tuple-element.108), calls=%async_computation | async-start | bytes 983040 | tf_op jit(solution)/shard_map/all_to_all | solution.py:1040
  38.0 14.7 %all-to-all-start.1 = ((f32[8,32,384]{2,1,0:T(8,128)}), f32[8,32,384]{2,1,0:T(8,128)S(1)}, u32[]{:S(2)}, u32[]{:S(2)}) async-start(f32[8,32,384]{2,1,0:T(8,128)} %shard_map.280), calls=%async_computation.1 | async-start | bytes 786432 | tf_op jit(solution)/shard_map/all_to_all | solution.py:1046
  56.8 1.4 collective-permute-start.1
  58.9 3.7 %collective-permute-start.2 = (f32[8,512]{1,0:T(8,128)S(1)}, f32[8,512]{1,0:T(8,128)S(1)}, u32[]{:S(2)}, u32[]{:S(2)}) collective-permute-start(f32[8,512]{1,0:T(8,128)S(1)} %add.70), channel_id=1, source_target_pairs={{0,2},{1,3},{2,0},{3,1},{4,6},{5,7},{6,4},{7,5},{8,10},{9,11},{10,... | collective-permute-start | bytes 49160 | tf_op jit(solution)/shard_map/ppermute | solution.py:28
  67.1 14.5 %all-to-all-start.2 = ((f32[8,32,384]{2,1,0:T(8,128)}), f32[8,32,384]{2,1,0:T(8,128)S(1)}, u32[]{:S(2)}, u32[]{:S(2)}) async-start(f32[8,32,384]{2,1,0:T(8,128)} %get-tuple-element.123), calls=%async_computation.2 | async-start | bytes 786432 | tf_op jit(solution)/shard_map/all_to_all | solution.py:1077
  79.0 10.3 %collective-permute-start.14 = (bf16[2,512,192]{2,1,0:T(8,128)(2,1)}, bf16[2,512,192]{2,1,0:T(8,128)(2,1)}, u32[]{:S(2)}, u32[]{:S(2)}) collective-permute-start(bf16[2,512,192]{2,1,0:T(8,128)(2,1)} %get-tuple-element.159), channel_id=1, source_target_pairs={{0,1},{1,0},{2,3},{3,2},{4,5},{5,4},{6,7},{7,6},{8,9},{9,8},{10,11... | collective-permute-start | bytes 1179656 | tf_op jit(solution)/shard_map/ppermute | solution.py:28
  79.1 20.7 %collective-permute-start.3 = (bf16[4,192,384]{2,1,0:T(8,128)(2,1)}, bf16[4,192,384]{2,1,0:T(8,128)(2,1)S(1)}, u32[]{:S(2)}, u32[]{:S(2)}) collective-permute-start(bf16[4,192,384]{2,1,0:T(8,128)(2,1)} %get-tuple-element.125), channel_id=1, source_target_pairs={{0,4},{4,0},{8,12},{12,8},{16,20},{20,16},{24,28},{28,24},{1,5},{5... | collective-permute-start | bytes 1769480 | tf_op jit(solution)/shard_map/ppermute | solution.py:28
  84.3 16.1 %all-to-all-start.3 = ((f32[8,32,384]{2,1,0:T(8,128)}), f32[8,32,384]{2,1,0:T(8,128)S(1)}, u32[]{:S(2)}, u32[]{:S(2)}) async-start(f32[8,32,384]{2,1,0:T(8,128)} %shard_map.285), calls=%async_computation.3 | async-start | bytes 786432 | tf_op jit(solution)/shard_map/all_to_all | solution.py:1123
  90.3 52.2 %collective-permute-start.15 = (bf16[1,512,192]{2,1,0:T(8,128)(2,1)S(1)}, bf16[1,512,192]{2,1,0:T(8,128)(2,1)}, u32[]{:S(2)}, u32[]{:S(2)}) collective-permute-start(bf16[1,512,192]{2,1,0:T(8,128)(2,1)S(1)} %add_convert_fusion.2), channel_id=1, source_target_pairs={{0,2},{1,3},{2,0},{3,1},{4,6},{5,7},{6,4},{7,5},{8,10},{9,11},{10,... | collective-permute-start | bytes 589832 | tf_op jit(solution)/shard_map/ppermute | solution.py:28
  105.5 12.3 %collective-permute-start.6 = (f32[512,64]{1,0:T(8,128)S(1)}, f32[512,64]{1,0:T(8,128)S(1)}, u32[]{:S(2)}, u32[]{:S(2)}) collective-permute-start(f32[512,64]{1,0:T(8,128)S(1)} %get-tuple-element.205), channel_id=1, source_target_pairs={{0,3},{1,2},{2,1},{3,0},{4,7},{5,6},{6,5},{7,4},{8,11},{9,10},{10,... | collective-permute-start | bytes 393224 | tf_op jit(solution)/shard_map/ppermute | solution.py:28
  105.6 13.6 %collective-permute-start.5 = (f32[512,64]{1,0:T(8,128)S(1)}, f32[512,64]{1,0:T(8,128)S(1)}, u32[]{:S(2)}, u32[]{:S(2)}) collective-permute-start(f32[512,64]{1,0:T(8,128)S(1)} %get-tuple-element.204), channel_id=1, source_target_pairs={{0,1},{1,0},{2,3},{3,2},{4,5},{5,4},{6,7},{7,6},{8,9},{9,8},{10,11... | collective-permute-start | bytes 393224 | tf_op jit(solution)/shard_map/ppermute | solution.py:28
  107.2 12.6 %collective-permute-start.4 = (f32[512,64]{1,0:T(8,128)S(1)}, f32[512,64]{1,0:T(8,128)S(1)}, u32[]{:S(2)}, u32[]{:S(2)}) collective-permute-start(f32[512,64]{1,0:T(8,128)S(1)} %slice_bitcast_fusion.5), channel_id=1, source_target_pairs={{0,2},{1,3},{2,0},{3,1},{4,6},{5,7},{6,4},{7,5},{8,10},{9,11},{10,... | collective-permute-start | bytes 393224 | tf_op jit(solution)/shard_map/ppermute | solution.py:28
  108.5 18.8 %collective-permute-start.7 = (bf16[192,384]{1,0:T(8,128)(2,1)}, bf16[192,384]{1,0:T(8,128)(2,1)S(1)}, u32[]{:S(2)}, u32[]{:S(2)}) collective-permute-start(bf16[192,384]{1,0:T(8,128)(2,1)} %get-tuple-element.200), channel_id=1, source_target_pairs={{0,16},{4,20},{8,24},{12,28},{16,0},{20,4},{24,8},{28,12},{1,17},{... | collective-permute-start | bytes 442376 | tf_op jit(solution)/shard_map/ppermute | solution.py:28
  117.7 9.6 %collective-permute-start.8 = (bf16[192,384]{1,0:T(8,128)(2,1)S(1)}, bf16[192,384]{1,0:T(8,128)(2,1)S(1)}, u32[]{:S(2)}, u32[]{:S(2)}) collective-permute-start(bf16[192,384]{1,0:T(8,128)(2,1)S(1)} %copy-done.17), channel_id=1, source_target_pairs={{0,8},{4,12},{8,0},{12,4},{16,24},{20,28},{24,16},{28,20},{1,9},{5... | collective-permute-start | bytes 442376 | tf_op jit(solution)/shard_map/ppermute | solution.py:28
  119.3 8.1 %collective-permute-start.9 = (bf16[192,384]{1,0:T(8,128)(2,1)S(1)}, bf16[192,384]{1,0:T(8,128)(2,1)S(1)}, u32[]{:S(2)}, u32[]{:S(2)}) collective-permute-start(bf16[192,384]{1,0:T(8,128)(2,1)S(1)} %get-tuple-element.198), channel_id=1, source_target_pairs={{0,24},{4,28},{8,16},{12,20},{16,8},{20,12},{24,0},{28,4},{1,25},{... | collective-permute-start | bytes 442376 | tf_op jit(solution)/shard_map/ppermute | solution.py:28
  126.0 9.1 %collective-permute-start.16 = (f32[2,16,448]{2,1,0:T(8,128)S(1)}, f32[2,16,448]{2,1,0:T(8,128)S(1)}, u32[]{:S(2)}, u32[]{:S(2)}) collective-permute-start(f32[2,16,448]{2,1,0:T(8,128)S(1)} %pad_maximum_fusion.1), channel_id=1, source_target_pairs={{4,0},{8,4},{12,8},{16,12},{20,16},{24,20},{28,24},{5,1},{9,5},{13... | collective-permute-start | bytes 172040 | tf_op jit(solution)/shard_map/ppermute | solution.py:23
  128.0 16.7 %collective-permute-start.10 = (bf16[4,128,384]{2,1,0:T(8,128)(2,1)}, bf16[4,128,384]{2,1,0:T(8,128)(2,1)S(1)}, u32[]{:S(2)}, u32[]{:S(2)}) collective-permute-start(bf16[4,128,384]{2,1,0:T(8,128)(2,1)} %get-tuple-element.153), channel_id=1, source_target_pairs={{0,4},{4,0},{8,12},{12,8},{16,20},{20,16},{24,28},{28,24},{1,5},{5... | collective-permute-start | bytes 1179656 | tf_op jit(solution)/shard_map/ppermute | solution.py:28
  131.7 19.5 %collective-permute-start.19 = (bf16[192,384]{1,0:T(8,128)(2,1)S(1)}, bf16[192,384]{1,0:T(8,128)(2,1)S(1)}, u32[]{:S(2)}, u32[]{:S(2)}) collective-permute-start(bf16[192,384]{1,0:T(8,128)(2,1)S(1)} %add_convert_fusion.4), channel_id=1, source_target_pairs={{0,24},{4,28},{8,16},{12,20},{16,8},{20,12},{24,0},{28,4},{1,25},{... | collective-permute-start | bytes 442376 | tf_op jit(solution)/shard_map/ppermute | solution.py:28
  135.1 16.6 %collective-permute-start.18 = (bf16[192,384]{1,0:T(8,128)(2,1)S(1)}, bf16[192,384]{1,0:T(8,128)(2,1)S(1)}, u32[]{:S(2)}, u32[]{:S(2)}) collective-permute-start(bf16[192,384]{1,0:T(8,128)(2,1)S(1)} %add_convert_fusion.4), channel_id=1, source_target_pairs={{0,8},{4,12},{8,0},{12,4},{16,24},{20,28},{24,16},{28,20},{1,9},{5... | collective-permute-start | bytes 442376 | tf_op jit(solution)/shard_map/ppermute | solution.py:28
  135.1 16.6 %collective-permute-start.17 = (bf16[192,384]{1,0:T(8,128)(2,1)S(1)}, bf16[192,384]{1,0:T(8,128)(2,1)S(1)}, u32[]{:S(2)}, u32[]{:S(2)}) collective-permute-start(bf16[192,384]{1,0:T(8,128)(2,1)S(1)} %add_convert_fusion.4), channel_id=1, source_target_pairs={{0,16},{4,20},{8,24},{12,28},{16,0},{20,4},{24,8},{28,12},{1,17},{... | collective-permute-start | bytes 442376 | tf_op jit(solution)/shard_map/ppermute | solution.py:28
  147.3 8.9 %collective-permute-start.11 = (bf16[128,384]{1,0:T(8,128)(2,1)}, bf16[128,384]{1,0:T(8,128)(2,1)S(1)}, u32[]{:S(2)}, u32[]{:S(2)}) collective-permute-start(bf16[128,384]{1,0:T(8,128)(2,1)} %get-tuple-element.155), channel_id=1, source_target_pairs={{0,16},{4,20},{8,24},{12,28},{16,0},{20,4},{24,8},{28,12},{1,17},{... | collective-permute-start | bytes 294920 | tf_op jit(solution)/shard_map/ppermute | solution.py:28
  149.2 7.1 %collective-permute-start.12 = (bf16[128,384]{1,0:T(8,128)(2,1)}, bf16[128,384]{1,0:T(8,128)(2,1)S(1)}, u32[]{:S(2)}, u32[]{:S(2)}) collective-permute-start(bf16[128,384]{1,0:T(8,128)(2,1)} %get-tuple-element.156), channel_id=1, source_target_pairs={{0,8},{4,12},{8,0},{12,4},{16,24},{20,28},{24,16},{28,20},{1,9},{5... | collective-permute-start | bytes 294920 | tf_op jit(solution)/shard_map/ppermute | solution.py:28
  151.2 6.7 %collective-permute-start.13 = (bf16[128,384]{1,0:T(8,128)(2,1)}, bf16[128,384]{1,0:T(8,128)(2,1)S(1)}, u32[]{:S(2)}, u32[]{:S(2)}) collective-permute-start(bf16[128,384]{1,0:T(8,128)(2,1)} %get-tuple-element.157), channel_id=1, source_target_pairs={{0,24},{4,28},{8,16},{12,20},{16,8},{20,12},{24,0},{28,4},{1,25},{... | collective-permute-start | bytes 294920 | tf_op jit(solution)/shard_map/ppermute | solution.py:28
  151.8 15.5 %copy-start.4 = (bf16[4,192,384]{2,1,0:T(8,128)(2,1)}, bf16[4,192,384]{2,1,0:T(8,128)(2,1)S(1)}, u32[]{:S(2)}) copy-start(bf16[4,192,384]{2,1,0:T(8,128)(2,1)S(1)} %pad_maximum_fusion.near_ref) | copy-start | bytes 1769476
  160.6 23.7 %all-to-all-start.4 = ((bf16[8,128,384]{2,1,0:T(8,128)(2,1)}), bf16[8,128,384]{2,1,0:T(8,128)(2,1)S(1)}, u32[]{:S(2)}, u32[]{:S(2)}) async-start(bf16[8,128,384]{2,1,0:T(8,128)(2,1)} %shard_map.293), calls=%async_computation.4 | async-start | bytes 1572864 | tf_op jit(solution)/shard_map/all_to_all | solution.py:1260
  164.8 8.7 %collective-permute-start.23 = (bf16[512,256]{1,0:T(8,128)(2,1)S(1)}, bf16[512,256]{1,0:T(8,128)(2,1)S(1)}, u32[]{:S(2)}, u32[]{:S(2)}) collective-permute-start(bf16[512,256]{1,0:T(8,128)(2,1)S(1)} %get-tuple-element.203), channel_id=1, source_target_pairs={{0,3},{1,2},{2,1},{3,0},{4,7},{5,6},{6,5},{7,4},{8,11},{9,10},{10,... | collective-permute-start | bytes 786440 | tf_op jit(solution)/shard_map/ppermute | solution.py:28
  164.9 8.6 %collective-permute-start.22 = (bf16[512,256]{1,0:T(8,128)(2,1)S(1)}, bf16[512,256]{1,0:T(8,128)(2,1)S(1)}, u32[]{:S(2)}, u32[]{:S(2)}) collective-permute-start(bf16[512,256]{1,0:T(8,128)(2,1)S(1)} %get-tuple-element.202), channel_id=1, source_target_pairs={{0,1},{1,0},{2,3},{3,2},{4,5},{5,4},{6,7},{7,6},{8,9},{9,8},{10,11... | collective-permute-start | bytes 786440 | tf_op jit(solution)/shard_map/ppermute | solution.py:28
  166.2 12.4 %collective-permute-start.21 = (bf16[512,256]{1,0:T(8,128)(2,1)S(1)}, bf16[512,256]{1,0:T(8,128)(2,1)S(1)}, u32[]{:S(2)}, u32[]{:S(2)}) collective-permute-start(bf16[512,256]{1,0:T(8,128)(2,1)S(1)} %slice_bitcast_fusion.2), channel_id=1, source_target_pairs={{0,2},{1,3},{2,0},{3,1},{4,6},{5,7},{6,4},{7,5},{8,10},{9,11},{10,... | collective-permute-start | bytes 786440 | tf_op jit(solution)/shard_map/ppermute | solution.py:28
  167.3 21.1 %collective-permute-start.20 = (bf16[4,192,384]{2,1,0:T(8,128)(2,1)S(1)}, bf16[4,192,384]{2,1,0:T(8,128)(2,1)}, u32[]{:S(2)}, u32[]{:S(2)}) collective-permute-start(bf16[4,192,384]{2,1,0:T(8,128)(2,1)S(1)} %pad_maximum_fusion.near_ref), channel_id=1, source_target_pairs={{0,4},{4,0},{8,12},{12,8},{16,20},{20,16},{24,28},{28,24},{1,5},{5... | collective-permute-start | bytes 1769480 | tf_op jit(solution)/shard_map/ppermute | solution.py:28
  184.4 6.9 %collective-permute-start.24 = (bf16[1,8,32,384]{3,2,1,0:T(8,128)(2,1)S(1)}, bf16[1,8,32,384]{3,2,1,0:T(8,128)(2,1)S(1)}, u32[]{:S(2)}, u32[]{:S(2)}) collective-permute-start(bf16[1,8,32,384]{3,2,1,0:T(8,128)(2,1)S(1)} %slice_bitcast_fusion.6), channel_id=1, source_target_pairs={{0,2},{1,3},{2,0},{3,1},{4,6},{5,7},{6,4},{7,5},{8,10},{9,11},{10,... | collective-permute-start | bytes 589832 | tf_op jit(solution)/shard_map/ppermute | solution.py:28
  191.3 1.8 collective-permute-start.25
  (23 other events, 82.4 us)
